TPU v7x, 32 devices: a whole 2x2x4 slice. The times are simulated.
32 devices in a mesh: seq: 8 (over z, core), fsdp: 4 (over y, x).
Axes of the slice: x: 2, y: 2, z: 4, core: 2. Of those that a mesh axis runs over, the one named last changes fastest.
Arguments:
- tokens: bfloat16 [4, 1024, 2048], P('fsdp', 'seq'), may hold values from -6 to 6
- cotangent: bfloat16 [4, 1024, 2048], P('fsdp', 'seq'), may hold values from -6 to 6
- mix_gain: bfloat16 [2048], P(('seq', 'fsdp')), may hold values from 0.099609375 to 1.8984375
- lru_in_weight: bfloat16 [2048, 2560], P(('seq', 'fsdp')), may hold values from -0.125 to 0.125
- gelu_in_weight: bfloat16 [2048, 2560], P(('seq', 'fsdp')), may hold values from -0.125 to 0.125
- out_weight: bfloat16 [2560, 2048], P(('seq', 'fsdp')), may hold values from -0.3125 to 0.3125
- conv_weight: bfloat16 [2560, 4], P(('seq', 'fsdp')), may hold values from -3 to 3
- conv_bias: bfloat16 [2560], P(('seq', 'fsdp')), may hold values from -3 to 3
- recurrence_weight: bfloat16 [2560, 160], P(('seq', 'fsdp')), may hold values from -0.5 to 0.5
- recurrence_bias: bfloat16 [2560], P(('seq', 'fsdp')), may hold values from -3 to 3
- input_gate_weight: bfloat16 [2560, 160], P(('seq', 'fsdp')), may hold values from -0.5 to 0.5
- input_gate_bias: bfloat16 [2560], P(('seq', 'fsdp')), may hold values from -3 to 3
- decay_param: bfloat16 [2560], P(('seq', 'fsdp')), may hold values from 3 to 13
- mlp_gain: bfloat16 [2048], P(('seq', 'fsdp')), may hold values from 0.099609375 to 1.8984375
- gate_weight: bfloat16 [2048, 6144], P(('seq', 'fsdp')), may hold values from -0.125 to 0.125
- up_weight: bfloat16 [2048, 6144], P(('seq', 'fsdp')), may hold values from -0.125 to 0.125
- down_weight: bfloat16 [6144, 2048], P(('seq', 'fsdp')), may hold values from -0.109375 to 0.109375
Outputs:
- result: bfloat16 [4, 1024, 2048], P('fsdp', 'seq')
- tokens_grad: bfloat16 [4, 1024, 2048], P('fsdp', 'seq')
- mix_gain_grad: float32 [2048], P(('seq', 'fsdp'))
- lru_in_weight_grad: float32 [2048, 2560], P(('seq', 'fsdp'))
- gelu_in_weight_grad: float32 [2048, 2560], P(('seq', 'fsdp'))
- out_weight_grad: float32 [2560, 2048], P(('seq', 'fsdp'))
- conv_weight_grad: float32 [2560, 4], P(('seq', 'fsdp'))
- conv_bias_grad: float32 [2560], P(('seq', 'fsdp'))
- recurrence_weight_grad: float32 [2560, 160], P(('seq', 'fsdp'))
- recurrence_bias_grad: float32 [2560], P(('seq', 'fsdp'))
- input_gate_weight_grad: float32 [2560, 160], P(('seq', 'fsdp'))
- input_gate_bias_grad: float32 [2560], P(('seq', 'fsdp'))
- decay_param_grad: float32 [2560], P(('seq', 'fsdp'))
- mlp_gain_grad: float32 [2048], P(('seq', 'fsdp'))
- gate_weight_grad: float32 [2048, 6144], P(('seq', 'fsdp'))
- up_weight_grad: float32 [2048, 6144], P(('seq', 'fsdp'))
- down_weight_grad: float32 [6144, 2048], P(('seq', 'fsdp'))
All inputs are finite; a program needn't handle non-finite values.
Results may differ from a plain program's by a relative error of at most 0.012.
Values may be sent and summed in bfloat16 or wider, within the bound.
A program may use at most 512 MiB of HBM per device.

v0:
```python
import jax
import jax.numpy as jnp
from jax import lax
from jax.sharding import PartitionSpec as P

EPSILON = 1e-06
RATE_SCALE = 8.0


def rms_scale(values, gain):
    scale = lax.rsqrt(jnp.mean(values * values, axis=-1, keepdims=True) + EPSILON)
    return values * scale * gain


def linear_pair(first, second):
    return (first[0] * second[0], second[0] * first[1] + second[1])


def coefficients(gate_pre, input_pre, inputs, gate_bias, input_bias, decay_param):
    recur_gate = jax.nn.sigmoid(gate_pre + gate_bias)
    input_gate = jax.nn.sigmoid(input_pre + input_bias)
    log_decay = -RATE_SCALE * recur_gate * jax.nn.softplus(-decay_param)
    factor = jnp.exp(log_decay)
    driving = jnp.sqrt(-jnp.expm1(2.0 * log_decay)) * input_gate * inputs
    return (factor, driving)


def convolve(extended, taps_weight, conv_bias, positions):
    summed = jnp.zeros_like(extended[:positions]) + conv_bias
    taps = taps_weight.shape[1]
    for offset in range(taps):
        summed = (
            summed
            + taps_weight[:, offset] * extended[taps - 1 - offset : taps - 1 - offset + positions]
        )
    return summed


def block_product(values, weight):
    row_count = values.shape[0]
    block_width = weight.shape[1]
    block_count = weight.shape[0] // block_width
    shaped = values.reshape(row_count, block_count, block_width)
    return jnp.einsum(
        "tnk,nkj->tnj",
        shaped,
        weight.reshape(block_count, block_width, block_width),
        preferred_element_type=jnp.float32,
    ).reshape(row_count, block_count * block_width)


def block_transpose(gradient, weight):
    row_count = gradient.shape[0]
    block_width = weight.shape[1]
    block_count = weight.shape[0] // block_width
    shaped = gradient.reshape(row_count, block_count, block_width)
    return jnp.einsum(
        "tnj,nkj->tnk",
        shaped,
        weight.reshape(block_count, block_width, block_width),
        preferred_element_type=jnp.float32,
    ).reshape(row_count, block_count * block_width)


def block_outer(values, gradient, block_width):
    row_count = values.shape[0]
    block_count = values.shape[1] // block_width
    summed = jnp.einsum(
        "tnk,tnj->nkj",
        values.reshape(row_count, block_count, block_width),
        gradient.reshape(row_count, block_count, block_width),
        preferred_element_type=jnp.float32,
    )
    return summed.reshape(block_count * block_width, block_width)


def outer_sum(left, right):
    return lax.dot_general(
        left, right, (((0,), (0,)), ((), ())), preferred_element_type=jnp.float32
    )


def times_transpose(left, right):
    return lax.dot_general(
        left, right, (((1,), (1,)), ((), ())), preferred_element_type=jnp.float32
    )


def zero_carry(products, states):
    return jnp.zeros_like(states)


def zero_edge(edge_rows):
    return jnp.zeros_like(edge_rows)


def mixer_forward(values, edge_rows, params, carry_fn):
    (
        conv_weight,
        conv_bias,
        recurrence_weight,
        recurrence_bias,
        input_gate_weight,
        input_gate_bias,
        decay_param,
    ) = params
    positions = values.shape[0]
    extended = jnp.concatenate([edge_rows, values], axis=0).astype(jnp.float32)
    conv_out = convolve(
        extended, conv_weight.astype(jnp.float32), conv_bias.astype(jnp.float32), positions
    )
    conv_low = conv_out.astype(jnp.bfloat16)
    gate_pre = block_product(conv_low, recurrence_weight)
    input_pre = block_product(conv_low, input_gate_weight)
    factor, driving = coefficients(
        gate_pre,
        input_pre,
        conv_low.astype(jnp.float32),
        recurrence_bias.astype(jnp.float32),
        input_gate_bias.astype(jnp.float32),
        decay_param.astype(jnp.float32),
    )
    products, local_states = lax.associative_scan(linear_pair, (factor, driving), axis=0)
    start_state = carry_fn(products[-1], local_states[-1])
    states = local_states + products * start_state
    return (states, (extended, conv_low, gate_pre, input_pre, factor, states, start_state))


def mixer_backward(states_grad, saved, params, carry_fn, edge_fn):
    extended, conv_low, gate_pre, input_pre, factor, states, start_state = saved
    (
        conv_weight,
        conv_bias,
        recurrence_weight,
        recurrence_bias,
        input_gate_weight,
        input_gate_bias,
        decay_param,
    ) = params
    positions = states_grad.shape[0]
    taps = conv_weight.shape[1]
    shifted = jnp.concatenate([factor[1:], jnp.ones_like(factor[:1])], axis=0)
    products, local_grad = lax.associative_scan(
        linear_pair, (shifted, states_grad), reverse=True, axis=0
    )
    incoming = carry_fn(factor[0] * products[0], factor[0] * local_grad[0])
    adjoint = local_grad + products * incoming
    before = jnp.concatenate([start_state[None], states[:-1]], axis=0)
    pieces = (
        gate_pre,
        input_pre,
        conv_low.astype(jnp.float32),
        recurrence_bias.astype(jnp.float32),
        input_gate_bias.astype(jnp.float32),
        decay_param.astype(jnp.float32),
    )
    unused, pullback = jax.vjp(coefficients, *pieces)
    gate_grad, input_grad, conv_grad, rbias_grad, ibias_grad, decay_grad = pullback(
        (adjoint * before, adjoint)
    )
    gate_low = gate_grad.astype(jnp.bfloat16)
    input_low = input_grad.astype(jnp.bfloat16)
    conv_grad = (
        conv_grad
        + block_transpose(gate_low, recurrence_weight)
        + block_transpose(input_low, input_gate_weight)
    )
    block_width = recurrence_weight.shape[1]
    rweight_grad = block_outer(conv_low, gate_low, block_width)
    iweight_grad = block_outer(conv_low, input_low, block_width)
    next_rows = edge_fn(conv_grad[: taps - 1])
    extended_grad = jnp.concatenate([conv_grad, next_rows], axis=0)
    taps_weight = conv_weight.astype(jnp.float32)
    values_grad = jnp.zeros_like(conv_grad)
    tap_grads = []
    for offset in range(taps):
        values_grad = (
            values_grad + taps_weight[:, offset] * extended_grad[offset : offset + positions]
        )
        tap_grads.append(
            jnp.sum(conv_grad * extended[taps - 1 - offset : taps - 1 - offset + positions], axis=0)
        )
    cweight_grad = jnp.stack(tap_grads, axis=1)
    cbias_grad = jnp.sum(conv_grad, axis=0)
    return (
        values_grad,
        (cweight_grad, cbias_grad, rweight_grad, rbias_grad, iweight_grad, ibias_grad, decay_grad),
    )


def local(
    tokens,
    cotangent,
    mix_gain,
    lru_in_weight,
    gelu_in_weight,
    out_weight,
    conv_weight,
    conv_bias,
    recurrence_weight,
    recurrence_bias,
    input_gate_weight,
    input_gate_bias,
    decay_param,
    mlp_gain,
    gate_weight,
    up_weight,
    down_weight,
):
    gathered = (
        lax.all_gather(mix_gain, ("seq", "fsdp"), axis=0, tiled=True),
        lax.all_gather(lru_in_weight, ("seq", "fsdp"), axis=0, tiled=True),
        lax.all_gather(gelu_in_weight, ("seq", "fsdp"), axis=0, tiled=True),
        lax.all_gather(out_weight, ("seq", "fsdp"), axis=0, tiled=True),
        lax.all_gather(conv_weight, ("seq", "fsdp"), axis=0, tiled=True),
        lax.all_gather(conv_bias, ("seq", "fsdp"), axis=0, tiled=True),
        lax.all_gather(recurrence_weight, ("seq", "fsdp"), axis=0, tiled=True),
        lax.all_gather(recurrence_bias, ("seq", "fsdp"), axis=0, tiled=True),
        lax.all_gather(input_gate_weight, ("seq", "fsdp"), axis=0, tiled=True),
        lax.all_gather(input_gate_bias, ("seq", "fsdp"), axis=0, tiled=True),
        lax.all_gather(decay_param, ("seq", "fsdp"), axis=0, tiled=True),
        lax.all_gather(mlp_gain, ("seq", "fsdp"), axis=0, tiled=True),
        lax.all_gather(gate_weight, ("seq", "fsdp"), axis=0, tiled=True),
        lax.all_gather(up_weight, ("seq", "fsdp"), axis=0, tiled=True),
        lax.all_gather(down_weight, ("seq", "fsdp"), axis=0, tiled=True),
    )
    (
        whole_mix_gain,
        whole_lru_in,
        whole_gelu_in,
        whole_out,
        whole_conv,
        whole_conv_bias,
        whole_rweight,
        whole_rbias,
        whole_iweight,
        whole_ibias,
        whole_decay,
        whole_mlp_gain,
        whole_gate,
        whole_up,
        whole_down,
    ) = gathered
    lru_params = (
        whole_conv,
        whole_conv_bias,
        whole_rweight,
        whole_rbias,
        whole_iweight,
        whole_ibias,
        whole_decay,
    )
    positions = tokens.shape[1]
    model_width = tokens.shape[2]
    resid_in = tokens.reshape(positions, model_width).astype(jnp.float32)
    grad_low = cotangent.reshape(positions, model_width)
    grad_out = grad_low.astype(jnp.float32)
    mix_scale = whole_mix_gain.astype(jnp.float32)
    normed_low = rms_scale(resid_in, mix_scale).astype(jnp.bfloat16)
    branch_x = jnp.dot(normed_low, whole_lru_in, preferred_element_type=jnp.float32).astype(
        jnp.bfloat16
    )
    branch_pre = jnp.dot(normed_low, whole_gelu_in, preferred_element_type=jnp.float32)
    branch_y = jax.nn.gelu(branch_pre)
    full_width = branch_x.shape[1]
    taps = whole_conv.shape[1]
    channels = full_width // lax.axis_size("seq")
    first_row = lax.axis_index("seq") * channels
    local_params = tuple(
        (lax.dynamic_slice_in_dim(member, first_row, channels, 0) for member in lru_params)
    )
    seq_values = lax.all_to_all(branch_x, "seq", split_axis=1, concat_axis=0, tiled=True)
    states, saved = mixer_forward(
        seq_values, jnp.zeros((taps - 1, channels), jnp.bfloat16), local_params, zero_carry
    )
    states_low = lax.all_to_all(
        states.astype(jnp.bfloat16), "seq", split_axis=0, concat_axis=1, tiled=True
    )
    states_f = states_low.astype(jnp.float32)
    product = (states_f * branch_y).astype(jnp.bfloat16)
    middle = resid_in + jnp.dot(product, whole_out, preferred_element_type=jnp.float32)
    mlp_scale = whole_mlp_gain.astype(jnp.float32)
    normed2_low = rms_scale(middle, mlp_scale).astype(jnp.bfloat16)
    gate_val = jnp.dot(normed2_low, whole_gate, preferred_element_type=jnp.float32)
    up_val = jnp.dot(normed2_low, whole_up, preferred_element_type=jnp.float32)
    hidden = (jax.nn.gelu(gate_val) * up_val).astype(jnp.bfloat16)
    result = middle + jnp.dot(hidden, whole_down, preferred_element_type=jnp.float32)
    down_grad = outer_sum(hidden, grad_low)
    hidden_grad = times_transpose(grad_low, whole_down)
    unused, pull_glu = jax.vjp(lambda first, second: jax.nn.gelu(first) * second, gate_val, up_val)
    gate_grad, up_grad = pull_glu(hidden_grad)
    gate_low = gate_grad.astype(jnp.bfloat16)
    up_low = up_grad.astype(jnp.bfloat16)
    gate_w_grad = outer_sum(normed2_low, gate_low)
    up_w_grad = outer_sum(normed2_low, up_low)
    normed2_grad = times_transpose(gate_low, whole_gate) + times_transpose(up_low, whole_up)
    unused, pull_norm2 = jax.vjp(rms_scale, middle, mlp_scale)
    middle_part, mlp_gain_grad = pull_norm2(normed2_grad)
    middle_grad = grad_out + middle_part
    mixed_low = middle_grad.astype(jnp.bfloat16)
    out_w_grad = outer_sum(product, mixed_low)
    product_grad = times_transpose(mixed_low, whole_out)
    states_grad = (product_grad * branch_y).astype(jnp.bfloat16)
    unused, pull_gelu = jax.vjp(jax.nn.gelu, branch_pre)
    (pre_grad,) = pull_gelu(product_grad * states_f)
    pre_low = pre_grad.astype(jnp.bfloat16)
    chan_grad = lax.all_to_all(states_grad, "seq", split_axis=1, concat_axis=0, tiled=True)
    values_grad, local_grads = mixer_backward(
        chan_grad.astype(jnp.float32), saved, local_params, zero_carry, zero_edge
    )
    x_low = lax.all_to_all(
        values_grad.astype(jnp.bfloat16), "seq", split_axis=0, concat_axis=1, tiled=True
    )
    lru_grads = tuple(
        (
            lax.dynamic_update_slice_in_dim(
                jnp.zeros((full_width,) + member.shape[1:], jnp.float32), member, first_row, 0
            )
            for member in local_grads
        )
    )
    lru_in_grad = outer_sum(normed_low, x_low)
    gelu_in_grad = outer_sum(normed_low, pre_low)
    normed_grad = times_transpose(x_low, whole_lru_in) + times_transpose(pre_low, whole_gelu_in)
    unused, pull_norm = jax.vjp(rms_scale, resid_in, mix_scale)
    input_part, mix_gain_grad = pull_norm(normed_grad)
    input_grad = middle_grad + input_part
    cweight_grad, cbias_grad, rweight_grad, rbias_grad, iweight_grad, ibias_grad, decay_grad = (
        lru_grads
    )
    summed = (
        lax.psum_scatter(mix_gain_grad, ("seq", "fsdp"), scatter_dimension=0, tiled=True),
        lax.psum_scatter(lru_in_grad, ("seq", "fsdp"), scatter_dimension=0, tiled=True),
        lax.psum_scatter(gelu_in_grad, ("seq", "fsdp"), scatter_dimension=0, tiled=True),
        lax.psum_scatter(out_w_grad, ("seq", "fsdp"), scatter_dimension=0, tiled=True),
        lax.psum_scatter(cweight_grad, ("seq", "fsdp"), scatter_dimension=0, tiled=True),
        lax.psum_scatter(cbias_grad, ("seq", "fsdp"), scatter_dimension=0, tiled=True),
        lax.psum_scatter(rweight_grad, ("seq", "fsdp"), scatter_dimension=0, tiled=True),
        lax.psum_scatter(rbias_grad, ("seq", "fsdp"), scatter_dimension=0, tiled=True),
        lax.psum_scatter(iweight_grad, ("seq", "fsdp"), scatter_dimension=0, tiled=True),
        lax.psum_scatter(ibias_grad, ("seq", "fsdp"), scatter_dimension=0, tiled=True),
        lax.psum_scatter(decay_grad, ("seq", "fsdp"), scatter_dimension=0, tiled=True),
        lax.psum_scatter(mlp_gain_grad, ("seq", "fsdp"), scatter_dimension=0, tiled=True),
        lax.psum_scatter(gate_w_grad, ("seq", "fsdp"), scatter_dimension=0, tiled=True),
        lax.psum_scatter(up_w_grad, ("seq", "fsdp"), scatter_dimension=0, tiled=True),
        lax.psum_scatter(down_grad, ("seq", "fsdp"), scatter_dimension=0, tiled=True),
    )
    return (
        result.astype(jnp.bfloat16).reshape(tokens.shape),
        input_grad.astype(jnp.bfloat16).reshape(tokens.shape),
        summed[0],
        summed[1],
        summed[2],
        summed[3],
        summed[4],
        summed[5],
        summed[6],
        summed[7],
        summed[8],
        summed[9],
        summed[10],
        summed[11],
        summed[12],
        summed[13],
        summed[14],
    )


def solution(mesh):
    return jax.shard_map(
        local,
        mesh=mesh,
        in_specs=(
            P("fsdp", "seq", None),
            P("fsdp", "seq", None),
            P(("seq", "fsdp")),
            P(("seq", "fsdp"), None),
            P(("seq", "fsdp"), None),
            P(("seq", "fsdp"), None),
            P(("seq", "fsdp"), None),
            P(("seq", "fsdp")),
            P(("seq", "fsdp"), None),
            P(("seq", "fsdp")),
            P(("seq", "fsdp"), None),
            P(("seq", "fsdp")),
            P(("seq", "fsdp")),
            P(("seq", "fsdp")),
            P(("seq", "fsdp"), None),
            P(("seq", "fsdp"), None),
            P(("seq", "fsdp"), None),
        ),
        out_specs=(
            P("fsdp", "seq", None),
            P("fsdp", "seq", None),
            P(("seq", "fsdp")),
            P(("seq", "fsdp"), None),
            P(("seq", "fsdp"), None),
            P(("seq", "fsdp"), None),
            P(("seq", "fsdp"), None),
            P(("seq", "fsdp")),
            P(("seq", "fsdp"), None),
            P(("seq", "fsdp")),
            P(("seq", "fsdp"), None),
            P(("seq", "fsdp")),
            P(("seq", "fsdp")),
            P(("seq", "fsdp")),
            P(("seq", "fsdp"), None),
            P(("seq", "fsdp"), None),
            P(("seq", "fsdp"), None),
        ),
        check_vma=False,
    )
```

profile of v0, /device:TPU:0, one launch (start us, length us, event | category | flops | bytes accessed | tf_op | source)
XLA Modules:
  0.0 4876.0 jit_solution(2591172525948006429)
XLA Ops:
  12.8 42.9 all-reduce.98
  56.8 44.2 all-gather.8.cloned.1.call-done
  111.3 80.1 %all-gather = bf16[32,80,4]{1,2,0:T(4,128)(2,1)S(1)} all-gather(bf16[1,80,4]{1,2,0:T(4,128)(2,1)S(1)} %bitcast.240), channel_id=1, replica_groups=mesh['seq'=8,'fsdp'=4] {'seq','fsdp'}, dimensions={0}, use_global_device_ids=true | all-gather | bytes 21120 | tf_op jit(solution)/shard_map/all_gather | solution.py:215
  191.7 78.6 %all_gather.45 = bf16[2560,160]{1,0:T(8,128)(2,1)S(1)} all-gather(bf16[80,160]{1,0:T(8,128)(2,1)S(1)} %copy-done.119), channel_id=1, replica_groups=mesh['seq'=8,'fsdp'=4] {'seq','fsdp'}, dimensions={0}, use_global_device_ids=true | all-gather | bytes 844800 | tf_op jit(solution)/shard_map/all_gather | solution.py:217
  270.3 80.7 %all_gather.52 = bf16[2560,160]{1,0:T(8,128)(2,1)S(1)} all-gather(bf16[80,160]{1,0:T(8,128)(2,1)S(1)} %copy-done.120), channel_id=1, replica_groups=mesh['seq'=8,'fsdp'=4] {'seq','fsdp'}, dimensions={0}, use_global_device_ids=true | all-gather | bytes 844800 | tf_op jit(solution)/shard_map/all_gather | solution.py:219
  358.0 23.8 slice.655
  381.9 23.8 slice.659
  405.6 24.5 slice.656
  430.1 25.1 slice.657
  458.3 13.0 slice.662
  471.3 13.0 slice.663
  484.3 13.0 slice.661
  497.4 13.2 slice.665
  651.5 13.0 slice.660
  664.5 13.2 slice.725
  680.8 23.8 slice.654
  704.6 24.7 slice.727
  818.6 12.2 pad.266
  831.7 26.5 pad.268
  860.0 13.4 pad.285
  873.5 13.4 pad.286
  891.9 24.8 pad.267
  916.7 26.4 pad.288
  944.2 26.6 pad.287
  979.1 18.1 all-to-all-done.1
  1014.6 13.4 fusion.97
  1028.0 13.4 fusion.98
  1041.5 17.5 multiply_convert_fusion
  1059.0 14.3 fusion.99
  1073.3 15.3 multiply_reduce_fusion.5
  1107.3 24.2 slice.751
  1131.5 23.8 slice.758
  1155.3 23.8 slice.749
  1196.5 23.8 slice.753
  1220.3 23.9 slice.755
  1261.3 13.0 slice.762
  1274.3 13.0 slice.763
  1287.4 13.0 slice.761
  1300.4 13.2 slice.765
  1459.1 13.0 slice.760
  1472.1 13.0 slice.825
  1488.3 24.2 slice.827
  1601.2 12.0 pad.326
  1616.5 24.2 pad.328
  1640.7 26.6 pad.327
  1669.9 13.3 rev.9
  1698.6 12.0 pad.306
  1711.5 26.7 pad.308
  1740.8 26.4 pad.307
  1769.8 13.2 rev.8
  1827.8 23.9 all_to_all.64
  1861.5 20.9 fusion.105
  1882.4 21.3 fusion.106
  1904.7 20.8 fusion.56
  1926.8 12.9 fusion.8
  1959.8 39.4 all-reduce.97
  2003.9 67.9 %reduce-scatter.18.cloned.1.call-done = f32[80,160]{1,0:T(8,128)} async-done(((f32[2560,160]{1,0:T(8,128)}), f32[80,160]{1,0:T(8,128)}) %reduce-scatter.18.cloned.1.call-update) | async-done | bytes 51216 | tf_op jit(solution)/shard_map/reduce_scatter | solution.py:338
  2071.8 137.0 %reduce-scatter.20.cloned.1.call-done = f32[80,160]{1,0:T(8,128)} async-done(((f32[2560,160]{1,0:T(8,128)}), f32[80,160]{1,0:T(8,128)}) %reduce-scatter.20.cloned.1.call-update) | async-done | bytes 51216 | tf_op jit(solution)/shard_map/reduce_scatter | solution.py:340
  2208.8 444.4 %reduce-scatter.16.cloned.1.call-done = f32[80,2048]{1,0:T(8,128)} async-done(((f32[2560,2048]{1,0:T(8,128)}), f32[80,2048]{1,0:T(8,128)}) %reduce-scatter.16.cloned.1.call-update) | async-done | bytes 655376 | tf_op jit(solution)/shard_map/reduce_scatter | solution.py:335
  2653.3 449.1 %reduce-scatter.14.cloned.1.call-done = f32[64,2560]{1,0:T(8,128)} async-done(((f32[2048,2560]{1,0:T(8,128)}), f32[64,2560]{1,0:T(8,128)}) %reduce-scatter.14.cloned.1.call-update) | async-done | bytes 655376 | tf_op jit(solution)/shard_map/reduce_scatter | solution.py:334
  3102.4 449.0 %reduce-scatter.12.cloned.1.call-done = f32[64,2560]{1,0:T(8,128)} async-done(((f32[2048,2560]{1,0:T(8,128)}), f32[64,2560]{1,0:T(8,128)}) %reduce-scatter.12.cloned.1.call-update) | async-done | bytes 655376 | tf_op jit(solution)/shard_map/reduce_scatter | solution.py:333
  3551.3 440.8 %reduce-scatter.22.cloned.1.call-done = f32[64,6144]{1,0:T(8,128)} async-done(((f32[2048,6144]{1,0:T(8,128)}), f32[64,6144]{1,0:T(8,128)}) %reduce-scatter.22.cloned.1.call-update) | async-done | bytes 1572880 | tf_op jit(solution)/shard_map/reduce_scatter | solution.py:344
  3992.1 438.7 %reduce-scatter.24.cloned.1.call-done = f32[64,6144]{1,0:T(8,128)} async-done(((f32[2048,6144]{1,0:T(8,128)}), f32[64,6144]{1,0:T(8,128)}) %reduce-scatter.24.cloned.1.call-update) | async-done | bytes 1572880 | tf_op jit(solution)/shard_map/reduce_scatter | solution.py:345
  4430.8 438.5 %reduce-scatter.26.cloned.1.call-done = f32[192,2048]{1,0:T(8,128)} async-done(((f32[6144,2048]{1,0:T(8,128)}), f32[192,2048]{1,0:T(8,128)}) %reduce-scatter.26.cloned.1.call-update) | async-done | bytes 1572880 | tf_op jit(solution)/shard_map/reduce_scatter | solution.py:346
  (700 shorter events, 693.0 us)
Async XLA Ops:
  7.2 93.8 %all-gather.8.cloned.1.call-start = ((), (), s32[]{:S(2)}) async-start(), calls=%async_computation.13 | async-start | bytes 10813440 | tf_op jit(solution)/shard_map/all_gather | solution.py:212
  7.9 992.1 %all-gather.10.cloned.1.call-start = ((), (), s32[]{:S(2)}) async-start(), calls=%async_computation.14 | async-start | bytes 10813440 | tf_op jit(solution)/shard_map/all_gather | solution.py:213
  8.7 998.9 %all-gather.12.cloned.1.call-start = ((), (), s32[]{:S(2)}) async-start(), calls=%async_computation.15 | async-start | bytes 10813440 | tf_op jit(solution)/shard_map/all_gather | solution.py:214
  9.5 47.1 copy-start
  9.5 1005.1 %all-gather.14.cloned.1.call-start = ((), (), s32[]{:S(2)}) async-start(), calls=%async_computation.16 | async-start | bytes 25952256 | tf_op jit(solution)/shard_map/all_gather | solution.py:223
  10.1 1018.0 %all-gather.16.cloned.1.call-start = ((), (), s32[]{:S(2)}) async-start(), calls=%async_computation.17 | async-start | bytes 25952256 | tf_op jit(solution)/shard_map/all_gather | solution.py:224
  10.6 1030.8 %all-gather.18.cloned.1.call-start = ((), (), s32[]{:S(2)}) async-start(), calls=%async_computation.18 | async-start | bytes 25952256 | tf_op jit(solution)/shard_map/all_gather | solution.py:225
  56.8 44.2 copy-start.125
  106.5 85.2 %copy-start.119 = (bf16[80,160]{1,0:T(8,128)(2,1)S(1)}, bf16[80,160]{1,0:T(8,128)(2,1)}, u32[]{:S(2)}) copy-start(bf16[80,160]{1,0:T(8,128)(2,1)} %param.25) | copy-start | bytes 76804
  107.6 162.7 %copy-start.120 = (bf16[80,160]{1,0:T(8,128)(2,1)S(1)}, bf16[80,160]{1,0:T(8,128)(2,1)}, u32[]{:S(2)}) copy-start(bf16[80,160]{1,0:T(8,128)(2,1)} %param.27) | copy-start | bytes 76804
  107.6 243.4 %all-to-all-start = ((bf16[128,8,320]{0,2,1:T(8,128)(2,1)}), bf16[128,8,320]{0,2,1:T(8,128)(2,1)S(1)}, u32[]{:S(2)}, u32[]{:S(2)}) async-start(bf16[128,8,320]{0,2,1:T(8,128)(2,1)} %bitcast.3), calls=%async_computation | async-start | bytes 1310720 | tf_op jit(solution)/shard_map/all_to_all | solution.py:272
  358.0 372.8 %copy-start.7 = (f32[1024,320]{0,1:T(8,128)}, f32[1024,320]{0,1:T(8,128)S(1)}, u32[]{:S(2)}) copy-start(f32[1024,320]{0,1:T(8,128)S(1)} %multiply_exponential_fusion) | copy-start | bytes 3932164
  542.8 20.7 copy-start.35
  748.6 5.8 copy-start.81
  748.7 5.8 copy-start.82
  754.4 6.3 copy-start.41
  756.0 9.3 copy-start.77
  756.0 9.3 copy-start.78
  765.2 7.1 copy-start.36
  765.3 9.9 copy-start.115
  768.6 10.8 copy-start.75
  768.6 10.8 copy-start.76
  779.4 18.4 copy-start.100
  831.7 26.5 copy-start.97
  916.7 26.4 slice-start
  916.7 26.4 copy-start.56
  944.2 26.6 copy-start.26
  975.5 21.6 all-to-all-start.1
  1000.0 7.6 copy-start.24
  1013.5 75.1 %copy-start.1 = (f32[128,2048]{1,0:T(8,128)}, f32[128,2048]{1,0:T(8,128)S(1)}, u32[]{:S(2)}) copy-start(f32[128,2048]{1,0:T(8,128)S(1)} %get-tuple-element.152) | copy-start | bytes 3145732
  1090.5 9.7 copy-start.15
  1100.2 6.5 copy-start.8
  1102.5 92.8 %all-to-all-start.2 = ((bf16[128,8,320]{0,2,1:T(8,128)(2,1)}), bf16[128,8,320]{0,2,1:T(8,128)(2,1)}, u32[]{:S(2)}, u32[]{:S(2)}) async-start(bf16[128,8,320]{0,2,1:T(8,128)(2,1)} %bitcast.232), calls=%async_computation.2 | async-start | bytes 1310720 | tf_op jit(solution)/shard_map/all_to_all | solution.py:307
  1106.7 836.4 %reduce-scatter.28.cloned.1.call-start = ((), (), s32[]{:S(2)}) async-start(), calls=%async_computation.27 | async-start | bytes 1351680
  1179.1 7.1 copy-start.59
  1179.1 11.7 copy-start.58
  1345.8 21.0 copy-start.37
  1531.4 5.7 copy-start.87
  1531.4 5.6 copy-start.88
  1537.0 6.3 copy-start.42
  1538.6 9.3 copy-start.83
  1538.6 9.3 copy-start.84
  1547.8 6.8 copy-start.38
  1547.9 9.6 copy-start.116
  1550.9 10.8 copy-start.79
  1550.9 10.8 copy-start.80
  1561.7 18.5 copy-start.103
  1669.9 13.3 copy-start.57
  1740.8 26.4 copy-start.27
  1769.8 13.2 copy-start.4
  1769.8 13.2 copy-start.122
  1783.0 5.6 copy-start.67
  1798.5 273.3 %reduce-scatter.18.cloned.1.call-start = ((), (), s32[]{:S(2)}) async-start(), calls=%async_computation.22 | async-start | bytes 2703360 | tf_op jit(solution)/shard_map/reduce_scatter | solution.py:338
  1801.1 407.8 %reduce-scatter.20.cloned.1.call-start = ((), (), s32[]{:S(2)}) async-start(), calls=%async_computation.23 | async-start | bytes 2703360 | tf_op jit(solution)/shard_map/reduce_scatter | solution.py:340
  1805.1 848.2 %reduce-scatter.16.cloned.1.call-start = ((), (), s32[]{:S(2)}) async-start(), calls=%async_computation.21 | async-start | bytes 21626880 | tf_op jit(solution)/shard_map/reduce_scatter | solution.py:335
  1815.5 1286.9 %reduce-scatter.14.cloned.1.call-start = ((), (), s32[]{:S(2)}) async-start(), calls=%async_computation.20 | async-start | bytes 21626880 | tf_op jit(solution)/shard_map/reduce_scatter | solution.py:334
  1825.3 1726.0 %reduce-scatter.12.cloned.1.call-start = ((), (), s32[]{:S(2)}) async-start(), calls=%async_computation.19 | async-start | bytes 21626880 | tf_op jit(solution)/shard_map/reduce_scatter | solution.py:333
  1851.7 8.7 copy-start.18
  1860.5 2131.6 %reduce-scatter.22.cloned.1.call-start = ((), (), s32[]{:S(2)}) async-start(), calls=%async_computation.24 | async-start | bytes 51904512 | tf_op jit(solution)/shard_map/reduce_scatter | solution.py:344
  1882.4 2548.4 %reduce-scatter.24.cloned.1.call-start = ((), (), s32[]{:S(2)}) async-start(), calls=%async_computation.25 | async-start | bytes 51904512 | tf_op jit(solution)/shard_map/reduce_scatter | solution.py:345
  1903.7 2965.6 %reduce-scatter.26.cloned.1.call-start = ((), (), s32[]{:S(2)}) async-start(), calls=%async_computation.26 | async-start | bytes 51904512 | tf_op jit(solution)/shard_map/reduce_scatter | solution.py:346
  1944.5 7.6 copy-start.62
  1952.1 7.7 copy-start.121
  1952.1 50.6 %copy-start.126 = (f32[128]{0:T(128)S(1)}, f32[128]{0:T(128)}, u32[]{:S(2)}) copy-start(f32[128]{0:T(128)} %copy-done.125) | copy-start | bytes 1540
  (88 other events, 219.2 us)
Sparse Core Ops, SparseCore 0:
  10.9 89.9 all-gather.7
  103.8 93.3 all-gather.9
  200.1 99.1 all-gather.11
  302.1 156.5 all-gather.13
  461.4 152.8 all-gather.15
  617.0 152.8 all-gather.17
  1798.6 135.6 reduce-scatter.27
  1937.2 134.5 reduce-scatter.17
  2074.8 134.0 reduce-scatter.19
  2211.7 441.5 reduce-scatter.15
  2656.3 446.0 reduce-scatter.13
  3105.2 446.0 reduce-scatter.11
  3559.4 432.6 reduce-scatter.21
  4000.1 430.6 reduce-scatter.23
  4438.8 430.4 reduce-scatter.25
where the time goes:
time: 4890 us; the launch traced here: 4880 us
  waiting for transfers between devices  2930 us (60%)
  local copies, waits for them, and re-layouts  1220 us (25%)
  blocking collectives  346 us (7%)
  matrix products  223 us (5%)
  other arithmetic  125 us (3%)
    reduce_scatter x1, waiting for transfers between devices, local(): lax.psum_scatter(gelu_in_grad, ('seq', 'fsdp'), scatter_dimension=0, tile...  449 us
    reduce_scatter x1, waiting for transfers between devices, local(): lax.psum_scatter(lru_in_grad, ('seq', 'fsdp'), scatter_dimension=0, tiled...  449 us
    reduce_scatter x1, waiting for transfers between devices, local(): lax.psum_scatter(out_w_grad, ('seq', 'fsdp'), scatter_dimension=0, tiled=...  444 us
    reduce_scatter x1, waiting for transfers between devices, local(): lax.psum_scatter(gate_w_grad, ('seq', 'fsdp'), scatter_dimension=0, tiled...  441 us
    reduce_scatter x1, waiting for transfers between devices, local(): lax.psum_scatter(up_w_grad, ('seq', 'fsdp'), scatter_dimension=0, tiled=T...  439 us
    reduce_scatter x1, waiting for transfers between devices, local(): lax.psum_scatter(down_grad, ('seq', 'fsdp'), scatter_dimension=0, tiled=T...  438 us
    slice x62, local copies, waits for them, and re-layouts, mixer_backward(): lax.associative_scan(linear_pair, (shifted, states_grad), reverse=True, a...  380 us
    slice x60, local copies, waits for them, and re-layouts, mixer_forward(): lax.associative_scan(linear_pair, (factor, driving), axis=0)  356 us
  transfers between devices with their start and end apart: 18, of which 10 were waited for; matrix products, arithmetic and copies ran while one was open for 18% of the time, Pallas kernels for 0%

commit v1 on v0

v1 whole, which is shorter than its diff:
```python
import functools

import jax
import jax.numpy as jnp
from jax import lax
from jax.experimental import pallas as pl
from jax.experimental.pallas import tpu as pltpu
from jax.sharding import PartitionSpec as P

EPSILON = 1e-06
RATE_SCALE = 8.0
CHUNK = 128
LOW = jnp.bfloat16
WIDE = jnp.float32


def rms_scale(values, gain):
    scale = lax.rsqrt(jnp.mean(values * values, axis=-1, keepdims=True) + EPSILON)
    return values * scale * gain


def dot(left, right):
    return jnp.dot(left, right, preferred_element_type=WIDE)


def outer_sum(left, right):
    return lax.dot_general(left, right, (((0,), (0,)), ((), ())), preferred_element_type=WIDE)


def times_transpose(left, right):
    return lax.dot_general(left, right, (((1,), (1,)), ((), ())), preferred_element_type=WIDE)


def one_minus_exp(value):
    series = jnp.full_like(value, 1.0 / 40320.0)
    for bottom in (5040.0, 720.0, 120.0, 24.0, 6.0, 2.0, 1.0):
        series = 1.0 / bottom - value * series
    return jnp.where(value < 0.4, value * series, 1.0 - jnp.exp(-value))


def sigmoid(value):
    return 0.5 * jnp.tanh(0.5 * value) + 0.5


def lane_tiles(channels):
    return -(-channels // 128)


def put(tiles, rows, value):
    channels = value.shape[1]
    for n in range(lane_tiles(channels)):
        size = min(128, channels - n * 128)
        tiles[n, rows, 0:size] = value[:, n * 128 : n * 128 + size]


def get(tiles, rows, channels):
    return jnp.concatenate(
        [
            tiles[n, rows, 0 : min(128, channels - n * 128)]
            for n in range(lane_tiles(channels))
        ],
        axis=1,
    )


def scan_segments(step, count, tiles):
    def body(i, carried):
        return tuple(step(i, n, *carried[n]) for n in range(tiles))

    start = (jnp.zeros((8, 128), WIDE), jnp.ones((8, 128), WIDE))
    ends = lax.fori_loop(0, count, body, (start,) * tiles, unroll=4)
    return [jnp.concatenate([end[which] for end in ends], axis=1) for which in (0, 1)]


def mixer_forward_kernel(
    x_ref, wr_ref, wi_ref, par_ref,
    conv_ref, r_ref, i_ref, f_ref, m_ref, st_ref,
    ext, factors, drive, prod,
):
    positions, channels = x_ref.shape
    segment = positions // 8
    chunks = positions // CHUNK
    ext[0:8, :] = jnp.zeros((8, channels), WIDE)
    st_ref[0:8, :] = jnp.zeros((8, channels), WIDE)

    @pl.loop(0, chunks)
    def _(c):
        base = pl.multiple_of(c * CHUNK, CHUNK)
        ext[pl.ds(base + 8, CHUNK), :] = x_ref[pl.ds(base, CHUNK), :].astype(WIDE)

    @pl.loop(0, chunks)
    def _(c):
        base = pl.multiple_of(c * CHUNK, CHUNK)
        rows = pl.ds(base, CHUNK)
        block = ext[pl.ds(base, CHUNK + 8), :]
        conv = jnp.broadcast_to(par_ref[4:5, :], (CHUNK, channels))
        for k in range(4):
            conv = conv + par_ref[k : k + 1, :] * block[8 - k : 8 - k + CHUNK]
        conv_low = conv.astype(LOW)
        conv_ref[rows, :] = conv_low
        r = jax.nn.sigmoid(dot(conv_low, wr_ref[...]) + par_ref[5:6, :])
        gate = jax.nn.sigmoid(dot(conv_low, wi_ref[...]) + par_ref[6:7, :])
        log_decay = r * par_ref[7:8, :]
        m = jnp.sqrt(one_minus_exp(-2.0 * log_decay))
        r_ref[rows, :] = r
        i_ref[rows, :] = gate
        factor = jnp.exp(log_decay)
        f_ref[rows, :] = factor
        m_ref[rows, :] = m
        put(factors, rows, factor)
        put(drive, rows, m * gate * conv_low.astype(WIDE))

    def step(i, n, state, product):
        rows = pl.ds(i, 8, stride=segment)
        factor = factors[n, rows, :]
        state = factor * state + drive[n, rows, :]
        product = factor * product
        drive[n, rows, :] = state
        prod[n, rows, :] = product
        return state, product

    state, product = scan_segments(step, segment, lane_tiles(channels))
    state, product = state[:, :channels], product[:, :channels]
    carry = jnp.zeros((1, channels), WIDE)
    for k in range(8):
        for part in range(segment // CHUNK):
            base = k * segment + part * CHUNK
            rows = slice(base, base + CHUNK)
            st_ref[base + 8 : base + 8 + CHUNK, :] = (
                get(drive, rows, channels) + get(prod, rows, channels) * carry
            )
        carry = state[k : k + 1] + product[k : k + 1] * carry


def mixer_backward_kernel(
    ds_ref, x_ref, conv_ref, r_ref, i_ref, f_ref, m_ref, st_ref, wr_ref, wi_ref, par_ref,
    xg_ref, wrg_ref, wig_ref, sums_ref,
    ext, factors, adj, prod, cg, carries, wr_sum, wi_sum,
):
    positions, channels = x_ref.shape
    segment = positions // 8
    chunks = positions // CHUNK
    ext[0:8, :] = jnp.zeros((8, channels), WIDE)
    cg[pl.ds(positions, 8), :] = jnp.zeros((8, channels), WIDE)
    wr_sum[...] = jnp.zeros_like(wr_sum)
    wi_sum[...] = jnp.zeros_like(wi_sum)

    @pl.loop(0, chunks)
    def _(c):
        base = pl.multiple_of(c * CHUNK, CHUNK)
        ext[pl.ds(base + 8, CHUNK), :] = x_ref[pl.ds(base, CHUNK), :].astype(WIDE)
        put(adj, pl.ds(base, CHUNK), ds_ref[pl.ds(base, CHUNK), :].astype(WIDE))
        put(factors, pl.ds(base, CHUNK), f_ref[pl.ds(base, CHUNK), :])

    def step(j, n, flow, product):
        rows = pl.ds(segment - 1 - j, 8, stride=segment)
        factor = factors[n, rows, :]
        adjoint = adj[n, rows, :] + flow
        adj[n, rows, :] = adjoint
        prod[n, rows, :] = product
        return factor * adjoint, factor * product

    flow, product = scan_segments(step, segment, lane_tiles(channels))
    flow, product = flow[:, :channels], product[:, :channels]
    carry = jnp.zeros((1, channels), WIDE)
    for k in range(7, -1, -1):
        carries[k : k + 1, :] = carry
        carry = flow[k : k + 1] + product[k : k + 1] * carry

    def grads(c, sums):
        base = pl.multiple_of(c * CHUNK, CHUNK)
        rows = pl.ds(base, CHUNK)
        adjoint = get(adj, rows, channels) + get(prod, rows, channels) * carries[pl.ds(base // segment, 1), :]
        before = st_ref[pl.ds(base, CHUNK + 8), :][7 : 7 + CHUNK]
        conv_low = conv_ref[rows, :]
        conv = conv_low.astype(WIDE)
        r = r_ref[rows, :]
        gate = i_ref[rows, :]
        factor = f_ref[rows, :]
        m = m_ref[rows, :]
        driven = adjoint * gate
        by_log = adjoint * before * factor - driven * conv * factor * factor / m
        by_r = by_log * par_ref[7:8, :] * r * (1.0 - r)
        by_i = adjoint * m * conv * gate * (1.0 - gate)
        by_r_low = by_r.astype(LOW)
        by_i_low = by_i.astype(LOW)
        conv_grad = (
            driven * m
            + times_transpose(by_r_low, wr_ref[...])
            + times_transpose(by_i_low, wi_ref[...])
        )
        cg[rows, :] = conv_grad
        wr_sum[...] += outer_sum(conv_low, by_r_low)
        wi_sum[...] += outer_sum(conv_low, by_i_low)
        block = ext[pl.ds(base, CHUNK + 8), :]
        rows_of = [conv_grad * block[8 - k : 8 - k + CHUNK] for k in range(4)]
        rows_of += [conv_grad, by_r, by_i, by_log * r]
        return tuple(
            total + jnp.sum(member, axis=0, keepdims=True) for total, member in zip(sums, rows_of)
        )

    zero = jnp.zeros((1, channels), WIDE)
    sums = lax.fori_loop(0, chunks, grads, (zero,) * 8)
    for k in range(8):
        sums_ref[k : k + 1, :] = sums[k]
    size = wrg_ref.shape[1]
    for n in range(channels // size):
        block = slice(n * size, (n + 1) * size)
        wrg_ref[block, :] = wr_sum[block, block]
        wig_ref[block, :] = wi_sum[block, block]

    @pl.loop(0, chunks)
    def _(c):
        base = pl.multiple_of(c * CHUNK, CHUNK)
        block = cg[pl.ds(base, CHUNK + 8), :]
        total = jnp.zeros((CHUNK, channels), WIDE)
        for k in range(4):
            total = total + par_ref[k : k + 1, :] * block[k : k + CHUNK]
        xg_ref[pl.ds(base, CHUNK), :] = total.astype(LOW)


def mixer_forward(x, wr, wi, par):
    positions, channels = x.shape
    wide = jax.ShapeDtypeStruct((positions, channels), WIDE)
    return pl.pallas_call(
        mixer_forward_kernel,
        out_shape=(
            jax.ShapeDtypeStruct((positions, channels), LOW), wide, wide, wide, wide,
            jax.ShapeDtypeStruct((positions + 8, channels), WIDE),
        ),
        scratch_shapes=[pltpu.VMEM((positions + 8, channels), WIDE)]
        + [pltpu.VMEM((lane_tiles(channels), positions, 128), WIDE)] * 3,
        compiler_params=pltpu.CompilerParams(vmem_limit_bytes=48 * 2**20),
        name="mixer_forward",
    )(x, wr, wi, par)


def mixer_backward(ds, x, saved, wr, wi, par, size):
    positions, channels = x.shape
    square = jax.ShapeDtypeStruct((channels, size), WIDE)
    return pl.pallas_call(
        mixer_backward_kernel,
        out_shape=(
            jax.ShapeDtypeStruct((positions, channels), LOW), square, square,
            jax.ShapeDtypeStruct((8, channels), WIDE),
        ),
        scratch_shapes=[pltpu.VMEM((positions + 8, channels), WIDE)]
        + [pltpu.VMEM((lane_tiles(channels), positions, 128), WIDE)] * 3
        + [pltpu.VMEM((positions + 8, channels), WIDE), pltpu.VMEM((8, channels), WIDE)]
        + [pltpu.VMEM((channels, channels), WIDE)] * 2,
        compiler_params=pltpu.CompilerParams(vmem_limit_bytes=48 * 2**20),
        name="mixer_backward",
    )(ds, x, *saved, wr, wi, par)


def gather_columns(weights):
    shards = lax.axis_size("seq")
    rows = weights[0].shape[0]
    widths = [member.shape[1] // shards for member in weights]
    stacked = jnp.concatenate(
        [member.reshape(rows, shards, width) for member, width in zip(weights, widths)], axis=2
    )
    mine = lax.all_to_all(stacked.transpose(1, 0, 2), "seq", split_axis=0, concat_axis=0)
    whole = lax.all_gather(mine, "fsdp", axis=1)
    return whole.reshape(-1, sum(widths))


def scatter_columns(grad, widths, rows):
    shards, groups = lax.axis_size("seq"), lax.axis_size("fsdp")
    parts = grad.astype(LOW).reshape(shards, groups, rows, sum(widths)).transpose(1, 0, 2, 3)
    mine = lax.psum_scatter(parts, "fsdp", scatter_dimension=0, tiled=False)
    swapped = lax.all_to_all(mine, "seq", split_axis=0, concat_axis=0).astype(WIDE)
    outs, first = [], 0
    for width in widths:
        outs.append(swapped[:, :, first : first + width].transpose(1, 0, 2).reshape(rows, -1))
        first += width
    return outs


def block_diagonal(weight, blocks):
    size = weight.shape[1]
    shaped = weight.reshape(blocks, size, size)
    full = jnp.zeros((blocks, size, blocks, size), weight.dtype)
    for n in range(blocks):
        full = full.at[n, :, n, :].set(shaped[n])
    return full.reshape(blocks * size, blocks * size)


def local(
    tokens, cotangent, mix_gain, lru_in_weight, gelu_in_weight, out_weight, conv_weight, conv_bias,
    recurrence_weight, recurrence_bias, input_gate_weight, input_gate_bias, decay_param, mlp_gain,
    gate_weight, up_weight, down_weight,
):
    positions, width = tokens.shape[1:]
    rows = lru_in_weight.shape[0]
    shards = lax.axis_size("seq")
    channels = lru_in_weight.shape[1] // shards
    hidden_width = gate_weight.shape[1] // shards
    size = recurrence_weight.shape[1]

    gains = lax.all_gather(
        jnp.stack([mix_gain, mlp_gain], axis=1), ("seq", "fsdp"), axis=0, tiled=True
    ).astype(WIDE)
    mix_scale, mlp_scale = gains[:, 0], gains[:, 1]
    in_whole = gather_columns([lru_in_weight, gelu_in_weight])
    lru_params = lax.all_gather(
        jnp.concatenate(
            [
                recurrence_weight, input_gate_weight, conv_weight, conv_bias[:, None],
                recurrence_bias[:, None], input_gate_bias[:, None], decay_param[:, None],
            ],
            axis=1,
        ),
        "fsdp", axis=0, tiled=True,
    )
    out_whole = lax.all_gather(out_weight, "fsdp", axis=0, tiled=True)
    glu_whole = gather_columns([gate_weight, up_weight])
    down_whole = lax.all_gather(down_weight, "fsdp", axis=0, tiled=True)

    wr = block_diagonal(lru_params[:, :size], channels // size)
    wi = block_diagonal(lru_params[:, size : 2 * size], channels // size)
    vectors = lru_params[:, 2 * size :].astype(WIDE).T
    decay = vectors[7]
    par = jnp.concatenate([vectors[:7], -RATE_SCALE * jax.nn.softplus(-decay)[None]], axis=0)

    resid_in = tokens.reshape(positions, width).astype(WIDE)
    grad_low = cotangent.reshape(positions, width)
    normed_low = rms_scale(resid_in, mix_scale).astype(LOW)
    normed_all = lax.all_gather(normed_low, "seq", axis=0, tiled=True)
    grad_all = lax.all_gather(grad_low, "seq", axis=0, tiled=True)
    branch_x = dot(normed_all, in_whole[:, :channels]).astype(LOW)
    branch_pre = dot(normed_all, in_whole[:, channels:])
    branch_y = jax.nn.gelu(branch_pre)

    saved = mixer_forward(branch_x, wr, wi, par)
    states_f = saved[5][8:].astype(LOW).astype(WIDE)
    product = (states_f * branch_y).astype(LOW)
    mixed = lax.psum_scatter(
        dot(product, out_whole).astype(LOW), "seq", scatter_dimension=0, tiled=True
    )
    middle = resid_in + mixed.astype(WIDE)
    normed2_low = rms_scale(middle, mlp_scale).astype(LOW)
    normed2_all = lax.all_gather(normed2_low, "seq", axis=0, tiled=True)
    gate_whole, up_whole = glu_whole[:, :hidden_width], glu_whole[:, hidden_width:]
    gate_val = dot(normed2_all, gate_whole)
    up_val = dot(normed2_all, up_whole)
    hidden = (jax.nn.gelu(gate_val) * up_val).astype(LOW)
    fed = lax.psum_scatter(
        dot(hidden, down_whole).astype(LOW), "seq", scatter_dimension=0, tiled=True
    )
    result = middle + fed.astype(WIDE)

    hidden_grad = times_transpose(grad_all, down_whole)
    unused, pull_glu = jax.vjp(lambda first, second: jax.nn.gelu(first) * second, gate_val, up_val)
    gate_grad, up_grad = pull_glu(hidden_grad)
    gate_low, up_low = gate_grad.astype(LOW), up_grad.astype(LOW)
    normed2_grad = lax.psum_scatter(
        (times_transpose(gate_low, gate_whole) + times_transpose(up_low, up_whole)).astype(LOW),
        "seq", scatter_dimension=0, tiled=True,
    ).astype(WIDE)
    unused, pull_norm2 = jax.vjp(rms_scale, middle, mlp_scale)
    middle_part, mlp_gain_grad = pull_norm2(normed2_grad)
    middle_grad = grad_low.astype(WIDE) + middle_part
    mixed_all = lax.all_gather(middle_grad.astype(LOW), "seq", axis=0, tiled=True)

    product_grad = times_transpose(mixed_all, out_whole)
    states_grad = (product_grad * branch_y).astype(LOW)
    unused, pull_gelu = jax.vjp(jax.nn.gelu, branch_pre)
    (pre_grad,) = pull_gelu(product_grad * states_f)
    pre_low = pre_grad.astype(LOW)
    x_low, wr_grad, wi_grad, sums = mixer_backward(states_grad, branch_x, saved, wr, wi, par, size)

    normed_grad = lax.psum_scatter(
        (
            times_transpose(x_low, in_whole[:, :channels])
            + times_transpose(pre_low, in_whole[:, channels:])
        ).astype(LOW),
        "seq", scatter_dimension=0, tiled=True,
    ).astype(WIDE)
    unused, pull_norm = jax.vjp(rms_scale, resid_in, mix_scale)
    input_part, mix_gain_grad = pull_norm(normed_grad)
    input_grad = middle_grad + input_part

    down_grad = lax.psum_scatter(
        outer_sum(hidden, grad_all).astype(LOW), "fsdp", scatter_dimension=0, tiled=True
    ).astype(WIDE)
    glu_grad = jnp.concatenate(
        [outer_sum(normed2_all, gate_low), outer_sum(normed2_all, up_low)], axis=1
    )
    gate_w_grad, up_w_grad = scatter_columns(glu_grad, [hidden_width] * 2, rows)
    out_grad = lax.psum_scatter(
        outer_sum(product, mixed_all).astype(LOW), "fsdp", scatter_dimension=0, tiled=True
    ).astype(WIDE)
    in_grad = jnp.concatenate(
        [outer_sum(normed_all, x_low), outer_sum(normed_all, pre_low)], axis=1
    )
    lru_in_grad, gelu_in_grad = scatter_columns(in_grad, [channels] * 2, rows)
    small = jnp.concatenate(
        [
            wr_grad, wi_grad, sums[:7].T,
            (sums[7] * RATE_SCALE * jax.nn.sigmoid(-decay))[:, None],
        ],
        axis=1,
    )
    small = lax.psum_scatter(
        small.reshape(lax.axis_size("fsdp"), -1, small.shape[1]),
        "fsdp", scatter_dimension=0, tiled=False,
    )
    gain_parts = jnp.stack([mix_gain_grad, mlp_gain_grad]).reshape(2, -1, rows).transpose(1, 0, 2)
    gain_grads = lax.psum_scatter(
        gain_parts, ("seq", "fsdp"), scatter_dimension=0, tiled=False
    )
    first = 2 * size
    return (
        result.astype(LOW).reshape(tokens.shape),
        input_grad.astype(LOW).reshape(tokens.shape),
        gain_grads[0],
        lru_in_grad,
        gelu_in_grad,
        out_grad,
        small[:, first : first + 4],
        small[:, first + 4],
        small[:, :size],
        small[:, first + 5],
        small[:, size : 2 * size],
        small[:, first + 6],
        small[:, first + 7],
        gain_grads[1],
        gate_w_grad,
        up_w_grad,
        down_grad,
    )


def solution(mesh):
    tokens = P("fsdp", "seq", None)
    vector = P(("seq", "fsdp"))
    matrix = P(("seq", "fsdp"), None)
    ranks = (1, 2, 2, 2, 2, 1, 2, 1, 2, 1, 1, 1, 2, 2, 2)
    specs = (tokens, tokens) + tuple(vector if rank == 1 else matrix for rank in ranks)
    return jax.shard_map(local, mesh=mesh, in_specs=specs, out_specs=specs, check_vma=False)
```

time: 4890 us -> 1060 us (0.22)
  waiting for transfers between devices: 2930 us -> 606 us
  local copies, waits for them, and re-layouts: 1220 us -> 57.3 us
  blocking collectives: 346 us -> 206 us
  matrix products: 223 us -> 105 us
  other arithmetic: 125 us -> 27.9 us
    reduce_scatter x8 -> x6, waiting for transfers between devices: 2870 us -> 159 us  [the longest x1 50.3 us: local(): lax.psum_scatter((times_transpose(x_low, in_whole[:, :channels]) + times_...]
    slice x124 -> x5, local copies, waits for them, and re-layouts: 736 us -> 4.35 us  [the longest x1 1.71 us: local(): small[:, first + 7]]
    pad x72 -> x0, local copies, waits for them, and re-layouts: 410 us -> none  [the longest x36 207 us: mixer_forward(): lax.associative_scan(linear_pair, (factor, driving), axis=0)]
    all_gather x6 -> x8, waiting for transfers between devices: 44.2 us -> 257 us  [the longest x2 69.9 us: gather_columns(): whole = lax.all_gather(mine, 'fsdp', axis=1)]
    unnamed x16 -> x18, waiting for transfers between devices: 3.8 us -> 175 us
    all_gather x3 -> x2, blocking collectives: 239 us -> 73.2 us  [the longest x1 65.7 us: local(): lax.all_gather(jnp.stack([mix_gain, mlp_gain], axis=1), ('seq', 'fsdp'),...]
    add x77 -> x0, other arithmetic: 75.5 us -> none  [the longest x38 42.1 us: linear_pair(): return (first[0] * second[0], second[0] * first[1] + second[1])]
    all_to_all x1 -> x2, blocking collectives: 23.9 us -> 93.2 us  [gather_columns(): lax.all_to_all(stacked.transpose(1, 0, 2), 'seq', split_axis=0, concat_ax...]
  transfers between devices with their start and end apart: 18 -> 18, of which waited for: 10 -> 16; matrix products, arithmetic and copies ran while one was open for 18% -> 11% of each run, Pallas kernels for 0% -> 1%
where the time goes in v1:
time: 1060 us; the launch traced here: 1050 us
  waiting for transfers between devices  606 us (57%)
  blocking collectives  206 us (19%)
  matrix products  105 us (10%)
  local copies, waits for them, and re-layouts  57.3 us (5%)
  other arithmetic  27.9 us (3%)
  Pallas kernels  25.4 us (2%)
  between operations  15.1 us (1%)
    unnamed x18, waiting for transfers between devices  175 us
    all_to_all x2, blocking collectives, gather_columns(): lax.all_to_all(stacked.transpose(1, 0, 2), 'seq', split_axis=0, concat_ax...  93.2 us
    all_gather x2, waiting for transfers between devices, gather_columns(): whole = lax.all_gather(mine, 'fsdp', axis=1)  69.9 us
    all_gather x1, blocking collectives, local(): lax.all_gather(jnp.stack([mix_gain, mlp_gain], axis=1), ('seq', 'fsdp'),...  65.7 us
    reduce_scatter x1, waiting for transfers between devices, local(): lax.psum_scatter((times_transpose(x_low, in_whole[:, :channels]) + times_...  50.3 us
    reduce_scatter x1, waiting for transfers between devices, local(): lax.psum_scatter((times_transpose(gate_low, gate_whole) + times_transpose...  48.8 us
    all_gather x1, waiting for transfers between devices, local(): grad_all = lax.all_gather(grad_low, 'seq', axis=0, tiled=True)  48.8 us
    all_gather x1, waiting for transfers between devices, local(): normed2_all = lax.all_gather(normed2_low, 'seq', axis=0, tiled=True)  41.8 us
  transfers between devices with their start and end apart: 18, of which 16 were waited for; matrix products, arithmetic and copies ran while one was open for 11% of the time, Pallas kernels for 1%

profile of v1, /device:TPU:0, one launch (start us, length us, event | category | flops | bytes accessed | tf_op | source)
XLA Modules:
  0.0 1051.8 jit_solution(18307707404158970074)
XLA Ops:
  10.3 24.4 %all_to_all.20 = bf16[8,64,640]{2,1,0:T(8,128)(2,1)S(1)} all-to-all(bf16[8,64,640]{2,1,0:T(8,128)(2,1)S(1)} %copy.163), channel_id=1, replica_groups=mesh['seq'=8,'fsdp'=4] {'seq'}, dimensions={0} | all-to-all | bytes 1310720 | tf_op jit(solution)/shard_map/all_to_all | solution.py:263
  36.0 65.7 %all-gather.3 = bf16[32,64,2]{1,2,0:T(2,128)(2,1)S(1)} all-gather(bf16[1,64,2]{1,2,0:T(2,128)(2,1)S(1)} %maximum_bitcast_fusion.5), channel_id=1, replica_groups=mesh['seq'=8,'fsdp'=4] {'seq','fsdp'}, dimensions={0}, use_global_device_ids=true | all-gather | bytes 8448 | tf_op jit(solution)/shard_map/all_gather | solution.py:301
  104.7 7.4 all_gather.40
  113.7 3.6 copy.165
  117.3 29.0 %all-gather.13.cloned.1.call-done = bf16[1024,2048]{1,0:T(8,128)(2,1)} async-done(((bf16[128,2048]{1,0:T(8,128)(2,1)}), bf16[1024,2048]{1,0:T(8,128)(2,1)}) %all-gather.13.cloned.1.call-update) | async-done | bytes 4194320 | tf_op jit(solution)/shard_map/all_gather | solution.py:329
  146.3 5.1 convolution_convert_fusion.7.x_ref
  151.4 11.6 %mixer_forward.1 = (bf16[1024,320]{1,0:T(8,128)(2,1)S(1)}, f32[1024,320]{1,0:T(8,128)S(1)}, f32[1024,320]{1,0:T(8,128)S(1)}, f32[1024,320]{1,0:T(8,128)}, f32[1024,320]{1,0:T(8,128)}, /*index=5*/f32[1032,320]{1,0:T(8,128)}) custom-call(bf16[1024,320]{1,0:T(8,128)(2,1)S(1)} %convolution_convert_fusion.7.x_ref, bf16[320,320]{1,0:T(8,128)(2,1)S(1)} %reshape.354.wr_ref, ...), custom_call_target="tpu_custom_call" | custom-call | tf_op jit(solution)/shard_map/mixer_forward/pallas_call | solution.py:225
  165.1 5.6 fusion.21
  170.7 5.0 all-gather.15.cloned.1.call-done
  175.7 5.9 convolution_convert_fusion
  184.8 68.7 %all_to_all.21 = bf16[8,64,1536]{2,1,0:T(8,128)(2,1)S(1)} all-to-all(bf16[8,64,1536]{2,1,0:T(8,128)(2,1)S(1)} %copy.180), channel_id=1, replica_groups=mesh['seq'=8,'fsdp'=4] {'seq'}, dimensions={0} | all-to-all | bytes 3145728 | tf_op jit(solution)/shard_map/all_to_all | solution.py:263
  253.5 2.0 copy.181
  255.6 5.3 reduce-scatter.16.cloned.1.call-done
  262.3 2.0 multiply_convert_fusion.3
  266.1 69.8 %all-gather.25.cloned.1.call-done = bf16[8,256,1536]{2,0,1:T(8,128)(2,1)} async-done(((bf16[8,64,1536]{2,0,1:T(8,128)(2,1)}), bf16[8,256,1536]{2,0,1:T(8,128)(2,1)}) %all-gather.25.cloned.1.call-update) | async-done | bytes 6291472 | tf_op jit(solution)/shard_map/all_gather | solution.py:264
  335.9 7.4 copy.182
  343.3 41.8 %all-gather.17.cloned.1.call-done = bf16[1024,2048]{1,0:T(8,128)(2,1)} async-done(((bf16[128,2048]{1,0:T(8,128)(2,1)}), bf16[1024,2048]{1,0:T(8,128)(2,1)}) %all-gather.17.cloned.1.call-update) | async-done | bytes 4194320 | tf_op jit(solution)/shard_map/all_gather | solution.py:343
  385.1 8.4 fusion.15
  393.5 5.1 fusion.19
  398.6 31.1 %all-gather.19.cloned.1.call-done = bf16[768,2048]{1,0:T(8,128)(2,1)} async-done(((bf16[192,2048]{1,0:T(8,128)(2,1)}), bf16[768,2048]{1,0:T(8,128)(2,1)}) %all-gather.19.cloned.1.call-update) | async-done | bytes 3145744 | tf_op jit(solution)/shard_map/all_gather | solution.py:318
  429.7 48.8 %all-gather.27.cloned.1.call-done = bf16[1,1024,2048]{2,1,0:T(8,128)(2,1)} async-done(((bf16[1,128,2048]{2,1,0:T(8,128)(2,1)}), bf16[1,1024,2048]{2,1,0:T(8,128)(2,1)}) %all-gather.27.cloned.1.call-update) | async-done | bytes 4194320 | tf_op jit(solution)/shard_map/all_gather | solution.py:330
  478.5 12.0 %multiply_convert_fusion = (bf16[1024,768]{1,0:T(8,128)(2,1)S(1)}, bf16[1024,768]{1,0:T(8,128)(2,1)S(1)}, bf16[1024,768]{1,0:T(8,128)(2,1)}) fusion(f32[1024,768]{1,0:T(8,128)} %fusion.19, f32[1024,768]{1,0:T(8,128)} %fusion.15, bf16[768,2048]{1,0:T(8,128)(2,1)} %all-gather.19.cloned.1.call-done, bf16[1,1024,2048]{2,1,0:T(8,128)(2,1)} %all-gather.27.cloned.1.call-done), kind=kOutput, calls=%fused_computation.21 | convolution fusion | flops 3241672704 | bytes 18350080 | tf_op jit(solution)/shard_map/dot_general | solution.py:31
  490.4 6.5 fusion.17
  496.9 6.9 add_convert_fusion.1
  503.9 48.8 %reduce-scatter.20.cloned.1.call-done = bf16[128,2048]{1,0:T(8,128)(2,1)} async-done(((bf16[1024,2048]{1,0:T(8,128)(2,1)}), bf16[128,2048]{1,0:T(8,128)(2,1)}) %reduce-scatter.20.cloned.1.call-update) | async-done | bytes 524304 | tf_op jit(solution)/shard_map/reduce_scatter | solution.py:357
  552.7 1.7 fusion.41
  554.4 2.6 fusion.56
  557.1 6.3 convolution_convert_fusion.2
  563.5 3.9 convolution_convert_fusion.3
  567.4 3.2 maximum_bitcast_fusion
  570.7 31.7 %all-gather.21.cloned.1.call-done = bf16[1024,2048]{1,0:T(8,128)(2,1)} async-done(((bf16[128,2048]{1,0:T(8,128)(2,1)}), bf16[1024,2048]{1,0:T(8,128)(2,1)}) %all-gather.21.cloned.1.call-update) | async-done | bytes 4194320 | tf_op jit(solution)/shard_map/all_gather | solution.py:364
  602.4 7.8 fusion.28
  611.1 2.7 convolution_convert_fusion.5
  613.8 2.5 copy.187
  618.6 13.8 %mixer_backward.1 = (bf16[1024,320]{1,0:T(8,128)(2,1)S(1)}, f32[320,160]{1,0:T(8,128)S(1)}, f32[320,160]{1,0:T(8,128)S(1)}, f32[8,320]{1,0:T(8,128)S(1)}) custom-call(bf16[1024,320]{1,0:T(8,128)(2,1)S(1)} %copy-done.5, bf16[1024,320]{1,0:T(8,128)(2,1)S(1)} %convolution_convert_fusion.7.x_ref, bf16[1024,320]{1,0:T(8,128)(2,1)S(1)} %copy-done.4, ...), custom_call_target="tpu_custom_call" | custom-call | tf_op jit(solution)/shard_map/mixer_backward/pallas_call | solution.py:241
  633.3 2.7 convolution_convert_fusion.6
  636.0 2.6 copy.186
  638.6 4.0 maximum_bitcast_fusion.1
  642.7 1.3 copy-done.43
  644.0 7.0 fusion.4
  653.5 5.6 convolution_convert_fusion.4
  659.2 2.4 fusion.32
  661.6 4.5 add_convert_fusion
  666.2 2.2 copy-done.39
  668.3 6.4 convolution_convert_fusion.1
  676.0 146.7 %all-reduce.9.cloned.1.call-done = (bf16[4,8,64,640]{3,2,0,1:T(8,128)(2,1)}, bf16[4,8,64,1536]{3,2,0,1:T(8,128)(2,1)}) async-done(((bf16[4,8,64,640]{3,2,0,1:T(8,128)(2,1)}, bf16[4,8,64,1536]{3,2,0,1:T(8,128)(2,1)}), (bf16[4,8,64,640]{3,2,0,1:T(8,128)(2,1)}, bf16[4,8,64,1536]{3,2,0,1:T(8,128)(2,1)})) %all-reduce.9.cloned.1.call-update) | async-done | bytes 8912912
  822.7 2.6 dynamic-slice_bitcast_fusion.1
  825.3 4.6 all-to-all-start.2
  830.0 3.3 dynamic-slice_bitcast_fusion
  833.3 14.9 %all-to-all-done.2 = bf16[8,64,640]{2,1,0:T(8,128)(2,1)S(1)} async-done(((bf16[8,64,640]{2,1,0:T(8,128)(2,1)}), bf16[8,64,640]{2,1,0:T(8,128)(2,1)S(1)}, u32[]{:S(2)}, u32[]{:S(2)}) %all-to-all-start.2) | async-done | bytes 655392 | tf_op jit(solution)/shard_map/all_to_all | solution.py:272
  849.0 3.6 all-to-all-start.3
  852.6 17.5 %reduce-scatter.26.cloned.1.call-done = bf16[192,2048]{1,0:T(8,128)(2,1)} async-done(((bf16[768,2048]{1,0:T(8,128)(2,1)}), bf16[192,2048]{1,0:T(8,128)(2,1)}) %reduce-scatter.26.cloned.1.call-update) | async-done | bytes 786448 | tf_op jit(solution)/shard_map/reduce_scatter | solution.py:384
  870.1 2.5 convert_element_type.129
  872.7 25.8 %reduce-scatter.28.cloned.1.call-done = f32[1,80,328]{2,1,0:T(8,128)} async-done(((f32[4,80,328]{2,1,0:T(8,128)}), f32[1,80,328]{2,1,0:T(8,128)}) %reduce-scatter.28.cloned.1.call-update) | async-done | bytes 104976
  900.0 1.7 slice_reduce_fusion
  901.7 1.7 fusion.57
  903.4 27.8 %reduce-scatter.24.cloned.1.call-done = bf16[80,2048]{1,0:T(8,128)(2,1)} async-done(((bf16[320,2048]{1,0:T(8,128)(2,1)}), bf16[80,2048]{1,0:T(8,128)(2,1)}) %reduce-scatter.24.cloned.1.call-update) | async-done | bytes 327696 | tf_op jit(solution)/shard_map/reduce_scatter | solution.py:391
  931.2 1.9 convert_element_type.126
  933.1 50.3 %reduce-scatter.22.cloned.1.call-done = bf16[128,2048]{1,0:T(8,128)(2,1)} async-done(((bf16[1024,2048]{1,0:T(8,128)(2,1)}), bf16[128,2048]{1,0:T(8,128)(2,1)}) %reduce-scatter.22.cloned.1.call-update) | async-done | bytes 524304 | tf_op jit(solution)/shard_map/reduce_scatter | solution.py:373
  983.4 1.6 fusion.42
  985.1 40.0 %all-reduce.2 = f32[32,2,64]{2,1,0:T(2,128)S(1)} all-reduce(f32[32,2,64]{2,1,0:T(2,128)S(1)} %maximum_bitcast_fusion.4), channel_id=9, replica_groups=mesh['seq'=8,'fsdp'=4] {'seq','fsdp'}, use_global_device_ids=true, to_apply=%region_10.11.clone | all-reduce | flops 4096 | bytes 32768
  1025.6 9.1 reduce-scatter.18.cloned.1.call-done
  1034.8 3.3 fusion.49
  1042.2 1.3 copy.205
  (187 shorter events, 33.6 us)
Async XLA Ops:
  7.2 106.5 %all-gather.23.cloned.1.call-start = ((), (), s32[]{:S(2)}) async-start(), calls=%async_computation.22 | async-start | bytes 3276800 | tf_op jit(solution)/shard_map/all_gather | solution.py:264
  9.8 26.2 %copy-start.40 = (bf16[64]{0:T(256)(128)(2,1)S(1)}, bf16[64]{0:T(256)(128)(2,1)}, u32[]{:S(2)}) copy-start(bf16[64]{0:T(256)(128)(2,1)} %param.38) | copy-start | bytes 388
  9.8 26.2 %copy-start.41 = (bf16[64]{0:T(256)(128)(2,1)S(1)}, bf16[64]{0:T(256)(128)(2,1)}, u32[]{:S(2)}) copy-start(bf16[64]{0:T(256)(128)(2,1)} %param.27) | copy-start | bytes 388
  9.8 92.0 %copy-start.6 = (bf16[1,128,2048]{2,1,0:T(8,128)(2,1)S(1)}, bf16[1,128,2048]{2,1,0:T(8,128)(2,1)}, u32[]{:S(2)}) copy-start(bf16[1,128,2048]{2,1,0:T(8,128)(2,1)} %param.25) | copy-start | bytes 1572868
  10.2 93.7 %copy-start.27 = (bf16[80,4]{0,1:T(4,128)(2,1)S(1)}, bf16[80,4]{0,1:T(4,128)(2,1)}, u32[]{:S(2)}) copy-start(bf16[80,4]{0,1:T(4,128)(2,1)} %param.31) | copy-start | bytes 1924
  10.2 93.8 %copy-start.30 = (bf16[80]{0:T(256)(128)(2,1)S(1)}, bf16[80]{0:T(256)(128)(2,1)}, u32[]{:S(2)}) copy-start(bf16[80]{0:T(256)(128)(2,1)} %param.32) | copy-start | bytes 484
  10.2 93.9 %copy-start.31 = (bf16[80]{0:T(256)(128)(2,1)S(1)}, bf16[80]{0:T(256)(128)(2,1)}, u32[]{:S(2)}) copy-start(bf16[80]{0:T(256)(128)(2,1)} %param.34) | copy-start | bytes 484
  10.2 94.1 %copy-start.32 = (bf16[80]{0:T(256)(128)(2,1)S(1)}, bf16[80]{0:T(256)(128)(2,1)}, u32[]{:S(2)}) copy-start(bf16[80]{0:T(256)(128)(2,1)} %param.36) | copy-start | bytes 484
  10.2 94.2 %copy-start.33 = (bf16[80]{0:T(256)(128)(2,1)S(1)}, bf16[80]{0:T(256)(128)(2,1)}, u32[]{:S(2)}) copy-start(bf16[80]{0:T(256)(128)(2,1)} %param.37) | copy-start | bytes 484
  10.2 94.3 %copy-start.19 = (bf16[80,160]{1,0:T(8,128)(2,1)S(1)}, bf16[80,160]{1,0:T(8,128)(2,1)}, u32[]{:S(2)}) copy-start(bf16[80,160]{1,0:T(8,128)(2,1)} %param.33) | copy-start | bytes 76804
  10.3 94.3 %copy-start.20 = (bf16[80,160]{1,0:T(8,128)(2,1)S(1)}, bf16[80,160]{1,0:T(8,128)(2,1)}, u32[]{:S(2)}) copy-start(bf16[80,160]{1,0:T(8,128)(2,1)} %param.35) | copy-start | bytes 76804
  35.9 110.3 %all-gather.13.cloned.1.call-start = ((), (), s32[]{:S(2)}) async-start(), calls=%async_computation.11 | async-start | bytes 4718592 | tf_op jit(solution)/shard_map/all_gather | solution.py:329
  102.0 1.8 copy-start.28
  102.1 11.4 %copy-start.23 = (f32[128]{0:T(128)}, f32[128]{0:T(128)S(1)}, u32[]{:S(2)}) copy-start(f32[128]{0:T(128)S(1)} %fusion.54) | copy-start | bytes 1540
  103.1 72.6 %all-gather.15.cloned.1.call-start = ((), (), s32[]{:S(2)}) async-start(), calls=%async_computation.12 | async-start | bytes 1638400 | tf_op jit(solution)/shard_map/all_gather | solution.py:316
  103.9 157.1 %reduce-scatter.16.cloned.1.call-start = ((), (), s32[]{:S(2)}) async-start(), calls=%async_computation.13 | async-start | bytes 4718592 | tf_op jit(solution)/shard_map/reduce_scatter | solution.py:338
  113.6 37.8 %copy-start.18 = (f32[8,320]{1,0:T(8,128)}, f32[8,320]{1,0:T(8,128)S(1)}, u32[]{:S(2)}) copy-start(f32[8,320]{1,0:T(8,128)S(1)} %convert_bitcast_fusion) | copy-start | bytes 30724
  146.3 18.8 %copy-start.9 = (bf16[8,256,640]{2,1,0:T(8,128)(2,1)S(1)}, bf16[8,256,640]{2,1,0:T(8,128)(2,1)}, u32[]{:S(2)}) copy-start(bf16[8,256,640]{2,1,0:T(8,128)(2,1)} %copy.165) | copy-start | bytes 7864324
  146.3 18.8 %copy-start.34 = (bf16[1024,2048]{1,0:T(8,128)(2,1)S(1)}, bf16[1024,2048]{1,0:T(8,128)(2,1)}, u32[]{:S(2)}) copy-start(bf16[1024,2048]{1,0:T(8,128)(2,1)} %all-gather.13.cloned.1.call-done) | copy-start | bytes 12582916
  163.1 1.1 copy-start
  164.2 0.9 copy-start.3
  181.6 154.3 %all-gather.25.cloned.1.call-start = ((), (), s32[]{:S(2)}) async-start(), calls=%async_computation.23 | async-start | bytes 7864320 | tf_op jit(solution)/shard_map/all_gather | solution.py:264
  255.6 129.5 %all-gather.17.cloned.1.call-start = ((), (), s32[]{:S(2)}) async-start(), calls=%async_computation.14 | async-start | bytes 4718592 | tf_op jit(solution)/shard_map/all_gather | solution.py:343
  262.2 292.1 %copy-start.21 = (f32[128]{0:T(128)}, f32[128]{0:T(128)S(1)}, u32[]{:S(2)}) copy-start(f32[128]{0:T(128)S(1)} %fusion.55) | copy-start | bytes 1540
  264.3 165.4 %all-gather.19.cloned.1.call-start = ((), (), s32[]{:S(2)}) async-start(), calls=%async_computation.15 | async-start | bytes 3932160 | tf_op jit(solution)/shard_map/all_gather | solution.py:318
  265.1 213.4 %all-gather.27.cloned.1.call-start = ((), (), s32[]{:S(2)}) async-start(), calls=%async_computation.24 | async-start | bytes 4718592 | tf_op jit(solution)/shard_map/all_gather | solution.py:330
  265.8 286.9 %reduce-scatter.20.cloned.1.call-start = ((), (), s32[]{:S(2)}) async-start(), calls=%async_computation.17 | async-start | bytes 4718592 | tf_op jit(solution)/shard_map/reduce_scatter | solution.py:357
  385.1 8.4 copy-start.11
  385.1 8.4 copy-start.37
  490.4 6.5 copy-start.44
  490.4 6.5 copy-start.46
  503.8 98.6 %all-gather.21.cloned.1.call-start = ((), (), s32[]{:S(2)}) async-start(), calls=%async_computation.18 | async-start | bytes 4718592 | tf_op jit(solution)/shard_map/all_gather | solution.py:364
  554.4 9.1 copy-start.25
  557.0 265.7 %all-reduce.9.cloned.1.call-start = ((), (), s32[]{:S(2)}) async-start(), calls=%async_computation.26 | async-start | bytes 17825792
  557.1 6.4 copy-start.38
  557.1 6.4 copy-start.45
  602.4 8.7 copy-start.35
  610.2 0.9 copy-start.16
  616.3 1.1 copy-start.4
  617.5 1.1 copy-start.5
  618.6 14.7 %copy-start.36 = (bf16[1024,2048]{1,0:T(8,128)(2,1)S(1)}, bf16[1024,2048]{1,0:T(8,128)(2,1)}, u32[]{:S(2)}) copy-start(bf16[1024,2048]{1,0:T(8,128)(2,1)} %all-gather.13.cloned.1.call-done) | copy-start | bytes 12582916
  632.4 0.9 copy-start.1
  636.0 2.7 copy-start.12
  642.6 1.4 copy-start.43
  642.6 227.5 %reduce-scatter.26.cloned.1.call-start = ((), (), s32[]{:S(2)}) async-start(), calls=%async_computation.21 | async-start | bytes 3932160 | tf_op jit(solution)/shard_map/reduce_scatter | solution.py:384
  651.0 247.5 %reduce-scatter.28.cloned.1.call-start = ((), (), s32[]{:S(2)}) async-start(), calls=%async_computation.25 | async-start | bytes 614400
  653.5 5.7 copy-start.2
  653.5 5.7 copy-start.10
  653.5 277.8 %reduce-scatter.24.cloned.1.call-start = ((), (), s32[]{:S(2)}) async-start(), calls=%async_computation.20 | async-start | bytes 1638400 | tf_op jit(solution)/shard_map/reduce_scatter | solution.py:391
  659.1 324.3 %reduce-scatter.22.cloned.1.call-start = ((), (), s32[]{:S(2)}) async-start(), calls=%async_computation.19 | async-start | bytes 4718592 | tf_op jit(solution)/shard_map/reduce_scatter | solution.py:373
  659.2 2.4 copy-start.17
  666.1 2.3 copy-start.39
  666.1 368.7 %reduce-scatter.18.cloned.1.call-start = ((), (), s32[]{:S(2)}) async-start(), calls=%async_computation.16 | async-start | bytes 4718592 | tf_op jit(solution)/shard_map/reduce_scatter | solution.py:348
  825.3 22.8 %all-to-all-start.2 = ((bf16[8,64,640]{2,1,0:T(8,128)(2,1)}), bf16[8,64,640]{2,1,0:T(8,128)(2,1)S(1)}, u32[]{:S(2)}, u32[]{:S(2)}) async-start(bf16[8,64,640]{2,1,0:T(8,128)(2,1)} %dynamic-slice_bitcast_fusion.1), calls=%async_computation.6 | async-start | bytes 1310720 | tf_op jit(solution)/shard_map/all_to_all | solution.py:272
  833.3 150.1 %copy-start.7 = (bf16[1,128,2048]{2,1,0:T(8,128)(2,1)S(1)}, bf16[1,128,2048]{2,1,0:T(8,128)(2,1)}, u32[]{:S(2)}) copy-start(bf16[1,128,2048]{2,1,0:T(8,128)(2,1)} %param.25) | copy-start | bytes 1572868
  833.3 150.1 %copy-start.24 = (f32[128]{0:T(128)S(1)}, f32[128]{0:T(128)}, u32[]{:S(2)}) copy-start(f32[128]{0:T(128)} %copy-done.23) | copy-start | bytes 1540
  848.1 0.8 copy-start.14
  849.0 192.5 %all-to-all-start.3 = ((bf16[8,64,1536]{2,1,0:T(8,128)(2,1)}), bf16[8,64,1536]{2,1,0:T(8,128)(2,1)S(1)}, u32[]{:S(2)}, u32[]{:S(2)}) async-start(bf16[8,64,1536]{2,1,0:T(8,128)(2,1)} %dynamic-slice_bitcast_fusion), calls=%async_computation.8 | async-start | bytes 3145728 | tf_op jit(solution)/shard_map/all_to_all | solution.py:272
  852.6 172.6 %copy-start.29 = (f32[128]{0:T(128)S(1)}, f32[128]{0:T(128)}, u32[]{:S(2)}) copy-start(f32[128]{0:T(128)} %copy-done.28) | copy-start | bytes 1540
  852.6 182.2 %copy-start.8 = (bf16[128,2048]{1,0:T(8,128)(2,1)S(1)}, bf16[128,2048]{1,0:T(8,128)(2,1)}, u32[]{:S(2)}) copy-start(bf16[128,2048]{1,0:T(8,128)(2,1)} %reduce-scatter.16.cloned.1.call-done) | copy-start | bytes 1572868
  852.6 182.2 %copy-start.13 = (bf16[1,128,2048]{2,1,0:T(8,128)(2,1)S(1)}, bf16[1,128,2048]{2,1,0:T(8,128)(2,1)}, u32[]{:S(2)}) copy-start(bf16[1,128,2048]{2,1,0:T(8,128)(2,1)} %param.26) | copy-start | bytes 1572868
  852.6 182.2 %copy-start.22 = (f32[128]{0:T(128)S(1)}, f32[128]{0:T(128)}, u32[]{:S(2)}) copy-start(f32[128]{0:T(128)} %copy-done.21) | copy-start | bytes 1540
  852.6 182.2 %copy-start.26 = (f32[128]{0:T(128)S(1)}, f32[128]{0:T(128)}, u32[]{:S(2)}) copy-start(f32[128]{0:T(128)} %copy-done.25) | copy-start | bytes 1540
  1034.8 3.3 copy-start.15
  (1 other events, 0.7 us)
Sparse Core Ops, SparseCore 0:
  36.1 38.6 all-gather.22
  103.2 43.0 all-gather.12
  148.1 27.5 all-gather.14
  181.7 79.1 reduce-scatter.15
  262.6 73.2 all-gather.24
  337.9 47.1 all-gather.16
  387.0 42.6 all-gather.18
  431.3 47.1 all-gather.26
  503.9 48.7 reduce-scatter.19
  557.2 45.2 all-gather.20
  642.7 179.9 all-reduce.8
  825.8 44.2 reduce-scatter.25
  873.8 24.6 reduce-scatter.27
  901.9 29.3 reduce-scatter.23
  933.4 49.9 reduce-scatter.21
  985.5 49.1 reduce-scatter.17

commit v2 on v1

--- a/solution.py
+++ b/solution.py
@@ -70,6 +70,526 @@
     start = (jnp.zeros((8, 128), WIDE), jnp.ones((8, 128), WIDE))
     ends = lax.fori_loop(0, count, body, (start,) * tiles, unroll=4)
     return [jnp.concatenate([end[which] for end in ends], axis=1) for which in (0, 1)]
+
+
+MESH = pl.DeviceIdType.MESH
+VMEM_BYTES = 58 * 2**20
+ANY = pl.BlockSpec(memory_space=pl.ANY)
+HELD = pl.BlockSpec(memory_space=pltpu.VMEM)
+ROOT = 0.7978845608028654
+CUBE = 0.044715
+
+
+def dma(*shape):
+    return pltpu.SemaphoreType.DMA(shape)
+
+
+def remote(src, dst, send, recv, axis, index):
+    return pltpu.make_async_remote_copy(
+        src_ref=src, dst_ref=dst, send_sem=send, recv_sem=recv,
+        device_id={axis: index}, device_id_type=MESH,
+    )
+
+
+def gelu(value):
+    return 0.5 * value * (1.0 + jnp.tanh(ROOT * (value + CUBE * value * value * value)))
+
+
+def gelu_and_slope(value):
+    square = value * value
+    bent = jnp.tanh(ROOT * (value + CUBE * square * value))
+    half = 0.5 * (1.0 + bent)
+    slope = half + 0.5 * value * (1.0 - bent * bent) * (ROOT * (1.0 + 3.0 * CUBE * square))
+    return value * half, slope
+
+
+class Place:
+    def __init__(self, shards, groups):
+        self.shards, self.groups, self.line = shards, groups, shards // 2
+        self.s, self.f = lax.axis_index("seq"), lax.axis_index("fsdp")
+        self.z, self.c = self.s // 2, lax.rem(self.s, 2)
+        self.sibling = 2 * self.z + 1 - self.c
+
+    def enter(self, seq=True, fsdp=True):
+        barrier = pltpu.get_barrier_semaphore()
+        met = 0
+        for axis, mine, count, wanted in (
+            ("seq", self.s, self.shards, seq), ("fsdp", self.f, self.groups, fsdp),
+        ):
+            for d in range(1, count if wanted else 1):
+                pl.semaphore_signal(
+                    barrier, inc=1, device_id={axis: lax.rem(mine + d, count)}, device_id_type=MESH
+                )
+                met += 1
+        pl.semaphore_wait(barrier, met)
+
+
+class Spread:
+    def __init__(self, at, src, dst, send, recv, axis="fsdp"):
+        self.at, self.src, self.dst, self.send, self.recv, self.axis = at, src, dst, send, recv, axis
+        self.mine, self.count = (at.f, at.groups) if axis == "fsdp" else (at.s, at.shards)
+
+    def copy(self, d):
+        peer = lax.rem(self.mine + d, self.count)
+        return remote(
+            self.src(peer), self.dst(self.mine), self.send.at[d], self.recv.at[d], self.axis, peer
+        )
+
+    def start(self):
+        for d in range(1, self.count):
+            self.copy(d).start()
+
+    def source(self, d):
+        return lax.rem(self.mine + self.count - d, self.count)
+
+    def arrive(self, d):
+        origin = self.source(d)
+        remote(
+            self.src(origin), self.dst(origin), self.send.at[d], self.recv.at[d], self.axis, origin
+        ).wait_recv()
+
+    def sent(self):
+        for d in range(1, self.count):
+            self.copy(d).wait_send()
+
+    def finish(self):
+        for d in range(1, self.count):
+            self.arrive(d)
+        self.sent()
+
+
+class LineGather:
+    def __init__(self, at, src, buf, send, recv, pieces):
+        self.at, self.src, self.buf, self.send, self.recv, self.pieces = at, src, buf, send, recv, pieces
+        self.rows = buf.shape[1] // pieces
+
+    def copy(self, slot, piece, kind, first=False):
+        at = self.at
+        rows = pl.ds(piece * self.rows, self.rows)
+        there = self.buf.at[slot, rows]
+        peer = (at.sibling, at.s + 2, at.s - 2)[kind]
+        return remote(
+            self.src.at[rows] if first else there, there,
+            self.send.at[slot, piece, kind], self.recv.at[slot, piece], "seq", peer,
+        )
+
+    def start(self):
+        at = self.at
+        for piece in range(self.pieces):
+            @pl.when(at.z + 1 < at.line)
+            def _():
+                self.copy(at.s, piece, 1, True).start()
+
+            @pl.when(at.z > 0)
+            def _():
+                self.copy(at.s, piece, 2, True).start()
+
+            self.copy(at.s, piece, 0, True).start()
+
+    def arrive(self, chip):
+        at = self.at
+        slot = 2 * chip + at.c
+        for piece in range(self.pieces):
+            self.copy(slot, piece, 0).wait_recv()
+
+            @pl.when((chip < at.z) & (at.z + 1 < at.line))
+            def _():
+                self.copy(slot, piece, 1).start()
+
+            @pl.when((chip > at.z) & (at.z > 0))
+            def _():
+                self.copy(slot, piece, 2).start()
+
+            self.copy(slot, piece, 0).start()
+
+    def settle(self, chip):
+        for piece in range(self.pieces):
+            self.copy(2 * chip + 1 - self.at.c, piece, 0).wait_recv()
+
+    def distances(self, body):
+        at = self.at
+        self.settle(at.z)
+        body(at.z)
+
+        @pl.loop(1, at.line)
+        def _(d):
+            @pl.when(at.z - d >= 0)
+            def _():
+                self.arrive(at.z - d)
+
+            @pl.when(at.z + d < at.line)
+            def _():
+                self.arrive(at.z + d)
+
+            @pl.loop(0, 2)
+            def _(side):
+                chip = at.z - d + 2 * d * side
+
+                @pl.when((chip >= 0) & (chip < at.line))
+                def _():
+                    self.settle(chip)
+                    body(chip)
+
+    def sent(self):
+        at = self.at
+        for chip in range(at.line):
+            slot = 2 * chip + at.c
+            for piece in range(self.pieces):
+                self.copy(slot, piece, 0).wait_send()
+
+                @pl.when((chip <= at.z) & (at.z + 1 < at.line))
+                def _():
+                    self.copy(slot, piece, 1).wait_send()
+
+                @pl.when((chip >= at.z) & (at.z > 0))
+                def _():
+                    self.copy(slot, piece, 2).wait_send()
+
+
+class LineScatter:
+    def __init__(self, at, own, other, heard, out, into, sems, pieces):
+        self.at, self.own, self.other, self.heard, self.out, self.into = at, own, other, heard, out, into
+        self.sib_send, self.sib_recv, self.send, self.recv = sems
+        self.pieces = pieces
+        self.rows = own.shape[1] // pieces
+
+    @staticmethod
+    def scratch(line, rows, width, pieces):
+        low = pltpu.VMEM((line, rows, width), LOW)
+        return [
+            pltpu.VMEM((line, rows, width), WIDE), low, low, low,
+            pltpu.VMEM((line + 1, rows, width), LOW),
+            dma(line), dma(line), dma(line, pieces), dma(line + 1, pieces),
+        ]
+
+    def across(self, chip):
+        return remote(
+            self.other.at[chip], self.heard.at[chip], self.sib_send.at[chip],
+            self.sib_recv.at[chip], "seq", self.at.sibling,
+        )
+
+    def along(self, chip, piece, up):
+        at = self.at
+        rows = pl.ds(pl.multiple_of(piece * self.rows, self.rows), self.rows)
+        there = chip if up else jnp.where(chip == at.z - 1, at.line, chip)
+        return remote(
+            self.out.at[chip, rows], self.into.at[there, rows], self.send.at[chip, piece],
+            self.recv.at[there, piece], "seq", at.s + 2 if up else at.s - 2,
+        )
+
+    def landed(self, index, piece):
+        rows = pl.ds(pl.multiple_of(piece * self.rows, self.rows), self.rows)
+        there = self.into.at[index, rows]
+        remote(
+            there, there, self.recv.at[index, piece], self.recv.at[index, piece], "seq", self.at.sibling
+        ).wait_recv()
+
+    def add(self, chip, piece, extras, store):
+        @pl.loop(0, self.rows // 16)
+        def _(block):
+            rows = pl.ds(pl.multiple_of(piece * self.rows + block * 16, 16), 16)
+            total = self.own[chip, rows, :] + self.heard[chip, rows, :].astype(WIDE)
+            for known, index in extras:
+                total = total + jnp.where(known, self.into[index, rows, :].astype(WIDE), 0.0)
+            store(rows, total)
+
+    def step(self, k):
+        at = self.at
+        for up in (True, False):
+            chip = at.line - 1 - k if up else k
+            passes = at.z > 0 if up else at.z + 1 < at.line
+
+            @pl.when(chip > at.z if up else chip < at.z)
+            def _():
+                self.across(chip).wait_recv()
+
+                @pl.loop(0, self.pieces)
+                def _(piece):
+                    @pl.when(passes)
+                    def _():
+                        self.landed(chip, piece)
+
+                    def store(rows, total):
+                        self.out[chip, rows, :] = total.astype(LOW)
+
+                    self.add(chip, piece, [(passes, chip)], store)
+                    self.along(chip, piece, up).start()
+
+    def steps(self, first=0):
+        @pl.loop(first, self.at.line - 1)
+        def _(k):
+            self.step(k)
+
+    def finish(self, store):
+        at = self.at
+        below, above = at.z > 0, at.z + 1 < at.line
+        self.across(at.z).wait_recv()
+
+        @pl.loop(0, self.pieces)
+        def _(piece):
+            @pl.when(below)
+            def _():
+                self.landed(at.z, piece)
+
+            @pl.when(above)
+            def _():
+                self.landed(at.line, piece)
+
+            self.add(at.z, piece, [(below, at.z), (above, at.line)], store)
+
+    def sent(self):
+        at = self.at
+        for chip in range(at.line):
+            self.across(chip).wait_send()
+
+            @pl.loop(0, self.pieces)
+            def _(piece):
+                @pl.when(chip > at.z)
+                def _():
+                    self.along(chip, piece, True).wait_send()
+
+                @pl.when(chip < at.z)
+                def _():
+                    self.along(chip, piece, False).wait_send()
+
+
+def normalise(source, gain, store, rows):
+    @pl.loop(0, rows // 16)
+    def _(block):
+        here = pl.ds(pl.multiple_of(block * 16, 16), 16)
+        values = source(here)
+        scale = lax.rsqrt(jnp.mean(values * values, axis=-1, keepdims=True) + EPSILON)
+        store(here, (values * scale * gain).astype(LOW))
+
+
+def mixer_rows(positions):
+    return [pl.ds(pl.multiple_of(n, CHUNK), CHUNK) for n in range(0, positions, CHUNK)]
+
+
+def mix_in_kernel(
+    tokens, in_shard, glu_shard, out_shard, down_shard, small, vecs, gain_shard,
+    normed, in_whole, x_ref, pre_ref, conv_ref, r_ref, i_ref, f_ref, m_ref, st_ref,
+    product_ref, par_ref, wr_ref, wi_ref, gains, glu_mine, out_whole, down_whole,
+    held, small_all, vecs_all, gain_all, ext, factors, drive, prod,
+    local_sems, tok_send, tok_recv, in_sems, in_xy_send, in_xy_recv, glu_sems, xy_sems, gain_sems,
+):
+    groups, shards = in_whole.shape[1], in_whole.shape[0]
+    at = Place(shards, groups)
+    s, f = at.s, at.f
+    positions, channels = x_ref.shape
+    width = tokens.shape[1]
+    rows = in_shard.shape[1]
+    segment = positions // 8
+    chunks = positions // CHUNK
+
+    keep = [
+        (tokens, held.at[s]), (in_shard.at[s], in_whole.at[s, f]), (glu_shard.at[s], glu_mine.at[s]),
+        (out_shard, out_whole.at[f]), (down_shard, down_whole.at[f]), (small, small_all.at[f]),
+        (vecs, vecs_all.at[f]), (gain_shard, gain_all.at[s, f]),
+    ]
+    keep = [pltpu.make_async_copy(a, b, local_sems.at[n]) for n, (a, b) in enumerate(keep)]
+    for copy in keep:
+        copy.start()
+    at.enter()
+
+    def over_fsdp(src, dst, n):
+        return Spread(at, lambda peer: src, lambda origin: dst.at[origin], xy_sems.at[n, 0], xy_sems.at[n, 1])
+
+    gain_xy = Spread(
+        at, lambda peer: gain_shard, lambda origin: gain_all.at[s, origin],
+        xy_sems.at[0, 0], xy_sems.at[0, 1],
+    )
+    small_xy = over_fsdp(small, small_all, 1)
+    vecs_xy = over_fsdp(vecs, vecs_all, 2)
+    out_xy = over_fsdp(out_shard, out_whole, 3)
+    down_xy = over_fsdp(down_shard, down_whole, 4)
+    in_z = Spread(
+        at, lambda peer: in_shard.at[peer], lambda origin: in_whole.at[origin, f],
+        in_sems.at[0], in_sems.at[1], "seq",
+    )
+    glu_z = Spread(
+        at, lambda peer: glu_shard.at[peer], lambda origin: glu_mine.at[origin],
+        glu_sems.at[0], glu_sems.at[1], "seq",
+    )
+    gain_z = Spread(
+        at, lambda peer: gain_all.at[s], lambda origin: gain_all.at[origin],
+        gain_sems.at[0], gain_sems.at[1], "seq",
+    )
+
+    def in_xy(index):
+        return Spread(
+            at, lambda peer: in_whole.at[index, f], lambda origin: in_whole.at[index, origin],
+            in_xy_send.at[index], in_xy_recv.at[index],
+        )
+
+    gather = LineGather(at, tokens, held, tok_send, tok_recv, tok_send.shape[1])
+    gain_xy.start()
+    in_z.start()
+    keep[1].wait()
+    in_xy(s).start()
+    gather.start()
+    vecs_xy.start()
+    small_xy.start()
+    keep[7].wait()
+    gain_xy.finish()
+    gain_z.start()
+    for d in range(1, shards):
+        in_z.arrive(d)
+        in_xy(in_z.source(d)).start()
+    out_xy.start()
+    gain_z.finish()
+    for origin in range(shards):
+        for other in range(groups):
+            first = (origin * groups + other) * rows
+            gains[:, first : first + rows] = gain_all[origin, other]
+    keep[0].wait()
+
+    def take(chip):
+        for core in range(2):
+            slot = 2 * chip + core
+
+            def store(here, value):
+                normed[slot, here, :] = value
+
+            normalise(
+                lambda here: held[slot, here, :].astype(WIDE), gains[0:1, :], store, tokens.shape[0]
+            )
+
+    gather.distances(take)
+    glu_z.start()
+    keep[6].wait()
+    vecs_xy.finish()
+    keep[5].wait()
+    small_xy.finish()
+    size = small.shape[1] // 2
+    local = small.shape[0]
+    wr_ref[...] = jnp.zeros_like(wr_ref)
+    wi_ref[...] = jnp.zeros_like(wi_ref)
+    flat = small_all[...].reshape(channels, 2 * size)
+    for n in range(channels // size):
+        block = slice(n * size, (n + 1) * size)
+        wr_ref[block, block] = flat[block, :size]
+        wi_ref[block, block] = flat[block, size:]
+    for other in range(groups):
+        par_ref[:, other * local : (other + 1) * local] = vecs_all[other]
+    ext[0:8, :] = jnp.zeros((8, channels), WIDE)
+    st_ref[0:8, :] = jnp.zeros((8, channels), WIDE)
+    for index in range(shards):
+        for d in range(1, groups):
+            in_xy(index).arrive(d)
+    down_xy.start()
+
+    @pl.loop(0, at.line)
+    def _(chip):
+        pair = normed[pl.ds(2 * chip, 2), :, :].reshape(2 * tokens.shape[0], width)
+        both = dot(pair, in_whole[...].reshape(width, 2 * channels))
+        base = pl.multiple_of(chip * 2 * tokens.shape[0], CHUNK)
+        here = pl.ds(base, 2 * tokens.shape[0])
+        x_low = both[:, :channels].astype(LOW)
+        x_ref[here, :] = x_low
+        ext[pl.ds(base + 8, 2 * tokens.shape[0]), :] = x_low.astype(WIDE)
+        pre_ref[here, :] = both[:, channels:]
+
+    @pl.loop(0, chunks)
+    def _(n):
+        base = pl.multiple_of(n * CHUNK, CHUNK)
+        here = pl.ds(base, CHUNK)
+        block = ext[pl.ds(base, CHUNK + 8), :]
+        conv = jnp.broadcast_to(par_ref[4:5, :], (CHUNK, channels))
+        for k in range(4):
+            conv = conv + par_ref[k : k + 1, :] * block[8 - k : 8 - k + CHUNK]
+        conv_low = conv.astype(LOW)
+        conv_ref[here, :] = conv_low
+        r = jax.nn.sigmoid(dot(conv_low, wr_ref[...]) + par_ref[5:6, :])
+        gate = jax.nn.sigmoid(dot(conv_low, wi_ref[...]) + par_ref[6:7, :])
+        log_decay = r * par_ref[7:8, :]
+        m = jnp.sqrt(one_minus_exp(-2.0 * log_decay))
+        factor = jnp.exp(log_decay)
+        r_ref[here, :] = r
+        i_ref[here, :] = gate
+        f_ref[here, :] = factor
+        m_ref[here, :] = m
+        put(factors, here, factor)
+        put(drive, here, m * gate * conv_low.astype(WIDE))
+
+    def step(i, n, state, product):
+        here = pl.ds(i, 8, stride=segment)
+        factor = factors[n, here, :]
+        state = factor * state + drive[n, here, :]
+        product = factor * product
+        drive[n, here, :] = state
+        prod[n, here, :] = product
+        return state, product
+
+    state, product = scan_segments(step, segment, lane_tiles(channels))
+    state, product = state[:, :channels], product[:, :channels]
+    carry = jnp.zeros((1, channels), WIDE)
+    for k in range(8):
+        for part in range(segment // CHUNK):
+            base = k * segment + part * CHUNK
+            here = slice(base, base + CHUNK)
+            states = get(drive, here, channels) + get(prod, here, channels) * carry
+            st_ref[base + 8 : base + 8 + CHUNK, :] = states
+            product_ref[here, :] = (
+                states.astype(LOW).astype(WIDE) * gelu(pre_ref[here, :])
+            ).astype(LOW)
+        carry = state[k : k + 1] + product[k : k + 1] * carry
+
+    glu_z.finish()
+    out_xy.finish()
+    down_xy.finish()
+    gather.sent()
+    in_z.sent()
+    for index in range(shards):
+        in_xy(index).sent()
+    for n in (2, 3, 4):
+        keep[n].wait()
+
+
+def mix_in(tokens, in_shard, glu_shard, out_shard, down_shard, small, vecs, gain_shard, groups):
+    shards, rows, both = in_shard.shape
+    block, width = tokens.shape
+    positions, channels = shards * block, both // 2
+    local = small.shape[0]
+    pieces = 2
+    wide = jax.ShapeDtypeStruct((positions, channels), WIDE)
+    low = jax.ShapeDtypeStruct((positions, channels), LOW)
+    square = jax.ShapeDtypeStruct((channels, channels), LOW)
+    held = [
+        jax.ShapeDtypeStruct((shards, block, width), LOW),
+        jax.ShapeDtypeStruct((shards, groups, rows, both), LOW),
+        low, wide, low, wide, wide, wide, wide,
+        jax.ShapeDtypeStruct((positions + 8, channels), WIDE),
+        low, jax.ShapeDtypeStruct((8, channels), WIDE), square, square,
+        jax.ShapeDtypeStruct((8, width), WIDE),
+    ]
+    far = [
+        jax.ShapeDtypeStruct((shards, rows, glu_shard.shape[2]), LOW),
+        jax.ShapeDtypeStruct((groups,) + out_shard.shape, LOW),
+        jax.ShapeDtypeStruct((groups,) + down_shard.shape, LOW),
+    ]
+    return pl.pallas_call(
+        mix_in_kernel,
+        out_shape=held + far,
+        in_specs=[HELD] + [ANY] * 7,
+        out_specs=[HELD] * len(held) + [ANY] * len(far),
+        scratch_shapes=[
+            pltpu.VMEM((shards, block, width), LOW),
+            pltpu.VMEM((groups,) + small.shape, LOW),
+            pltpu.VMEM((groups,) + vecs.shape, WIDE),
+            pltpu.VMEM((shards, groups) + gain_shard.shape, WIDE),
+            pltpu.VMEM((positions + 8, channels), WIDE),
+        ]
+        + [pltpu.VMEM((lane_tiles(channels), positions, 128), WIDE)] * 3
+        + [
+            dma(8), dma(shards, pieces, 3), dma(shards, pieces), dma(2, shards), dma(shards, groups),
+            dma(shards, groups), dma(2, shards), dma(5, 2, groups), dma(2, shards),
+        ],
+        compiler_params=pltpu.CompilerParams(
+            collective_id=1, has_side_effects=True, vmem_limit_bytes=VMEM_BYTES
+        ),
+        name="mix_in",
+    )(tokens, in_shard, glu_shard, out_shard, down_shard, small, vecs, gain_shard)
 
 
 def mixer_forward_kernel(
@@ -286,7 +806,7 @@
     return full.reshape(blocks * size, blocks * size)
 
 
-def local(
+def general(
     tokens, cotangent, mix_gain, lru_in_weight, gelu_in_weight, out_weight, conv_weight, conv_bias,
     recurrence_weight, recurrence_bias, input_gate_weight, input_gate_bias, decay_param, mlp_gain,
     gate_weight, up_weight, down_weight,
@@ -432,7 +952,159 @@
     )
 
 
+def aligned(
+    tokens, cotangent, mix_gain, lru_in_weight, gelu_in_weight, out_weight, conv_weight, conv_bias,
+    recurrence_weight, recurrence_bias, input_gate_weight, input_gate_bias, decay_param, mlp_gain,
+    gate_weight, up_weight, down_weight,
+):
+    positions, width = tokens.shape[1:]
+    rows = lru_in_weight.shape[0]
+    shards = lax.axis_size("seq")
+    channels = lru_in_weight.shape[1] // shards
+    hidden_width = gate_weight.shape[1] // shards
+    size = recurrence_weight.shape[1]
+
+    groups = lax.axis_size("fsdp")
+    resid_in = tokens.reshape(positions, width).astype(WIDE)
+    grad_low = cotangent.reshape(positions, width)
+
+    def by_column(first, second):
+        parts = [member.reshape(rows, shards, -1) for member in (first, second)]
+        return jnp.concatenate(parts, axis=2).transpose(1, 0, 2)
+
+    own_decay = decay_param.astype(WIDE)
+    vecs = jnp.concatenate(
+        [
+            conv_weight.astype(WIDE).T,
+            jnp.stack([conv_bias, recurrence_bias, input_gate_bias]).astype(WIDE),
+            -RATE_SCALE * jax.nn.softplus(-own_decay)[None],
+        ],
+        axis=0,
+    )
+    gain_shard = jnp.pad(jnp.stack([mix_gain, mlp_gain]).astype(WIDE), ((0, 6), (0, 0)))
+    (
+        normed_all, in_whole, branch_x, branch_pre, *saved, product, par, wr, wi, gains,
+        glu_mine, out_whole, down_whole,
+    ) = mix_in(
+        tokens.reshape(positions, width), by_column(lru_in_weight, gelu_in_weight),
+        by_column(gate_weight, up_weight), out_weight, down_weight,
+        jnp.concatenate([recurrence_weight, input_gate_weight], axis=1), vecs, gain_shard, groups,
+    )
+    normed_all = normed_all.reshape(-1, width)
+    in_whole = in_whole.reshape(width, -1)
+    out_whole = out_whole.reshape(-1, width)
+    down_whole = down_whole.reshape(-1, width)
+    mix_scale, mlp_scale = gains[0], gains[1]
+    glu_whole = lax.all_gather(glu_mine, "fsdp", axis=1).reshape(width, -1)
+    grad_all = lax.all_gather(grad_low, "seq", axis=0, tiled=True)
+    branch_y = jax.nn.gelu(branch_pre)
+    states_f = saved[5][8:].astype(LOW).astype(WIDE)
+    mixed = lax.psum_scatter(
+        dot(product, out_whole).astype(LOW), "seq", scatter_dimension=0, tiled=True
+    )
+    middle = resid_in + mixed.astype(WIDE)
+    normed2_low = rms_scale(middle, mlp_scale).astype(LOW)
+    normed2_all = lax.all_gather(normed2_low, "seq", axis=0, tiled=True)
+    gate_whole, up_whole = glu_whole[:, :hidden_width], glu_whole[:, hidden_width:]
+    gate_val = dot(normed2_all, gate_whole)
+    up_val = dot(normed2_all, up_whole)
+    hidden = (jax.nn.gelu(gate_val) * up_val).astype(LOW)
+    fed = lax.psum_scatter(
+        dot(hidden, down_whole).astype(LOW), "seq", scatter_dimension=0, tiled=True
+    )
+    result = middle + fed.astype(WIDE)
+
+    hidden_grad = times_transpose(grad_all, down_whole)
+    unused, pull_glu = jax.vjp(lambda first, second: jax.nn.gelu(first) * second, gate_val, up_val)
+    gate_grad, up_grad = pull_glu(hidden_grad)
+    gate_low, up_low = gate_grad.astype(LOW), up_grad.astype(LOW)
+    normed2_grad = lax.psum_scatter(
+        (times_transpose(gate_low, gate_whole) + times_transpose(up_low, up_whole)).astype(LOW),
+        "seq", scatter_dimension=0, tiled=True,
+    ).astype(WIDE)
+    unused, pull_norm2 = jax.vjp(rms_scale, middle, mlp_scale)
+    middle_part, mlp_gain_grad = pull_norm2(normed2_grad)
+    middle_grad = grad_low.astype(WIDE) + middle_part
+    mixed_all = lax.all_gather(middle_grad.astype(LOW), "seq", axis=0, tiled=True)
+
+    product_grad = times_transpose(mixed_all, out_whole)
+    states_grad = (product_grad * branch_y).astype(LOW)
+    unused, pull_gelu = jax.vjp(jax.nn.gelu, branch_pre)
+    (pre_grad,) = pull_gelu(product_grad * states_f)
+    pre_low = pre_grad.astype(LOW)
+    x_low, wr_grad, wi_grad, sums = mixer_backward(states_grad, branch_x, saved, wr, wi, par, size)
+
+    normed_grad = lax.psum_scatter(
+        (
+            times_transpose(x_low, in_whole[:, :channels])
+            + times_transpose(pre_low, in_whole[:, channels:])
+        ).astype(LOW),
+        "seq", scatter_dimension=0, tiled=True,
+    ).astype(WIDE)
+    unused, pull_norm = jax.vjp(rms_scale, resid_in, mix_scale)
+    input_part, mix_gain_grad = pull_norm(normed_grad)
+    input_grad = middle_grad + input_part
+
+    down_grad = lax.psum_scatter(
+        outer_sum(hidden, grad_all).astype(LOW), "fsdp", scatter_dimension=0, tiled=True
+    ).astype(WIDE)
+    glu_grad = jnp.concatenate(
+        [outer_sum(normed2_all, gate_low), outer_sum(normed2_all, up_low)], axis=1
+    )
+    gate_w_grad, up_w_grad = scatter_columns(glu_grad, [hidden_width] * 2, rows)
+    out_grad = lax.psum_scatter(
+        outer_sum(product, mixed_all).astype(LOW), "fsdp", scatter_dimension=0, tiled=True
+    ).astype(WIDE)
+    in_grad = jnp.concatenate(
+        [outer_sum(normed_all, x_low), outer_sum(normed_all, pre_low)], axis=1
+    )
+    lru_in_grad, gelu_in_grad = scatter_columns(in_grad, [channels] * 2, rows)
+    small = jnp.concatenate(
+        [
+            wr_grad, wi_grad, sums[:7].T,
+            (sums[7] * RATE_SCALE)[:, None],
+        ],
+        axis=1,
+    )
+    small = lax.psum_scatter(
+        small.reshape(lax.axis_size("fsdp"), -1, small.shape[1]),
+        "fsdp", scatter_dimension=0, tiled=False,
+    )
+    gain_parts = jnp.stack([mix_gain_grad, mlp_gain_grad]).reshape(2, -1, rows).transpose(1, 0, 2)
+    gain_grads = lax.psum_scatter(
+        gain_parts, ("seq", "fsdp"), scatter_dimension=0, tiled=False
+    )
+    first = 2 * size
+    return (
+        result.astype(LOW).reshape(tokens.shape),
+        input_grad.astype(LOW).reshape(tokens.shape),
+        gain_grads[0],
+        lru_in_grad,
+        gelu_in_grad,
+        out_grad,
+        small[:, first : first + 4],
+        small[:, first + 4],
+        small[:, :size],
+        small[:, first + 5],
+        small[:, size : 2 * size],
+        small[:, first + 6],
+        small[:, first + 7] * jax.nn.sigmoid(-own_decay),
+        gain_grads[1],
+        gate_w_grad,
+        up_w_grad,
+        down_grad,
+    )
+
+
 def solution(mesh):
+    shards, groups = mesh.shape["seq"], mesh.shape["fsdp"]
+
+    def local(*arrays):
+        rows, small_rows = arrays[3].shape[0], arrays[5].shape[0]
+        simple = shards % 2 == 0 and rows % 16 == 0 and small_rows % 16 == 0
+        simple = simple and arrays[0].shape[1] * shards % (8 * CHUNK) == 0
+        return (aligned if simple else general)(*arrays)
+
     tokens = P("fsdp", "seq", None)
     vector = P(("seq", "fsdp"))
     matrix = P(("seq", "fsdp"), None)

time: 1060 us -> 885 us (0.83)
  blocking collectives: 206 us -> 39.8 us
  Pallas kernels: 25.4 us -> 141 us
  waiting for transfers between devices: 606 us -> 510 us
  local copies, waits for them, and re-layouts: 57.3 us -> 33.1 us
    all_gather x8 -> x4, waiting for transfers between devices: 257 us -> 126 us  [the longest x1 48.8 us: aligned(): normed2_all = lax.all_gather(normed2_low, 'seq', axis=0, tiled=True)]
    pallas_call x1, Pallas kernels: 11.6 us -> 127 us  [mix_in(): pl.pallas_call(mix_in_kernel, out_shape=held + far, in_specs=[HELD] + [AN...]
    all_to_all x2 -> x0, blocking collectives: 93.2 us -> none  [gather_columns(): lax.all_to_all(stacked.transpose(1, 0, 2), 'seq', split_axis=0, concat_ax...]
    all_gather x2 -> x0, blocking collectives: 73.2 us -> none  [the longest x1 65.7 us: local(): lax.all_gather(jnp.stack([mix_gain, mlp_gain], axis=1), ('seq', 'fsdp'),...]
    reduce_scatter x6, waiting for transfers between devices: 159 us -> 199 us  [the longest x1 50.2 us: aligned(): lax.psum_scatter((times_transpose(x_low, in_whole[:, :channels]) + times_...]
    unnamed x102 -> x62, local copies, waits for them, and re-layouts: 15.7 us -> 4.51 us
    all_gather x2 -> x0, local copies, waits for them, and re-layouts: 11 us -> none  [gather_columns(): whole = lax.all_gather(mine, 'fsdp', axis=1)]
    dot_general x6 -> x4, matrix products: 36.5 us -> 26.7 us  [dot(): return jnp.dot(left, right, preferred_element_type=WIDE)]
  transfers between devices with their start and end apart: 18 -> 14, of which waited for: 16 -> 13; matrix products, arithmetic and copies ran while one was open for 11% -> 11% of each run, Pallas kernels for 1% -> 0%
where the time goes in v2:
time: 885 us; the launch traced here: 878 us
  waiting for transfers between devices  510 us (58%)
  Pallas kernels  141 us (16%)
  matrix products  94.8 us (11%)
  blocking collectives  39.8 us (4%)
  local copies, waits for them, and re-layouts  33.1 us (4%)
  other arithmetic  32.6 us (4%)
  between operations  16.4 us (2%)
  starting transfers between devices  9.43 us (1%)
    unnamed x14, waiting for transfers between devices  171 us
    pallas_call x1, Pallas kernels, mix_in(): pl.pallas_call(mix_in_kernel, out_shape=held + far, in_specs=[HELD] + [AN...  127 us
    reduce_scatter x1, waiting for transfers between devices, aligned(): lax.psum_scatter((times_transpose(x_low, in_whole[:, :channels]) + times_...  50.2 us
    reduce_scatter x1, waiting for transfers between devices, aligned(): lax.psum_scatter((times_transpose(gate_low, gate_whole) + times_transpose...  48.9 us
    all_gather x1, waiting for transfers between devices, aligned(): normed2_all = lax.all_gather(normed2_low, 'seq', axis=0, tiled=True)  48.8 us
    reduce_scatter x1, waiting for transfers between devices, aligned(): lax.psum_scatter(dot(product, out_whole).astype(LOW), 'seq', scatter_dime...  46 us
    dot_general x6, matrix products, times_transpose(): lax.dot_general(left, right, (((1,), (1,)), ((), ())), preferred_element_...  40 us
    unnamed x1, blocking collectives  39.8 us
  transfers between devices with their start and end apart: 14, of which 13 were waited for; matrix products, arithmetic and copies ran while one was open for 11% of the time, Pallas kernels for 0%

profile of v2, /device:TPU:0, one launch (start us, length us, event | category | flops | bytes accessed | tf_op | source)
XLA Modules:
  0.0 877.7 jit_solution(10336967196362067112)
XLA Ops:
  9.6 1.3 reshape.163
  10.9 1.3 reshape.164
  12.3 1.3 fusion.50.gain_shard
  13.5 1.5 pad_maximum_fusion.1.small
  15.0 1.0 maximum_bitcast_fusion.3.in_shard
  16.2 1.3 maximum_bitcast_fusion.2.glu_shard
  18.1 127.2 %mix_in.1 = (bf16[8,128,2048]{2,1,0:T(8,128)(2,1)}, bf16[8,4,64,640]{3,2,1,0:T(8,128)(2,1)}, bf16[1024,320]{1,0:T(8,128)(2,1)}, f32[1024,320]{1,0:T(8,128)}, bf1...) custom-call(bf16[128,2048]{1,0:T(8,128)(2,1)} %bitcast.148, ...), custom_call_target="tpu_custom_call" | custom-call | tf_op jit(solution)/shard_map/mix_in/pallas_call | solution.py:571
  145.4 5.9 convolution_convert_fusion
  152.0 0.9 fusion.57
  152.9 46.0 %reduce-scatter.16.cloned.1.call-done = bf16[128,2048]{1,0:T(8,128)(2,1)} async-done(((bf16[1024,2048]{1,0:T(8,128)(2,1)}), bf16[128,2048]{1,0:T(8,128)(2,1)}) %reduce-scatter.16.cloned.1.call-update) | async-done | bytes 524304 | tf_op jit(solution)/shard_map/reduce_scatter | solution.py:1002
  198.9 1.3 multiply_reduce_fusion
  200.2 2.0 multiply_convert_fusion.2
  203.3 17.7 %all-gather.11.cloned.1.call-done = bf16[8,256,1536]{2,1,0:T(8,128)(2,1)} async-done(((bf16[8,64,1536]{2,1,0:T(8,128)(2,1)}), bf16[8,256,1536]{2,1,0:T(8,128)(2,1)}) %all-gather.11.cloned.1.call-update) | async-done | bytes 6291472 | tf_op jit(solution)/shard_map/all_gather | solution.py:998
  221.0 48.8 %all-gather.7.cloned.1.call-done = bf16[1024,2048]{1,0:T(8,128)(2,1)} async-done(((bf16[128,2048]{1,0:T(8,128)(2,1)}), bf16[1024,2048]{1,0:T(8,128)(2,1)}) %all-gather.7.cloned.1.call-update) | async-done | bytes 4194320 | tf_op jit(solution)/shard_map/all_gather | solution.py:1007
  269.9 8.5 fusion.16
  278.4 5.1 fusion.20
  283.5 33.5 %all-gather.13.cloned.1.call-done = bf16[1,1024,2048]{2,1,0:T(8,128)(2,1)} async-done(((bf16[1,128,2048]{2,1,0:T(8,128)(2,1)}), bf16[1,1024,2048]{2,1,0:T(8,128)(2,1)}) %all-gather.13.cloned.1.call-update) | async-done | bytes 4194320 | tf_op jit(solution)/shard_map/all_gather | solution.py:999
  317.0 11.5 %fusion.14 = (bf16[1024,768]{1,0:T(8,128)(2,1)S(1)}, bf16[1024,768]{1,0:T(8,128)(2,1)S(1)}, bf16[1024,768]{1,0:T(8,128)(2,1)}) fusion(f32[1024,768]{1,0:T(8,128)} %fusion.20, f32[1024,768]{1,0:T(8,128)} %fusion.16, bf16[768,2048]{1,0:T(8,128)(2,1)} %bitcast.179, bf16[1,1024,2048]{2,1,0:T(8,128)(2,1)} %all-gather.13.cloned.1.call-done), kind=kOutput, calls=%fused_computation.23 | convolution fusion | flops 3241672704 | bytes 18350080 | tf_op jit(solution)/shard_map/dot_general | solution.py:31
  328.5 6.7 fusion.18
  335.2 6.9 add_convert_fusion.1
  342.2 48.9 %reduce-scatter.20.cloned.1.call-done = bf16[128,2048]{1,0:T(8,128)(2,1)} async-done(((bf16[1024,2048]{1,0:T(8,128)(2,1)}), bf16[128,2048]{1,0:T(8,128)(2,1)}) %reduce-scatter.20.cloned.1.call-update) | async-done | bytes 524304 | tf_op jit(solution)/shard_map/reduce_scatter | solution.py:1021
  391.1 1.7 fusion.36
  392.8 2.3 fusion.55
  395.2 6.4 copy.84
  401.6 6.4 convolution_convert_fusion.2
  408.0 3.8 convolution_convert_fusion.3
  411.8 3.2 maximum_bitcast_fusion
  415.0 25.5 %all-gather.9.cloned.1.call-done = bf16[1024,2048]{1,0:T(8,128)(2,1)} async-done(((bf16[128,2048]{1,0:T(8,128)(2,1)}), bf16[1024,2048]{1,0:T(8,128)(2,1)}) %all-gather.9.cloned.1.call-update) | async-done | bytes 4194320 | tf_op jit(solution)/shard_map/all_gather | solution.py:1028
  440.6 6.4 fusion.28
  447.1 14.0 %mixer_backward.1 = (bf16[1024,320]{1,0:T(8,128)(2,1)S(1)}, f32[320,160]{1,0:T(8,128)S(1)}, f32[320,160]{1,0:T(8,128)S(1)}, f32[8,320]{1,0:T(8,128)S(1)}) custom-call(bf16[1024,320]{1,0:T(8,128)(2,1)S(1)} %get-tuple-element.146.ds_ref, bf16[1024,320]{1,0:T(8,128)(2,1)S(1)} %copy-done.1, bf16[1024,320]{1,0:T(8,128)(2,1)S(1)} %copy-done.2, ...), custom_call_target="tpu_custom_call" | custom-call | tf_op jit(solution)/shard_map/mixer_backward/pallas_call | solution.py:761
  461.1 2.4 convolution_convert_fusion.6
  463.5 2.4 convolution_convert_fusion.5
  465.9 2.6 maximum_bitcast_fusion.1
  468.6 7.7 fusion.4
  477.3 0.9 mul.315
  478.2 2.0 pad_maximum_fusion
  480.3 5.3 convolution_convert_fusion.4
  485.9 3.9 fusion.30
  489.8 4.6 add_convert_fusion
  494.5 1.3 copy-done.25
  495.8 7.2 convolution_convert_fusion.1
  504.2 143.9 %all-reduce.8.cloned.1.call-done = (bf16[4,8,64,640]{3,2,0,1:T(8,128)(2,1)}, bf16[4,8,64,1536]{3,2,0,1:T(8,128)(2,1)}) async-done(((bf16[4,8,64,640]{3,2,0,1:T(8,128)(2,1)}, bf16[4,8,64,1536]{3,2,0,1:T(8,128)(2,1)}), (bf16[4,8,64,640]{3,2,0,1:T(8,128)(2,1)}, bf16[4,8,64,1536]{3,2,0,1:T(8,128)(2,1)})) %all-reduce.8.cloned.1.call-update) | async-done | bytes 8912912
  648.2 2.6 dynamic-slice_bitcast_fusion.1
  650.8 4.6 all-to-all-start
  655.4 3.3 dynamic-slice_bitcast_fusion
  658.7 14.9 %all-to-all-done = bf16[8,64,640]{2,1,0:T(8,128)(2,1)S(1)} async-done(((bf16[8,64,640]{2,1,0:T(8,128)(2,1)}), bf16[8,64,640]{2,1,0:T(8,128)(2,1)S(1)}, u32[]{:S(2)}, u32[]{:S(2)}) %all-to-all-start) | async-done | bytes 655392 | tf_op jit(solution)/shard_map/all_to_all | solution.py:792
  674.4 3.6 all-to-all-start.1
  678.0 17.6 %reduce-scatter.26.cloned.1.call-done = bf16[192,2048]{1,0:T(8,128)(2,1)} async-done(((bf16[768,2048]{1,0:T(8,128)(2,1)}), bf16[192,2048]{1,0:T(8,128)(2,1)}) %reduce-scatter.26.cloned.1.call-update) | async-done | bytes 786448 | tf_op jit(solution)/shard_map/reduce_scatter | solution.py:1048
  695.6 2.5 convert_element_type.120
  698.2 25.8 %reduce-scatter.28.cloned.1.call-done = f32[1,80,328]{2,1,0:T(8,128)} async-done(((f32[4,80,328]{2,1,0:T(8,128)}), f32[1,80,328]{2,1,0:T(8,128)}) %reduce-scatter.28.cloned.1.call-update) | async-done | bytes 104976
  724.0 0.9 slice.98
  725.5 1.7 slice_reduce_fusion
  727.7 1.7 fusion.56
  729.4 27.2 %reduce-scatter.24.cloned.1.call-done = bf16[80,2048]{1,0:T(8,128)(2,1)} async-done(((bf16[320,2048]{1,0:T(8,128)(2,1)}), bf16[80,2048]{1,0:T(8,128)(2,1)}) %reduce-scatter.24.cloned.1.call-update) | async-done | bytes 327696 | tf_op jit(solution)/shard_map/reduce_scatter | solution.py:1055
  756.6 1.9 convert_element_type.117
  758.5 50.2 %reduce-scatter.22.cloned.1.call-done = bf16[128,2048]{1,0:T(8,128)(2,1)} async-done(((bf16[1024,2048]{1,0:T(8,128)(2,1)}), bf16[128,2048]{1,0:T(8,128)(2,1)}) %reduce-scatter.22.cloned.1.call-update) | async-done | bytes 524304 | tf_op jit(solution)/shard_map/reduce_scatter | solution.py:1037
  808.7 1.6 fusion.37
  810.4 39.8 %all-reduce.1 = f32[32,2,64]{2,1,0:T(2,128)S(1)} all-reduce(f32[32,2,64]{2,1,0:T(2,128)S(1)} %maximum_bitcast_fusion.4), channel_id=8, replica_groups=mesh['seq'=8,'fsdp'=4] {'seq','fsdp'}, use_global_device_ids=true, to_apply=%region_10.11.clone | all-reduce | flops 4096 | bytes 32768
  850.7 9.2 %reduce-scatter.18.cloned.1.call-done = bf16[128,2048]{1,0:T(8,128)(2,1)} async-done(((bf16[1024,2048]{1,0:T(8,128)(2,1)}), bf16[128,2048]{1,0:T(8,128)(2,1)}) %reduce-scatter.18.cloned.1.call-update) | async-done | bytes 524304 | tf_op jit(solution)/shard_map/reduce_scatter | solution.py:1012
  859.9 3.3 fusion.46
  864.0 1.0 reshape.176
  865.5 1.0 reshape.175
  867.4 1.3 copy.108
  868.7 1.3 copy.107
  (110 shorter events, 11.7 us)
Async XLA Ops:
  8.0 8.1 copy-start.15
  8.0 8.1 copy-start.16
  8.0 190.8 %reduce-scatter.16.cloned.1.call-start = ((), (), s32[]{:S(2)}) async-start(), calls=%async_computation.9 | async-start | bytes 4718592 | tf_op jit(solution)/shard_map/reduce_scatter | solution.py:1002
  16.1 1.4 copy-start.17
  16.1 1.4 copy-start.18
  16.1 1.4 copy-start.19
  151.3 47.6 %copy-start.6 = (bf16[1,128,2048]{2,1,0:T(8,128)(2,1)S(1)}, bf16[1,128,2048]{2,1,0:T(8,128)(2,1)}, u32[]{:S(2)}) copy-start(bf16[1,128,2048]{2,1,0:T(8,128)(2,1)} %param.17) | copy-start | bytes 1572868
  151.3 69.7 %all-gather.11.cloned.1.call-start = ((), (), s32[]{:S(2)}) async-start(), calls=%async_computation.17 | async-start | bytes 7864320 | tf_op jit(solution)/shard_map/all_gather | solution.py:998
  151.9 118.0 %all-gather.7.cloned.1.call-start = ((), (), s32[]{:S(2)}) async-start(), calls=%async_computation.10 | async-start | bytes 4718592 | tf_op jit(solution)/shard_map/all_gather | solution.py:1007
  202.2 114.7 %all-gather.13.cloned.1.call-start = ((), (), s32[]{:S(2)}) async-start(), calls=%async_computation.18 | async-start | bytes 4718592 | tf_op jit(solution)/shard_map/all_gather | solution.py:999
  202.8 188.3 %reduce-scatter.20.cloned.1.call-start = ((), (), s32[]{:S(2)}) async-start(), calls=%async_computation.12 | async-start | bytes 4718592 | tf_op jit(solution)/shard_map/reduce_scatter | solution.py:1021
  269.9 8.5 copy-start.20
  269.9 8.5 copy-start.21
  328.5 6.7 copy-start.26
  328.5 6.7 copy-start.28
  342.1 49.0 %copy-start.7 = (bf16[128,2048]{1,0:T(8,128)(2,1)S(1)}, bf16[128,2048]{1,0:T(8,128)(2,1)}, u32[]{:S(2)}) copy-start(bf16[128,2048]{1,0:T(8,128)(2,1)} %reduce-scatter.16.cloned.1.call-done) | copy-start | bytes 1572868
  342.1 50.7 %copy-start.9 = (bf16[1,128,2048]{2,1,0:T(8,128)(2,1)S(1)}, bf16[1,128,2048]{2,1,0:T(8,128)(2,1)}, u32[]{:S(2)}) copy-start(bf16[1,128,2048]{2,1,0:T(8,128)(2,1)} %param.18) | copy-start | bytes 1572868
  342.1 98.4 %all-gather.9.cloned.1.call-start = ((), (), s32[]{:S(2)}) async-start(), calls=%async_computation.13 | async-start | bytes 4718592 | tf_op jit(solution)/shard_map/all_gather | solution.py:1028
  395.1 253.1 %all-reduce.8.cloned.1.call-start = ((), (), s32[]{:S(2)}) async-start(), calls=%async_computation.20 | async-start | bytes 17825792
  401.6 6.4 copy-start.22
  401.6 6.4 copy-start.27
  411.8 28.8 %copy-start.14 = (f32[1032,320]{1,0:T(8,128)S(1)}, f32[1032,320]{1,0:T(8,128)}, u32[]{:S(2)}) copy-start(f32[1032,320]{1,0:T(8,128)} %get-tuple-element.51.st_ref) | copy-start | bytes 3962884
  440.6 6.5 copy-start
  440.6 6.5 copy-start.1
  440.6 6.5 copy-start.2
  440.6 6.5 copy-start.3
  440.6 6.5 copy-start.4
  440.6 6.5 copy-start.5
  447.1 14.0 %copy-start.10 = (bf16[2048,1024]{1,0:T(8,128)(2,1)S(1)}, bf16[2048,1024]{1,0:T(8,128)(2,1)}, u32[]{:S(2)}) copy-start(bf16[2048,1024]{1,0:T(8,128)(2,1)} %copy.84) | copy-start | bytes 12582916
  468.6 227.0 %reduce-scatter.26.cloned.1.call-start = ((), (), s32[]{:S(2)}) async-start(), calls=%async_computation.16 | async-start | bytes 3932160 | tf_op jit(solution)/shard_map/reduce_scatter | solution.py:1048
  476.4 247.6 %reduce-scatter.28.cloned.1.call-start = ((), (), s32[]{:S(2)}) async-start(), calls=%async_computation.19 | async-start | bytes 614400
  480.2 276.4 %reduce-scatter.24.cloned.1.call-start = ((), (), s32[]{:S(2)}) async-start(), calls=%async_computation.15 | async-start | bytes 1638400 | tf_op jit(solution)/shard_map/reduce_scatter | solution.py:1055
  485.6 323.1 %reduce-scatter.22.cloned.1.call-start = ((), (), s32[]{:S(2)}) async-start(), calls=%async_computation.14 | async-start | bytes 4718592 | tf_op jit(solution)/shard_map/reduce_scatter | solution.py:1037
  485.9 3.9 copy-start.11
  494.4 1.4 copy-start.25
  494.4 365.5 %reduce-scatter.18.cloned.1.call-start = ((), (), s32[]{:S(2)}) async-start(), calls=%async_computation.11 | async-start | bytes 4718592 | tf_op jit(solution)/shard_map/reduce_scatter | solution.py:1012
  503.0 0.7 copy-start.24
  650.8 22.8 %all-to-all-start = ((bf16[8,64,640]{2,1,0:T(8,128)(2,1)}), bf16[8,64,640]{2,1,0:T(8,128)(2,1)S(1)}, u32[]{:S(2)}, u32[]{:S(2)}) async-start(bf16[8,64,640]{2,1,0:T(8,128)(2,1)} %dynamic-slice_bitcast_fusion.1), calls=%async_computation.4 | async-start | bytes 1310720 | tf_op jit(solution)/shard_map/all_to_all | solution.py:792
  658.7 68.5 %copy-start.23 = (bf16[80]{0:T(256)(128)(2,1)S(1)}, bf16[80]{0:T(256)(128)(2,1)}, u32[]{:S(2)}) copy-start(bf16[80]{0:T(256)(128)(2,1)} %param.29) | copy-start | bytes 484
  673.6 0.8 copy-start.12
  674.4 192.2 %all-to-all-start.1 = ((bf16[8,64,1536]{2,1,0:T(8,128)(2,1)}), bf16[8,64,1536]{2,1,0:T(8,128)(2,1)S(1)}, u32[]{:S(2)}, u32[]{:S(2)}) async-start(bf16[8,64,1536]{2,1,0:T(8,128)(2,1)} %dynamic-slice_bitcast_fusion), calls=%async_computation.6 | async-start | bytes 3145728 | tf_op jit(solution)/shard_map/all_to_all | solution.py:792
  678.0 181.9 %copy-start.8 = (bf16[128,2048]{1,0:T(8,128)(2,1)S(1)}, bf16[128,2048]{1,0:T(8,128)(2,1)}, u32[]{:S(2)}) copy-start(bf16[128,2048]{1,0:T(8,128)(2,1)} %reduce-scatter.20.cloned.1.call-done) | copy-start | bytes 1572868
  859.9 3.3 copy-start.13
Sparse Core Ops, SparseCore 0:
  151.5 47.3 reduce-scatter.15
  342.2 48.8 reduce-scatter.19
  395.2 45.2 all-gather.8
Sparse Core Ops, SparseCore 1:
  153.7 67.3 all-gather.10
  223.1 46.7 all-gather.6
  271.4 45.6 all-gather.12
  468.7 179.4 all-reduce.7
  651.5 44.1 reduce-scatter.25
  699.3 24.6 reduce-scatter.27
  727.3 29.3 reduce-scatter.23
  758.8 49.8 reduce-scatter.21
  810.8 49.0 reduce-scatter.17

commit v3 on v2

--- a/solution.py
+++ b/solution.py
@@ -288,7 +288,7 @@
         @pl.loop(0, self.rows // 16)
         def _(block):
             rows = pl.ds(pl.multiple_of(piece * self.rows + block * 16, 16), 16)
-            total = self.own[chip, rows, :] + self.heard[chip, rows, :].astype(WIDE)
+            total = self.own[chip, rows, :].astype(WIDE) + self.heard[chip, rows, :].astype(WIDE)
             for known, index in extras:
                 total = total + jnp.where(known, self.into[index, rows, :].astype(WIDE), 0.0)
             store(rows, total)
@@ -368,15 +368,15 @@
 
 def mix_in_kernel(
     tokens, in_shard, glu_shard, out_shard, down_shard, small, vecs, gain_shard,
-    normed, in_whole, x_ref, pre_ref, conv_ref, r_ref, i_ref, f_ref, m_ref, st_ref,
+    normed, in_whole, ext, pre_ref, conv_ref, r_ref, i_ref, st_ref,
     product_ref, par_ref, wr_ref, wi_ref, gains, glu_mine, out_whole, down_whole,
-    held, small_all, vecs_all, gain_all, ext, factors, drive, prod,
+    held, small_all, vecs_all, gain_all, factors, drive, prod,
     local_sems, tok_send, tok_recv, in_sems, in_xy_send, in_xy_recv, glu_sems, xy_sems, gain_sems,
 ):
     groups, shards = in_whole.shape[1], in_whole.shape[0]
     at = Place(shards, groups)
     s, f = at.s, at.f
-    positions, channels = x_ref.shape
+    positions, channels = pre_ref.shape
     width = tokens.shape[1]
     rows = in_shard.shape[1]
     segment = positions // 8
@@ -485,9 +485,7 @@
         both = dot(pair, in_whole[...].reshape(width, 2 * channels))
         base = pl.multiple_of(chip * 2 * tokens.shape[0], CHUNK)
         here = pl.ds(base, 2 * tokens.shape[0])
-        x_low = both[:, :channels].astype(LOW)
-        x_ref[here, :] = x_low
-        ext[pl.ds(base + 8, 2 * tokens.shape[0]), :] = x_low.astype(WIDE)
+        ext[pl.ds(base + 8, 2 * tokens.shape[0]), :] = both[:, :channels].astype(LOW).astype(WIDE)
         pre_ref[here, :] = both[:, channels:]
 
     @pl.loop(0, chunks)
@@ -507,8 +505,6 @@
         factor = jnp.exp(log_decay)
         r_ref[here, :] = r
         i_ref[here, :] = gate
-        f_ref[here, :] = factor
-        m_ref[here, :] = m
         put(factors, here, factor)
         put(drive, here, m * gate * conv_low.astype(WIDE))
 
@@ -554,12 +550,12 @@
     pieces = 2
     wide = jax.ShapeDtypeStruct((positions, channels), WIDE)
     low = jax.ShapeDtypeStruct((positions, channels), LOW)
+    longer = jax.ShapeDtypeStruct((positions + 8, channels), WIDE)
     square = jax.ShapeDtypeStruct((channels, channels), LOW)
     held = [
         jax.ShapeDtypeStruct((shards, block, width), LOW),
         jax.ShapeDtypeStruct((shards, groups, rows, both), LOW),
-        low, wide, low, wide, wide, wide, wide,
-        jax.ShapeDtypeStruct((positions + 8, channels), WIDE),
+        longer, wide, low, wide, wide, longer,
         low, jax.ShapeDtypeStruct((8, channels), WIDE), square, square,
         jax.ShapeDtypeStruct((8, width), WIDE),
     ]
@@ -578,7 +574,6 @@
             pltpu.VMEM((groups,) + small.shape, LOW),
             pltpu.VMEM((groups,) + vecs.shape, WIDE),
             pltpu.VMEM((shards, groups) + gain_shard.shape, WIDE),
-            pltpu.VMEM((positions + 8, channels), WIDE),
         ]
         + [pltpu.VMEM((lane_tiles(channels), positions, 128), WIDE)] * 3
         + [
@@ -590,6 +585,641 @@
         ),
         name="mix_in",
     )(tokens, in_shard, glu_shard, out_shard, down_shard, small, vecs, gain_shard)
+
+
+def feed_kernel(
+    product, out_whole, glu_mine, down_in, cotangent, tokens, gains,
+    middle, middle_grad, mixed_low, gain_sums, fed_own, fed_other, glu_grad, down_grad,
+    held, cots, glu, down, both, hidden, wide_pair, hidden_pair, tile, normed2, staged, down_staged,
+    own, other, heard, out, into, sib_send, sib_recv, line_send, line_recv,
+    local_sems, glu_send, glu_recv, two_send, two_recv, cot_send, cot_recv, stage_sems,
+):
+    shards, groups = glu.shape[0], glu.shape[1]
+    at = Place(shards, groups)
+    s, f = at.s, at.f
+    block, width = tokens.shape
+    units = down.shape[0]
+    pair = 2 * block
+
+    keep = [(glu_mine, glu.at[:, f]), (down_in, down), (cotangent, cots.at[s])]
+    keep = [pltpu.make_async_copy(a, b, local_sems.at[n]) for n, (a, b) in enumerate(keep)]
+    for copy in keep:
+        copy.start()
+    at.enter()
+    def glu_xy(index):
+        return Spread(
+            at, lambda peer: glu_mine.at[index], lambda origin: glu.at[index, origin],
+            glu_send.at[index], glu_recv.at[index],
+        )
+
+    cot_z = LineGather(at, cotangent, cots, cot_send, cot_recv, cot_send.shape[1])
+    two_z = LineGather(at, normed2, held, two_send, two_recv, two_send.shape[1])
+    sums = LineScatter(
+        at, own, other, heard, out, into, (sib_send, sib_recv, line_send, line_recv), line_send.shape[1]
+    )
+    for index in range(shards):
+        glu_xy(index).start()
+    cot_z.start()
+
+    def split(chip, columns, value, mine, theirs):
+        tile[...] = value.reshape(2, block, value.shape[1])
+        mine[chip, :, columns] = tile[at.c].astype(mine.dtype)
+        theirs[chip, :, columns] = tile[1 - at.c].astype(theirs.dtype)
+
+    def columns_of(j):
+        return pl.ds(pl.multiple_of(j * 256, 256), 256)
+
+    def pair_rows(chip):
+        return pl.ds(pl.multiple_of(chip * pair, pair), pair)
+
+    def project(chip):
+        @pl.loop(0, width // 256)
+        def _(j):
+            value = dot(product[pair_rows(chip), :], out_whole[:, columns_of(j)])
+            split(chip, columns_of(j), value, own, other)
+
+        sums.across(chip).start()
+
+    for k in range(at.line // 2):
+        project(at.line - 1 - k)
+        project(k)
+        sums.step(k)
+    sums.steps(at.line // 2)
+
+    def to_middle(here, total):
+        values = total + tokens[here, :].astype(WIDE)
+        middle[here, :] = values
+        scale = lax.rsqrt(jnp.mean(values * values, axis=-1, keepdims=True) + EPSILON)
+        normed2[here, :] = (values * scale * gains[1:2, :]).astype(LOW)
+
+    sums.finish(to_middle)
+    two_z.start()
+    own_copy = pltpu.make_async_copy(normed2, held.at[s], local_sems.at[3])
+    own_copy.start()
+    keep[0].wait()
+    keep[1].wait()
+    keep[2].wait()
+    sums.sent()
+    own_copy.wait()
+    for index in range(shards):
+        glu_xy(index).finish()
+
+    def feed(chip):
+        here = pair_rows(chip)
+        rows = held[pl.ds(2 * chip, 2), :, :].reshape(pair, width)
+        grads = cots[pl.ds(2 * chip, 2), :, :].reshape(pair, width)
+
+        @pl.loop(0, 2 * units // 256)
+        def _(j):
+            wide_pair[:, columns_of(j)] = dot(
+                rows, glu[:, :, :, columns_of(j)].reshape(width, 256)
+            )
+
+        @pl.loop(0, units // 256)
+        def _(j):
+            hidden_pair[:, columns_of(j)] = times_transpose(grads, down[columns_of(j), :])
+
+        @pl.loop(0, pair // 16)
+        def _(n):
+            part = pl.ds(pl.multiple_of(n * 16, 16), 16)
+            there = pl.ds(pl.multiple_of(chip * pair + n * 16, 16), 16)
+            opened, slope = gelu_and_slope(wide_pair[part, :units])
+            up = wide_pair[part, units:]
+            grad = hidden_pair[part, :]
+            hidden[there, :] = (opened * up).astype(LOW)
+            both[there, :units] = (grad * up * slope).astype(LOW)
+            both[there, units:] = (grad * opened).astype(LOW)
+
+        @pl.loop(0, shards)
+        def _(j):
+            value = times_transpose(both[here, :], glu[j].reshape(width // shards, 2 * units))
+            split(chip, columns_of(j), value, own, other)
+
+        sums.across(chip).start()
+
+        @pl.loop(0, width // 256)
+        def _(j):
+            split(chip, columns_of(j), dot(hidden[here, :], down[:, columns_of(j)]), fed_own, fed_other)
+
+    two_z.settle(at.z)
+    cot_z.settle(at.z)
+    feed(at.z)
+
+    @pl.loop(1, at.line)
+    def _(d):
+        for gather in (two_z, cot_z):
+            @pl.when(at.z - d >= 0)
+            def _():
+                gather.arrive(at.z - d)
+
+            @pl.when(at.z + d < at.line)
+            def _():
+                gather.arrive(at.z + d)
+
+        @pl.loop(0, 2)
+        def _(side):
+            chip = at.z - d + 2 * d * side
+
+            @pl.when((chip >= 0) & (chip < at.line))
+            def _():
+                two_z.settle(chip)
+                cot_z.settle(chip)
+                feed(chip)
+
+    def glu_out(j):
+        return pltpu.make_async_copy(
+            staged.at[lax.rem(j, 2)], glu_grad.at[:, j], stage_sems.at[lax.rem(j, 2)]
+        )
+
+    def glu_sums(first, last):
+        @pl.loop(first, last)
+        def _(j):
+            @pl.when(j >= 2)
+            def _():
+                glu_out(j - 2).wait()
+
+            rows = held[:, :, columns_of(j)].reshape(shards * block, 256)
+            staged[lax.rem(j, 2)] = outer_sum(rows, both[...]).astype(LOW).reshape(staged.shape[1:])
+            glu_out(j).start()
+
+    def down_out(j):
+        return pltpu.make_async_copy(
+            down_staged.at[lax.rem(j, 2)], down_grad.at[columns_of(j)], stage_sems.at[2 + lax.rem(j, 2)]
+        )
+
+    def down_sums():
+        @pl.loop(0, units // 256)
+        def _(j):
+            @pl.when(j >= 2)
+            def _():
+                down_out(j - 2).wait()
+
+            grads = cots[...].reshape(shards * block, width)
+            down_staged[lax.rem(j, 2)] = outer_sum(hidden[:, columns_of(j)], grads).astype(LOW)
+            down_out(j).start()
+
+    sums.step(0)
+    down_sums()
+    for k in range(1, at.line - 1):
+        sums.step(k)
+        glu_sums((k - 1) * shards // (at.line - 1), k * shards // (at.line - 1))
+    glu_sums((at.line - 2) * shards // (at.line - 1), shards)
+    gain_sums[...] = jnp.zeros_like(gain_sums)
+
+    def back(here, grad):
+        values = middle[here, :]
+        scale = lax.rsqrt(jnp.mean(values * values, axis=-1, keepdims=True) + EPSILON)
+        scaled = grad * gains[1:2, :]
+        along = jnp.mean(scaled * values, axis=-1, keepdims=True)
+        total = cotangent[here, :].astype(WIDE) + scale * scaled - values * (scale * scale * scale * along)
+        middle_grad[here, :] = total
+        mixed_low[here, :] = total.astype(LOW)
+        gain_sums[0:1, :] += jnp.sum(grad * values * scale, axis=0, keepdims=True)
+
+    sums.finish(back)
+    for j in range(shards - 2, shards):
+        glu_out(j).wait()
+    for j in range(max(units // 256 - 2, 0), units // 256):
+        down_out(j).wait()
+    sums.sent()
+    two_z.sent()
+    cot_z.sent()
+
+
+def feed(product, out_whole, glu_mine, down_whole, cotangent, tokens, gains, groups):
+    shards, rows, both = glu_mine.shape
+    block, width = tokens.shape
+    units = both // 2
+    line, pieces, thirds = shards // 2, 2, 4
+    own = jax.ShapeDtypeStruct((block, width), WIDE)
+    low = jax.ShapeDtypeStruct((line, block, width), LOW)
+    outs = [
+        own, own, jax.ShapeDtypeStruct((block, width), LOW), jax.ShapeDtypeStruct((8, width), WIDE),
+        low, low,
+        jax.ShapeDtypeStruct((groups, shards, rows, both), LOW),
+        jax.ShapeDtypeStruct((units, width), LOW),
+    ]
+    gathered = pltpu.VMEM((shards, block, width), LOW)
+    return pl.pallas_call(
+        feed_kernel,
+        out_shape=outs,
+        in_specs=[HELD, HELD, ANY, ANY, HELD, HELD, HELD],
+        out_specs=[HELD] * 6 + [ANY] * 2,
+        scratch_shapes=[
+            gathered, gathered,
+            pltpu.VMEM((shards, groups, rows, both), LOW),
+            pltpu.VMEM((units, width), LOW),
+            pltpu.VMEM((shards * block, both), LOW),
+            pltpu.VMEM((shards * block, units), LOW),
+            pltpu.VMEM((2 * block, both), WIDE),
+            pltpu.VMEM((2 * block, units), WIDE),
+            pltpu.VMEM((2, block, 256), WIDE),
+            pltpu.VMEM((block, width), LOW),
+            pltpu.VMEM((2, groups, rows, both), LOW),
+            pltpu.VMEM((2, 256, width), LOW),
+        ]
+        + LineScatter.scratch(line, block, width, thirds)
+        + [
+            dma(4), dma(shards, groups), dma(shards, groups), dma(shards, pieces, 3), dma(shards, pieces),
+            dma(shards, pieces, 3), dma(shards, pieces), dma(4),
+        ],
+        compiler_params=pltpu.CompilerParams(
+            collective_id=2, has_side_effects=True, vmem_limit_bytes=VMEM_BYTES
+        ),
+        name="feed",
+    )(product, out_whole, glu_mine, down_whole, cotangent, tokens, gains)
+
+
+def back_kernel(
+    mixed, fed_own, fed_other, middle, middle_grad, tokens, gains, par_ref, wr_ref, wi_ref,
+    out_far, in_far, normed_far, product_far, ext_far, pre_far, conv_far, r_far, i_far, st_far,
+    glu_grad, down_grad,
+    result, tokens_grad, gain_sums, wr_grad, wi_grad, sums_ref, out_grad, in_grad, glu_heard, down_heard,
+    held, in_whole, out_whole, product, ext, pre, conv_ref, r_ref, i_ref, st_ref,
+    both, pair_grad, tile, staged, factors, adj, prod, cg, carries, wr_sum, wi_sum,
+    fed_heard, fed_out, fed_into, fed_sib_send, fed_sib_recv, fed_send, fed_recv,
+    own, other, heard, out, into, sib_send, sib_recv, line_send, line_recv,
+    local_sems, held_send, held_recv, glu_sems, down_sems, stage_sems,
+):
+    shards, groups = in_whole.shape[0], in_whole.shape[1]
+    at = Place(shards, groups)
+    s, f = at.s, at.f
+    block, width = tokens.shape
+    positions, channels = product.shape
+    pair = 2 * block
+    segment = positions // 8
+    chunks = positions // CHUNK
+
+    keep = [
+        (mixed, held.at[s]), (out_far, out_whole), (pre_far, pre), (st_far, st_ref),
+        (product_far, product), (r_far, r_ref), (i_far, i_ref), (conv_far, conv_ref),
+        (ext_far, ext), (in_far, in_whole), (glu_grad.at[f], glu_heard.at[f]),
+        (down_grad.at[f], down_heard.at[f]), (normed_far, held),
+    ]
+    keep = [pltpu.make_async_copy(a, b, local_sems.at[n]) for n, (a, b) in enumerate(keep)]
+    for copy in keep[:-1]:
+        copy.start()
+    at.enter()
+    glu_xy = Spread(
+        at, lambda peer: glu_grad.at[peer], lambda origin: glu_heard.at[origin],
+        glu_sems.at[0], glu_sems.at[1],
+    )
+    down_xy = Spread(
+        at, lambda peer: down_grad.at[peer], lambda origin: down_heard.at[origin],
+        down_sems.at[0], down_sems.at[1],
+    )
+    mixed_z = LineGather(at, mixed, held, held_send, held_recv, held_send.shape[1])
+    fed = LineScatter(
+        at, fed_own, fed_other, fed_heard, fed_out, fed_into,
+        (fed_sib_send, fed_sib_recv, fed_send, fed_recv), fed_send.shape[1],
+    )
+    sums = LineScatter(
+        at, own, other, heard, out, into, (sib_send, sib_recv, line_send, line_recv), line_send.shape[1]
+    )
+    mixed_z.start()
+    down_xy.start()
+    glu_xy.start()
+    for k in range(at.line // 2):
+        fed.across(at.line - 1 - k).start()
+        fed.across(k).start()
+
+    def columns_of(j):
+        return pl.ds(pl.multiple_of(j * 256, 256), 256)
+
+    for n in (1, 2, 3):
+        keep[n].wait()
+    keep[0].wait()
+
+    def mixed_back(chip):
+        rows = held[pl.ds(2 * chip, 2), :, :].reshape(pair, width)
+        pair_grad[...] = times_transpose(rows, out_whole[...])
+
+        @pl.loop(0, pair // 64)
+        def _(n):
+            grad = pair_grad[pl.ds(pl.multiple_of(n * 64, 64), 64), :]
+            base = pl.multiple_of(chip * pair + n * 64, 64)
+            here = pl.ds(base, 64)
+            opened, slope = gelu_and_slope(pre[here, :])
+            states = st_ref[pl.ds(base + 8, 64), :].astype(LOW).astype(WIDE)
+            put(adj, here, (grad * opened).astype(LOW).astype(WIDE))
+            both[here, channels:] = (grad * states * slope).astype(LOW)
+
+    mixed_z.distances(mixed_back)
+    fed.step(0)
+    keep[5].wait()
+
+    @pl.loop(0, chunks)
+    def _(n):
+        here = pl.ds(pl.multiple_of(n * CHUNK, CHUNK), CHUNK)
+        put(factors, here, jnp.exp(r_ref[here, :] * par_ref[7:8, :]))
+
+    def step(j, n, flow, product):
+        here = pl.ds(segment - 1 - j, 8, stride=segment)
+        factor = factors[n, here, :]
+        adjoint = adj[n, here, :] + flow
+        adj[n, here, :] = adjoint
+        prod[n, here, :] = product
+        return factor * adjoint, factor * product
+
+    flow, through = scan_segments(step, segment, lane_tiles(channels))
+    flow, through = flow[:, :channels], through[:, :channels]
+    carry = jnp.zeros((1, channels), WIDE)
+    for k in range(7, -1, -1):
+        carries[k : k + 1, :] = carry
+        carry = flow[k : k + 1] + through[k : k + 1] * carry
+    fed.step(1)
+    for n in (6, 7, 8):
+        keep[n].wait()
+    cg[pl.ds(positions, 8), :] = jnp.zeros((8, channels), WIDE)
+    wr_sum[...] = jnp.zeros_like(wr_sum)
+    wi_sum[...] = jnp.zeros_like(wi_sum)
+
+    def grads(c, sums):
+        base = pl.multiple_of(c * CHUNK, CHUNK)
+        rows = pl.ds(base, CHUNK)
+        adjoint = get(adj, rows, channels) + get(prod, rows, channels) * carries[pl.ds(base // segment, 1), :]
+        before = st_ref[pl.ds(base, CHUNK + 8), :][7 : 7 + CHUNK]
+        conv_low = conv_ref[rows, :]
+        conv = conv_low.astype(WIDE)
+        r = r_ref[rows, :]
+        gate = i_ref[rows, :]
+        factor = get(factors, rows, channels)
+        m = jnp.sqrt(one_minus_exp(-2.0 * (r * par_ref[7:8, :])))
+        driven = adjoint * gate
+        by_log = adjoint * before * factor - driven * conv * factor * factor / m
+        by_r = by_log * par_ref[7:8, :] * r * (1.0 - r)
+        by_i = adjoint * m * conv * gate * (1.0 - gate)
+        by_r_low = by_r.astype(LOW)
+        by_i_low = by_i.astype(LOW)
+        conv_grad = (
+            driven * m
+            + times_transpose(by_r_low, wr_ref[...])
+            + times_transpose(by_i_low, wi_ref[...])
+        )
+        cg[rows, :] = conv_grad
+        wr_sum[...] += outer_sum(conv_low, by_r_low)
+        wi_sum[...] += outer_sum(conv_low, by_i_low)
+        near = ext[pl.ds(base, CHUNK + 8), :]
+        rows_of = [conv_grad * near[8 - k : 8 - k + CHUNK] for k in range(4)]
+        rows_of += [conv_grad, by_r, by_i, by_log * r]
+        return tuple(
+            total + jnp.sum(member, axis=0, keepdims=True) for total, member in zip(sums, rows_of)
+        )
+
+    zero = jnp.zeros((1, channels), WIDE)
+    totals = lax.fori_loop(0, chunks, grads, (zero,) * 8)
+    for k in range(8):
+        sums_ref[k : k + 1, :] = totals[k]
+    size = wr_grad.shape[1]
+    for n in range(channels // size):
+        part = slice(n * size, (n + 1) * size)
+        wr_grad[part, :] = wr_sum[part, part]
+        wi_grad[part, :] = wi_sum[part, part]
+
+    @pl.loop(0, chunks)
+    def _(c):
+        base = pl.multiple_of(c * CHUNK, CHUNK)
+        near = cg[pl.ds(base, CHUNK + 8), :]
+        total = jnp.zeros((CHUNK, channels), WIDE)
+        for k in range(4):
+            total = total + par_ref[k : k + 1, :] * near[k : k + CHUNK]
+        both[pl.ds(base, CHUNK), :channels] = total.astype(LOW)
+
+    fed.steps(2)
+    keep[9].wait()
+
+    def project(chip):
+        rows = both[pl.ds(pl.multiple_of(chip * pair, pair), pair), :]
+
+        @pl.loop(0, shards)
+        def _(j):
+            value = times_transpose(rows, in_whole[j].reshape(width // shards, 2 * channels))
+            tile[...] = value.reshape(2, block, value.shape[1])
+            own[chip, :, columns_of(j)] = tile[at.c]
+            other[chip, :, columns_of(j)] = tile[1 - at.c].astype(LOW)
+
+        sums.across(chip).start()
+
+    for k in range(at.line // 2):
+        project(at.line - 1 - k)
+        project(k)
+        sums.step(k)
+    keep[4].wait()
+
+    @pl.loop(0, width // 256)
+    def _(j):
+        columns = columns_of(j)
+        grads = held[:, :, columns].reshape(positions, 256)
+        out_grad[:, columns] = outer_sum(product[...], grads).astype(LOW)
+
+    mixed_z.sent()
+    keep[12].start()
+
+    def store_result(here, total):
+        result[here, :] = (middle[here, :] + total).astype(LOW)
+
+    fed.finish(store_result)
+    sums.steps(at.line // 2)
+    keep[12].wait()
+
+    def in_out(j):
+        return pltpu.make_async_copy(
+            staged.at[lax.rem(j, 2)], in_grad.at[:, j], stage_sems.at[lax.rem(j, 2)]
+        )
+
+    @pl.loop(0, shards)
+    def _(j):
+        @pl.when(j >= 2)
+        def _():
+            in_out(j - 2).wait()
+
+        rows = held[:, :, columns_of(j)].reshape(positions, 256)
+        staged[lax.rem(j, 2)] = outer_sum(rows, both[...]).astype(LOW).reshape(staged.shape[1:])
+        in_out(j).start()
+
+    gain_sums[...] = jnp.zeros_like(gain_sums)
+
+    def back(here, grad):
+        values = tokens[here, :].astype(WIDE)
+        scale = lax.rsqrt(jnp.mean(values * values, axis=-1, keepdims=True) + EPSILON)
+        scaled = grad * gains[0:1, :]
+        along = jnp.mean(scaled * values, axis=-1, keepdims=True)
+        total = middle_grad[here, :] + scale * scaled - values * (scale * scale * scale * along)
+        tokens_grad[here, :] = total.astype(LOW)
+        gain_sums[0:1, :] += jnp.sum(grad * values * scale, axis=0, keepdims=True)
+
+    sums.finish(back)
+    for j in range(shards - 2, shards):
+        in_out(j).wait()
+    fed.sent()
+    sums.sent()
+    keep[10].wait()
+    keep[11].wait()
+    down_xy.finish()
+    glu_xy.finish()
+
+
+def back(
+    mixed, fed_own, fed_other, middle, middle_grad, tokens, gains, par, wr, wi,
+    out_whole, in_whole, normed, product, ext, pre, conv, r, i, st, glu_grad, down_grad, size,
+):
+    shards, groups, rows, both = in_whole.shape
+    block, width = tokens.shape
+    positions, channels = product.shape
+    line, pieces, thirds = shards // 2, 2, 4
+    low = pltpu.VMEM((line, block, width), LOW)
+    short = jax.ShapeDtypeStruct((block, width), LOW)
+    square = jax.ShapeDtypeStruct((channels, size), WIDE)
+    outs = [
+        short, short, jax.ShapeDtypeStruct((8, width), WIDE), square, square,
+        jax.ShapeDtypeStruct((8, channels), WIDE),
+        jax.ShapeDtypeStruct((channels, width), LOW),
+        jax.ShapeDtypeStruct((groups, shards, rows, both), LOW),
+        jax.ShapeDtypeStruct(glu_grad.shape, LOW),
+        jax.ShapeDtypeStruct(down_grad.shape, LOW),
+    ]
+    far = [out_whole, in_whole, normed, product, ext, pre, conv, r, i, st]
+    near = [in_whole, out_whole, product, ext, pre, conv, r, i, st]
+    return pl.pallas_call(
+        back_kernel,
+        out_shape=outs,
+        in_specs=[HELD, HELD, ANY] + [HELD] * 7 + [ANY] * (len(far) + 2),
+        out_specs=[HELD] * 7 + [ANY] * 3,
+        scratch_shapes=[pltpu.VMEM((shards, block, width), LOW)]
+        + [pltpu.VMEM(member.shape, member.dtype) for member in near]
+        + [
+            pltpu.VMEM((positions, 2 * channels), LOW),
+            pltpu.VMEM((2 * block, channels), WIDE),
+            pltpu.VMEM((2, block, 256), WIDE),
+            pltpu.VMEM((2, groups, rows, both), LOW),
+        ]
+        + [pltpu.VMEM((lane_tiles(channels), positions, 128), WIDE)] * 3
+        + [pltpu.VMEM((positions + 8, channels), WIDE), pltpu.VMEM((8, channels), WIDE)]
+        + [pltpu.VMEM((channels, channels), WIDE)] * 2
+        + LineScatter.scratch(line, block, width, thirds)[2:]
+        + LineScatter.scratch(line, block, width, thirds)
+        + [
+            dma(13), dma(shards, pieces, 3), dma(shards, pieces), dma(2, groups), dma(2, groups), dma(2),
+        ],
+        compiler_params=pltpu.CompilerParams(
+            collective_id=3, has_side_effects=True, vmem_limit_bytes=VMEM_BYTES
+        ),
+        name="back",
+    )(
+        mixed, fed_own, fed_other, middle, middle_grad, tokens, gains, par, wr, wi, *far,
+        glu_grad, down_grad,
+    )
+
+
+def tail_kernel(
+    glu_far, in_grad, out_grad, small, gain_parts,
+    glu_out, in_out, out_heard, small_heard, gain_out,
+    glu_heard, glu_sum, in_heard, in_sum, gain_heard, gain_sum,
+    local_sems, in_xy_sems, out_sems, small_sems, gain_xy_sems, glu_sems, in_sems, gain_sems,
+):
+    groups, shards = glu_far.shape[0], glu_far.shape[1]
+    at = Place(shards, groups)
+    s, f = at.s, at.f
+    keep = [
+        (glu_far, glu_heard), (in_grad.at[f], in_heard.at[f]), (out_grad.at[f], out_heard.at[f]),
+        (small.at[f], small_heard.at[f]), (gain_parts.at[f], gain_heard.at[f]),
+    ]
+    keep = [pltpu.make_async_copy(a, b, local_sems.at[n]) for n, (a, b) in enumerate(keep)]
+    for copy in keep:
+        copy.start()
+    at.enter()
+
+    def over_fsdp(src, dst, sems):
+        return Spread(
+            at, lambda peer: src.at[peer], lambda origin: dst.at[origin], sems.at[0], sems.at[1]
+        )
+
+    def over_seq(src, dst, sems):
+        return Spread(
+            at, lambda peer: src.at[peer], lambda origin: dst.at[origin], sems.at[0], sems.at[1], "seq"
+        )
+
+    gain_xy = over_fsdp(gain_parts, gain_heard, gain_xy_sems)
+    in_xy = over_fsdp(in_grad, in_heard, in_xy_sems)
+    small_xy = over_fsdp(small, small_heard, small_sems)
+    out_xy = over_fsdp(out_grad, out_heard, out_sems)
+    glu_z = over_seq(glu_sum, glu_out, glu_sems)
+    in_z = over_seq(in_sum, in_out, in_sems)
+    gain_z = over_seq(gain_sum, gain_out, gain_sems)
+    for spread in (gain_xy, in_xy, small_xy, out_xy):
+        spread.start()
+
+    def add(parts, total, peer):
+        @pl.loop(0, total.shape[1] // 16)
+        def _(n):
+            here = pl.ds(pl.multiple_of(n * 16, 16), 16)
+            value = parts[0, peer, here, :].astype(WIDE)
+            for origin in range(1, groups):
+                value = value + parts[origin, peer, here, :].astype(WIDE)
+            total[peer, here, :] = value.astype(total.dtype)
+
+    def swap(parts, total, spread, into, sem):
+        @pl.loop(1, shards)
+        def _(d):
+            peer = lax.rem(s + d, shards)
+            add(parts, total, peer)
+            spread.copy(d).start()
+
+        add(parts, total, s)
+        mine = pltpu.make_async_copy(total.at[s], into.at[s], sem)
+        mine.start()
+        return mine
+
+    keep[0].wait()
+    glu_own = swap(glu_heard, glu_sum, glu_z, glu_out, local_sems.at[5])
+    gain_xy.finish()
+    keep[4].wait()
+    total = gain_heard[0]
+    for origin in range(1, groups):
+        total = total + gain_heard[origin]
+    gain_sum[...] = total
+    gain_z.start()
+    gain_own = pltpu.make_async_copy(gain_sum.at[s], gain_out.at[s], local_sems.at[6])
+    gain_own.start()
+    in_xy.finish()
+    keep[1].wait()
+    in_own = swap(in_heard, in_sum, in_z, in_out, local_sems.at[7])
+    for spread in (gain_z, small_xy, out_xy, glu_z, in_z):
+        spread.finish()
+    for copy in (keep[2], keep[3], glu_own, gain_own, in_own):
+        copy.wait()
+
+
+def tail(glu_heard, in_grad, out_grad, small, gain_parts):
+    groups, shards, rows, both = glu_heard.shape
+    wide = in_grad.shape[3]
+    outs = [
+        jax.ShapeDtypeStruct((shards, rows, both), LOW),
+        jax.ShapeDtypeStruct((shards, rows, wide), LOW),
+        jax.ShapeDtypeStruct(out_grad.shape, LOW),
+        jax.ShapeDtypeStruct(small.shape, WIDE),
+        jax.ShapeDtypeStruct(gain_parts.shape[1:], WIDE),
+    ]
+    return pl.pallas_call(
+        tail_kernel,
+        out_shape=outs,
+        in_specs=[ANY] * 5,
+        out_specs=[ANY] * 5,
+        scratch_shapes=[
+            pltpu.VMEM(glu_heard.shape, LOW),
+            pltpu.VMEM((shards, rows, both), LOW),
+            pltpu.VMEM(in_grad.shape, LOW),
+            pltpu.VMEM((shards, rows, wide), LOW),
+            pltpu.VMEM(gain_parts.shape, WIDE),
+            pltpu.VMEM(gain_parts.shape[1:], WIDE),
+            dma(8), dma(2, groups), dma(2, groups), dma(2, groups), dma(2, groups),
+            dma(2, shards), dma(2, shards), dma(2, shards),
+        ],
+        compiler_params=pltpu.CompilerParams(
+            collective_id=4, has_side_effects=True, vmem_limit_bytes=VMEM_BYTES
+        ),
+        name="tail",
+    )(glu_heard, in_grad, out_grad, small, gain_parts)
 
 
 def mixer_forward_kernel(
@@ -982,117 +1612,65 @@
         axis=0,
     )
     gain_shard = jnp.pad(jnp.stack([mix_gain, mlp_gain]).astype(WIDE), ((0, 6), (0, 0)))
+    tokens_low = tokens.reshape(positions, width)
     (
-        normed_all, in_whole, branch_x, branch_pre, *saved, product, par, wr, wi, gains,
-        glu_mine, out_whole, down_whole,
+        normed, in_whole, ext, branch_pre, conv_low, recur_gate, input_gate, states, product, par, wr, wi,
+        gains, glu_mine, out_whole, down_whole,
     ) = mix_in(
-        tokens.reshape(positions, width), by_column(lru_in_weight, gelu_in_weight),
-        by_column(gate_weight, up_weight), out_weight, down_weight,
-        jnp.concatenate([recurrence_weight, input_gate_weight], axis=1), vecs, gain_shard, groups,
-    )
-    normed_all = normed_all.reshape(-1, width)
-    in_whole = in_whole.reshape(width, -1)
+        tokens_low, by_column(lru_in_weight, gelu_in_weight), by_column(gate_weight, up_weight),
+        out_weight, down_weight, jnp.concatenate([recurrence_weight, input_gate_weight], axis=1),
+        vecs, gain_shard, groups,
+    )
     out_whole = out_whole.reshape(-1, width)
-    down_whole = down_whole.reshape(-1, width)
-    mix_scale, mlp_scale = gains[0], gains[1]
-    glu_whole = lax.all_gather(glu_mine, "fsdp", axis=1).reshape(width, -1)
-    grad_all = lax.all_gather(grad_low, "seq", axis=0, tiled=True)
-    branch_y = jax.nn.gelu(branch_pre)
-    states_f = saved[5][8:].astype(LOW).astype(WIDE)
-    mixed = lax.psum_scatter(
-        dot(product, out_whole).astype(LOW), "seq", scatter_dimension=0, tiled=True
-    )
-    middle = resid_in + mixed.astype(WIDE)
-    normed2_low = rms_scale(middle, mlp_scale).astype(LOW)
-    normed2_all = lax.all_gather(normed2_low, "seq", axis=0, tiled=True)
-    gate_whole, up_whole = glu_whole[:, :hidden_width], glu_whole[:, hidden_width:]
-    gate_val = dot(normed2_all, gate_whole)
-    up_val = dot(normed2_all, up_whole)
-    hidden = (jax.nn.gelu(gate_val) * up_val).astype(LOW)
-    fed = lax.psum_scatter(
-        dot(hidden, down_whole).astype(LOW), "seq", scatter_dimension=0, tiled=True
-    )
-    result = middle + fed.astype(WIDE)
-
-    hidden_grad = times_transpose(grad_all, down_whole)
-    unused, pull_glu = jax.vjp(lambda first, second: jax.nn.gelu(first) * second, gate_val, up_val)
-    gate_grad, up_grad = pull_glu(hidden_grad)
-    gate_low, up_low = gate_grad.astype(LOW), up_grad.astype(LOW)
-    normed2_grad = lax.psum_scatter(
-        (times_transpose(gate_low, gate_whole) + times_transpose(up_low, up_whole)).astype(LOW),
-        "seq", scatter_dimension=0, tiled=True,
-    ).astype(WIDE)
-    unused, pull_norm2 = jax.vjp(rms_scale, middle, mlp_scale)
-    middle_part, mlp_gain_grad = pull_norm2(normed2_grad)
-    middle_grad = grad_low.astype(WIDE) + middle_part
-    mixed_all = lax.all_gather(middle_grad.astype(LOW), "seq", axis=0, tiled=True)
-
-    product_grad = times_transpose(mixed_all, out_whole)
-    states_grad = (product_grad * branch_y).astype(LOW)
-    unused, pull_gelu = jax.vjp(jax.nn.gelu, branch_pre)
-    (pre_grad,) = pull_gelu(product_grad * states_f)
-    pre_low = pre_grad.astype(LOW)
-    x_low, wr_grad, wi_grad, sums = mixer_backward(states_grad, branch_x, saved, wr, wi, par, size)
-
-    normed_grad = lax.psum_scatter(
-        (
-            times_transpose(x_low, in_whole[:, :channels])
-            + times_transpose(pre_low, in_whole[:, channels:])
-        ).astype(LOW),
-        "seq", scatter_dimension=0, tiled=True,
-    ).astype(WIDE)
-    unused, pull_norm = jax.vjp(rms_scale, resid_in, mix_scale)
-    input_part, mix_gain_grad = pull_norm(normed_grad)
-    input_grad = middle_grad + input_part
-
-    down_grad = lax.psum_scatter(
-        outer_sum(hidden, grad_all).astype(LOW), "fsdp", scatter_dimension=0, tiled=True
-    ).astype(WIDE)
-    glu_grad = jnp.concatenate(
-        [outer_sum(normed2_all, gate_low), outer_sum(normed2_all, up_low)], axis=1
-    )
-    gate_w_grad, up_w_grad = scatter_columns(glu_grad, [hidden_width] * 2, rows)
-    out_grad = lax.psum_scatter(
-        outer_sum(product, mixed_all).astype(LOW), "fsdp", scatter_dimension=0, tiled=True
-    ).astype(WIDE)
-    in_grad = jnp.concatenate(
-        [outer_sum(normed_all, x_low), outer_sum(normed_all, pre_low)], axis=1
-    )
-    lru_in_grad, gelu_in_grad = scatter_columns(in_grad, [channels] * 2, rows)
+    middle, middle_grad, mixed_low, mlp_sums, fed_own, fed_other, glu_grad, down_grad = feed(
+        product, out_whole, glu_mine, down_whole.reshape(-1, width), grad_low, tokens_low, gains, groups
+    )
+    (
+        result, tokens_grad, mix_sums, wr_grad, wi_grad, sums, out_grad, in_grad, glu_heard, down_heard,
+    ) = back(
+        mixed_low, fed_own, fed_other, middle, middle_grad, tokens_low, gains, par, wr, wi,
+        out_whole, in_whole, normed, product, ext, branch_pre, conv_low, recur_gate, input_gate, states,
+        glu_grad, down_grad.reshape(groups, -1, width), size,
+    )
+    small_rows = recurrence_weight.shape[0]
+    vector_parts = sums.reshape(8, groups, small_rows).transpose(1, 0, 2)
     small = jnp.concatenate(
         [
-            wr_grad, wi_grad, sums[:7].T,
-            (sums[7] * RATE_SCALE)[:, None],
+            jnp.concatenate([wr_grad, wi_grad], axis=1).reshape(groups, small_rows, 2 * size),
+            jnp.pad(vector_parts, ((0, 0), (0, 0), (0, 2 * size - small_rows))),
         ],
         axis=1,
     )
-    small = lax.psum_scatter(
-        small.reshape(lax.axis_size("fsdp"), -1, small.shape[1]),
-        "fsdp", scatter_dimension=0, tiled=False,
-    )
-    gain_parts = jnp.stack([mix_gain_grad, mlp_gain_grad]).reshape(2, -1, rows).transpose(1, 0, 2)
-    gain_grads = lax.psum_scatter(
-        gain_parts, ("seq", "fsdp"), scatter_dimension=0, tiled=False
-    )
-    first = 2 * size
+    gain_parts = jnp.stack([mix_sums[0], mlp_sums[0]]).reshape(2, shards, groups, rows)
+    gain_parts = jnp.pad(gain_parts.transpose(2, 1, 0, 3), ((0, 0), (0, 0), (0, 6), (0, 0)))
+    glu_out, in_out, out_heard, small_heard, gain_out = tail(
+        glu_heard, in_grad, out_grad.reshape(groups, -1, width), small, gain_parts
+    )
+
+    def rows_of(parts, first, size):
+        return parts[:, :, first : first + size].astype(WIDE).transpose(1, 0, 2).reshape(rows, -1)
+
+    small = jnp.sum(small_heard, axis=0)
+    vector_sums = small[small_rows:, :small_rows]
+    gain_grads = jnp.sum(gain_out, axis=0)
     return (
-        result.astype(LOW).reshape(tokens.shape),
-        input_grad.astype(LOW).reshape(tokens.shape),
+        result.reshape(tokens.shape),
+        tokens_grad.reshape(tokens.shape),
         gain_grads[0],
-        lru_in_grad,
-        gelu_in_grad,
-        out_grad,
-        small[:, first : first + 4],
-        small[:, first + 4],
-        small[:, :size],
-        small[:, first + 5],
-        small[:, size : 2 * size],
-        small[:, first + 6],
-        small[:, first + 7] * jax.nn.sigmoid(-own_decay),
+        rows_of(in_out, 0, channels),
+        rows_of(in_out, channels, channels),
+        jnp.sum(out_heard.astype(WIDE), axis=0),
+        vector_sums[:4].T,
+        vector_sums[4],
+        small[:small_rows, :size],
+        vector_sums[5],
+        small[:small_rows, size : 2 * size],
+        vector_sums[6],
+        vector_sums[7] * RATE_SCALE * jax.nn.sigmoid(-own_decay),
         gain_grads[1],
-        gate_w_grad,
-        up_w_grad,
-        down_grad,
+        rows_of(glu_out, 0, hidden_width),
+        rows_of(glu_out, hidden_width, hidden_width),
+        jnp.sum(down_heard.astype(WIDE), axis=0),
     )
 
 

time: 885 us -> 554 us (0.63)
  waiting for transfers between devices: 510 us -> 0 us
  Pallas kernels: 141 us -> 521 us
  matrix products: 94.8 us -> 0 us
  blocking collectives: 39.8 us -> 0 us
  local copies, waits for them, and re-layouts: 33.1 us -> 14.6 us
  other arithmetic: 32.6 us -> 17 us
  between operations: 16.4 us -> 0.81 us
  starting transfers between devices: 9.43 us -> 0 us
    pallas_call x1 -> x3, Pallas kernels: 14 us -> 395 us  [the longest x1 187 us: feed(): pl.pallas_call(feed_kernel, out_shape=outs, in_specs=[HELD, HELD, ANY, AN...]
    reduce_scatter x6 -> x0, waiting for transfers between devices: 199 us -> none  [the longest x1 50.2 us: aligned(): lax.psum_scatter((times_transpose(x_low, in_whole[:, :channels]) + times_...]
    unnamed x14 -> x0, waiting for transfers between devices: 171 us -> none
    all_gather x4 -> x0, waiting for transfers between devices: 126 us -> none  [the longest x1 48.8 us: aligned(): normed2_all = lax.all_gather(normed2_low, 'seq', axis=0, tiled=True)]
    dot_general x16 -> x0, matrix products: 94.8 us -> none  [the longest x6 40 us: times_transpose(): lax.dot_general(left, right, (((1,), (1,)), ((), ())), preferred_element_...]
    unnamed x1 -> x0, blocking collectives: 39.8 us -> none
    all_to_all x2 -> x0, waiting for transfers between devices: 14.9 us -> none  [scatter_columns(): lax.all_to_all(mine, 'seq', split_axis=0, concat_axis=0).astype(WIDE)]
    convert_element_type x6 -> x0, other arithmetic: 9.14 us -> none  [the longest x1 2.45 us: aligned(): down_grad = lax.psum_scatter(outer_sum(hidden, grad_all).astype(LOW), 'fs...]
  transfers between devices with their start and end apart: 14 -> 0, of which waited for: 13 -> 0; matrix products, arithmetic and copies ran while one was open for 11% -> 0% of each run, Pallas kernels for 0% -> 0%
where the time goes in v3:
time: 554 us
  Pallas kernels  521 us (94%)
  other arithmetic  17 us (3%)
  local copies, waits for them, and re-layouts  14.6 us (3%)
    pallas_call x1, Pallas kernels, feed(): pl.pallas_call(feed_kernel, out_shape=outs, in_specs=[HELD, HELD, ANY, AN...  187 us
    pallas_call x1, Pallas kernels, back(): pl.pallas_call(back_kernel, out_shape=outs, in_specs=[HELD, HELD, ANY] +...  139 us
    pallas_call x1, Pallas kernels, mix_in(): pl.pallas_call(mix_in_kernel, out_shape=held + far, in_specs=[HELD] + [AN...  127 us
    pallas_call x1, Pallas kernels, tail(): pl.pallas_call(tail_kernel, out_shape=outs, in_specs=[ANY] * 5, out_specs...  68.4 us

profile of v3, /device:TPU:0, one launch (start us, length us, event | category | flops | bytes accessed | tf_op | source)
XLA Modules:
  0.0 553.6 jit_solution(7931133556469776424)
XLA Ops:
  0.7 0.0 copy-start.7
  0.7 0.7 fusion.6
  1.4 0.7 convert_bitcast_fusion.4
  2.1 0.7 maximum_convert_fusion
  2.8 0.6 pad_maximum_fusion.3.vecs
  3.4 1.3 fusion.3.gain_shard
  4.6 1.5 pad_maximum_fusion.1.small
  6.1 1.3 reshape.107
  7.5 0.0 copy-done.7
  7.5 0.0 copy-start.3
  7.5 0.0 copy-start.4
  7.5 0.3 reshape.108
  7.9 1.0 maximum_bitcast_fusion.1.in_shard
  8.9 0.0 copy-done.3
  8.9 0.0 copy-done.4
  8.9 0.2 copy_bitcast_fusion
  9.1 1.3 maximum_bitcast_fusion.glu_shard
  10.4 126.6 %mix_in.1 = (bf16[8,128,2048]{2,1,0:T(8,128)(2,1)}, bf16[8,4,64,640]{3,2,1,0:T(8,128)(2,1)}, f32[1032,320]{1,0:T(8,128)}, f32[1024,320]{1,0:T(8,128)}, bf16[1024...) custom-call(bf16[128,2048]{1,0:T(8,128)(2,1)} %bitcast.64, ...), custom_call_target="tpu_custom_call" | custom-call | tf_op jit(solution)/shard_map/mix_in/pallas_call | solution.py:567
  137.0 187.4 %feed.1 = (f32[128,2048]{1,0:T(8,128)}, f32[128,2048]{1,0:T(8,128)}, bf16[128,2048]{1,0:T(8,128)(2,1)}, f32[8,2048]{1,0:T(8,128)}, bf16[4,128,2048]{2,1,0:T(8,12...) custom-call(bf16[1024,320]{1,0:T(8,128)(2,1)} %get-tuple-element.56.product.prod, ...), custom_call_target="tpu_custom_call" | custom-call | tf_op jit(solution)/shard_map/feed/pallas_call | solution.py:803
  324.4 138.8 %back.1 = (bf16[128,2048]{1,0:T(8,128)(2,1)}, bf16[128,2048]{1,0:T(8,128)(2,1)}, f32[8,2048]{1,0:T(8,128)}, f32[320,160]{1,0:T(8,128)}, f32[320,160]{1,0:T(8,128...) custom-call(bf16[128,2048]{1,0:T(8,128)(2,1)} %get-tuple-element.61., ...), custom_call_target="tpu_custom_call" | custom-call | tf_op jit(solution)/shard_map/back/pallas_call | solution.py:1083
  463.2 0.8 slice.51
  464.1 0.8 slice.52
  464.9 0.1 reshape.120
  465.1 0.8 reshape.119
  465.9 0.7 pad.17.gain_parts
  466.5 1.2 pad_maximum_fusion
  467.7 0.8 select_maximum_fusion.small
  468.6 0.0 copy-start.8
  468.6 0.0 copy-start
  468.6 68.4 %tail.1 = (bf16[8,64,1536]{2,1,0:T(8,128)(2,1)}, bf16[8,64,640]{2,1,0:T(8,128)(2,1)}, bf16[4,80,2048]{2,1,0:T(8,128)(2,1)}, f32[4,88,320]{2,1,0:T(8,128)}, f32[8,8,64]{2,1,0:T(8,128)}) custom-call(bf16[4,8,64,1536]{3,2,1,0:T(8,128)(2,1)} %get-tuple-element.81.glu_far, bf16[4,8,64,640]{3,2,1,0:T(8,128)(2,1)} %get-tuple-element.82.in_grad, ...), custom_call_target="tpu_custom_call" | custom-call | tf_op jit(solution)/shard_map/tail/pallas_call | solution.py:1203
  537.0 0.8 reduce_sum.36
  537.8 1.1 reduce_sum.38
  538.9 0.5 slice_bitcast_fusion.4
  539.4 0.0 copy-done.8
  539.4 0.5 divide_multiply_fusion
  539.9 0.5 slice_bitcast_fusion.1
  540.5 0.6 slice_bitcast_fusion
  541.0 0.7 fusion.7
  541.8 2.4 convert_reduce_fusion.1
  544.2 0.0 copy-done
  544.2 0.0 copy-start.2
  544.2 1.7 convert_reduce_fusion
  545.9 0.0 copy-done.2
  545.9 0.2 convert_bitcast_fusion.2
  546.1 0.5 copy.41
  546.6 1.0 reshape.132
  547.6 0.0 copy-start.1
  547.7 0.5 copy.40
  548.1 1.0 reshape.130
  549.1 0.0 copy-done.1
  549.2 0.3 convert_bitcast_fusion
  549.5 1.3 copy.47
  550.8 0.0 copy-start.6
  550.8 0.0 copy-start.5
  550.8 1.3 copy.46
  552.0 0.0 copy-done.6
  552.1 0.8 copy.56
  552.8 0.0 copy-done.5
  552.8 0.8 copy.57
  (5 shorter events, 0.1 us)
Async XLA Ops:
  0.7 6.8 %copy-start.7 = (bf16[64,2560]{1,0:T(8,128)(2,1)S(1)}, bf16[64,2560]{1,0:T(8,128)(2,1)}, u32[]{:S(2)}) copy-start(bf16[64,2560]{1,0:T(8,128)(2,1)} %param.21) | copy-start | bytes 983044
  7.5 1.4 copy-start.3
  7.5 1.4 copy-start.4
  468.6 70.8 %copy-start.8 = (bf16[80]{0:T(256)(128)(2,1)S(1)}, bf16[80]{0:T(256)(128)(2,1)}, u32[]{:S(2)}) copy-start(bf16[80]{0:T(256)(128)(2,1)} %param.29) | copy-start | bytes 484
  468.6 75.6 %copy-start = (bf16[4,192,2048]{2,1,0:T(8,128)(2,1)S(1)}, bf16[4,192,2048]{2,1,0:T(8,128)(2,1)}, u32[]{:S(2)}) copy-start(bf16[4,192,2048]{2,1,0:T(8,128)(2,1)} %get-tuple-element.94) | copy-start | bytes 9437188
  544.2 1.7 copy-start.2
  547.6 1.5 copy-start.1
  550.8 1.3 copy-start.6
  550.8 2.1 copy-start.5

commit v4 on v3

--- a/solution.py
+++ b/solution.py
@@ -73,7 +73,7 @@
 
 
 MESH = pl.DeviceIdType.MESH
-VMEM_BYTES = 58 * 2**20
+VMEM_BYTES = 61 * 2**20
 ANY = pl.BlockSpec(memory_space=pl.ANY)
 HELD = pl.BlockSpec(memory_space=pltpu.VMEM)
 ROOT = 0.7978845608028654
@@ -109,6 +109,13 @@
         self.s, self.f = lax.axis_index("seq"), lax.axis_index("fsdp")
         self.z, self.c = self.s // 2, lax.rem(self.s, 2)
         self.sibling = 2 * self.z + 1 - self.c
+
+    def nearest(self, n):
+        chip = 0
+        for z in range(self.line):
+            for place, other in enumerate(sorted(range(self.line), key=lambda y: abs(y - z))):
+                chip = jnp.where((self.z == z) & (n == place), other, chip)
+        return chip
 
     def enter(self, seq=True, fsdp=True):
         barrier = pltpu.get_barrier_semaphore()
@@ -186,49 +193,47 @@
 
             self.copy(at.s, piece, 0, True).start()
 
-    def arrive(self, chip):
+    def arrive(self, chip, piece):
         at = self.at
         slot = 2 * chip + at.c
-        for piece in range(self.pieces):
-            self.copy(slot, piece, 0).wait_recv()
-
-            @pl.when((chip < at.z) & (at.z + 1 < at.line))
-            def _():
-                self.copy(slot, piece, 1).start()
-
-            @pl.when((chip > at.z) & (at.z > 0))
-            def _():
-                self.copy(slot, piece, 2).start()
-
-            self.copy(slot, piece, 0).start()
+        self.copy(slot, piece, 0).wait_recv()
+
+        @pl.when((chip < at.z) & (at.z + 1 < at.line))
+        def _():
+            self.copy(slot, piece, 1).start()
+
+        @pl.when((chip > at.z) & (at.z > 0))
+        def _():
+            self.copy(slot, piece, 2).start()
+
+        self.copy(slot, piece, 0).start()
 
     def settle(self, chip):
         for piece in range(self.pieces):
             self.copy(2 * chip + 1 - self.at.c, piece, 0).wait_recv()
 
-    def distances(self, body):
+    def pass_on(self, d):
         at = self.at
-        self.settle(at.z)
-        body(at.z)
-
-        @pl.loop(1, at.line)
-        def _(d):
-            @pl.when(at.z - d >= 0)
+        for piece in range(self.pieces):
+            for chip, known in ((at.z - d, at.z - d >= 0), (at.z + d, at.z + d < at.line)):
+                @pl.when(known)
+                def _():
+                    self.arrive(chip, piece)
+
+    def distances(self, body, beside=None):
+        at = self.at
+
+        @pl.loop(0, at.line)
+        def _(n):
+            @pl.when(n > 0)
             def _():
-                self.arrive(at.z - d)
-
-            @pl.when(at.z + d < at.line)
-            def _():
-                self.arrive(at.z + d)
-
-            @pl.loop(0, 2)
-            def _(side):
-                chip = at.z - d + 2 * d * side
-
-                @pl.when((chip >= 0) & (chip < at.line))
-                def _():
-                    self.settle(chip)
-                    body(chip)
+                self.pass_on(n)
+                if beside is not None:
+                    beside(n)
+
+            chip = at.nearest(n)
+            self.settle(chip)
+            body(chip)
 
     def sent(self):
         at = self.at
@@ -247,8 +252,8 @@
 
 
 class LineScatter:
-    def __init__(self, at, own, other, heard, out, into, sems, pieces):
-        self.at, self.own, self.other, self.heard, self.out, self.into = at, own, other, heard, out, into
+    def __init__(self, at, own, other, heard, into, sems, pieces):
+        self.at, self.own, self.other, self.heard, self.into = at, own, other, heard, into
         self.sib_send, self.sib_recv, self.send, self.recv = sems
         self.pieces = pieces
         self.rows = own.shape[1] // pieces
@@ -258,8 +263,7 @@
         low = pltpu.VMEM((line, rows, width), LOW)
         return [
             pltpu.VMEM((line, rows, width), WIDE), low, low, low,
-            pltpu.VMEM((line + 1, rows, width), LOW),
-            dma(line), dma(line), dma(line, pieces), dma(line + 1, pieces),
+            dma(line), dma(line), dma(line, pieces), dma(line, pieces),
         ]
 
     def across(self, chip):
@@ -268,20 +272,35 @@
             self.sib_recv.at[chip], "seq", self.at.sibling,
         )
 
-    def along(self, chip, piece, up):
+    def whole_way(self, chip, start):
+        if self.at.line < 4:
+            return False
+        return jnp.abs(chip - start) == self.at.line - 1
+
+    def joined(self, chip):
+        at = self.at
+        if at.line < 4:
+            return False
+        return ((at.z == 1) & (chip == at.line - 1)) | ((at.z == at.line - 2) & (chip == 0))
+
+    def along(self, chip, piece):
         at = self.at
         rows = pl.ds(pl.multiple_of(piece * self.rows, self.rows), self.rows)
-        there = chip if up else jnp.where(chip == at.z - 1, at.line, chip)
+        target, slot = chip, at.z
+        if at.line >= 4:
+            stop = jnp.where(chip > at.z, at.z + 1, at.z - 1)
+            target = jnp.where(self.whole_way(chip, at.z), stop, chip)
+            slot = jnp.where(self.whole_way(chip, at.z), stop, at.z)
         return remote(
-            self.out.at[chip, rows], self.into.at[there, rows], self.send.at[chip, piece],
-            self.recv.at[there, piece], "seq", at.s + 2 if up else at.s - 2,
+            self.other.at[chip, rows], self.into.at[slot, rows], self.send.at[chip, piece],
+            self.recv.at[slot, piece], "seq", 2 * target + at.c,
         )
 
-    def landed(self, index, piece):
+    def landed(self, slot, piece):
         rows = pl.ds(pl.multiple_of(piece * self.rows, self.rows), self.rows)
-        there = self.into.at[index, rows]
+        there = self.into.at[slot, rows]
         remote(
-            there, there, self.recv.at[index, piece], self.recv.at[index, piece], "seq", self.at.sibling
+            there, there, self.recv.at[slot, piece], self.recv.at[slot, piece], "seq", self.at.sibling
         ).wait_recv()
 
     def add(self, chip, piece, extras, store):
@@ -289,68 +308,74 @@
         def _(block):
             rows = pl.ds(pl.multiple_of(piece * self.rows + block * 16, 16), 16)
             total = self.own[chip, rows, :].astype(WIDE) + self.heard[chip, rows, :].astype(WIDE)
-            for known, index in extras:
-                total = total + jnp.where(known, self.into[index, rows, :].astype(WIDE), 0.0)
+            for known, slot in extras:
+                here = self.into[slot, rows, :].astype(WIDE)
+                total = total + (here if known is True else jnp.where(known, here, 0.0))
             store(rows, total)
 
-    def step(self, k):
+    def store_out(self, chip):
+        def store(rows, total):
+            self.other[chip, rows, :] = total.astype(LOW)
+
+        return store
+
+    def push(self, chip):
         at = self.at
-        for up in (True, False):
-            chip = at.line - 1 - k if up else k
-            passes = at.z > 0 if up else at.z + 1 < at.line
-
-            @pl.when(chip > at.z if up else chip < at.z)
+        goes = chip != at.z
+        if at.line >= 4:
+            goes = goes & jnp.logical_not(self.joined(chip))
+
+        @pl.when(goes)
+        def _():
+            self.across(chip).wait()
+
+            @pl.loop(0, self.pieces)
+            def _(piece):
+                self.add(chip, piece, [], self.store_out(chip))
+                self.along(chip, piece).start()
+
+    def join(self):
+        at = self.at
+        if at.line < 4:
+            return
+
+        @pl.when((at.z == 1) | (at.z == at.line - 2))
+        def _():
+            chip = jnp.where(at.z == 1, at.line - 1, 0)
+            self.across(chip).wait()
+
+            @pl.loop(0, self.pieces)
+            def _(piece):
+                self.landed(at.z, piece)
+                self.add(chip, piece, [(True, at.z)], self.store_out(chip))
+                self.along(chip, piece).start()
+
+    def finish(self, store):
+        at = self.at
+        self.across(at.z).wait_recv()
+
+        def known(chip):
+            heard = chip != at.z
+            return heard & jnp.logical_not(self.whole_way(chip, at.z)) if at.line >= 4 else heard
+
+        @pl.loop(0, self.pieces)
+        def _(piece):
+            for chip in range(at.line):
+                @pl.when(known(chip))
+                def _():
+                    self.landed(chip, piece)
+
+            self.add(at.z, piece, [(known(chip), chip) for chip in range(at.line)], store)
+
+    def sent(self):
+        at = self.at
+        self.across(at.z).wait_send()
+        for chip in range(at.line):
+            @pl.when(chip != at.z)
             def _():
-                self.across(chip).wait_recv()
-
                 @pl.loop(0, self.pieces)
                 def _(piece):
-                    @pl.when(passes)
-                    def _():
-                        self.landed(chip, piece)
-
-                    def store(rows, total):
-                        self.out[chip, rows, :] = total.astype(LOW)
-
-                    self.add(chip, piece, [(passes, chip)], store)
-                    self.along(chip, piece, up).start()
-
-    def steps(self, first=0):
-        @pl.loop(first, self.at.line - 1)
-        def _(k):
-            self.step(k)
-
-    def finish(self, store):
-        at = self.at
-        below, above = at.z > 0, at.z + 1 < at.line
-        self.across(at.z).wait_recv()
-
-        @pl.loop(0, self.pieces)
-        def _(piece):
-            @pl.when(below)
-            def _():
-                self.landed(at.z, piece)
-
-            @pl.when(above)
-            def _():
-                self.landed(at.line, piece)
-
-            self.add(at.z, piece, [(below, at.z), (above, at.line)], store)
-
-    def sent(self):
-        at = self.at
-        for chip in range(at.line):
-            self.across(chip).wait_send()
-
-            @pl.loop(0, self.pieces)
-            def _(piece):
-                @pl.when(chip > at.z)
-                def _():
-                    self.along(chip, piece, True).wait_send()
-
-                @pl.when(chip < at.z)
-                def _():
-                    self.along(chip, piece, False).wait_send()
+                    self.along(chip, piece).wait_send()
 
 
 def normalise(source, gain, store, rows):
@@ -437,6 +462,8 @@
         in_z.arrive(d)
         in_xy(in_z.source(d)).start()
     out_xy.start()
+    glu_z.start()
+    down_xy.start()
     gain_z.finish()
     for origin in range(shards):
         for other in range(groups):
@@ -456,7 +483,6 @@
             )
 
     gather.distances(take)
-    glu_z.start()
     keep[6].wait()
     vecs_xy.finish()
     keep[5].wait()
@@ -477,8 +503,6 @@
     for index in range(shards):
         for d in range(1, groups):
             in_xy(index).arrive(d)
-    down_xy.start()
-
     @pl.loop(0, at.line)
     def _(chip):
         pair = normed[pl.ds(2 * chip, 2), :, :].reshape(2 * tokens.shape[0], width)
@@ -567,7 +591,7 @@
     return pl.pallas_call(
         mix_in_kernel,
         out_shape=held + far,
-        in_specs=[HELD] + [ANY] * 7,
+        in_specs=[HELD] * 5 + [ANY] * 3,
         out_specs=[HELD] * len(held) + [ANY] * len(far),
         scratch_shapes=[
             pltpu.VMEM((shards, block, width), LOW),
@@ -590,8 +614,8 @@
 def feed_kernel(
     product, out_whole, glu_mine, down_in, cotangent, tokens, gains,
     middle, middle_grad, mixed_low, gain_sums, fed_own, fed_other, glu_grad, down_grad,
-    held, cots, glu, down, both, hidden, wide_pair, hidden_pair, tile, normed2, staged, down_staged,
-    own, other, heard, out, into, sib_send, sib_recv, line_send, line_recv,
+    held, cots, glu, down, both, hidden, wide_pair, hidden_pair, normed2, staged, down_staged,
+    own, other, heard, into, sib_send, sib_recv, line_send, line_recv,
     local_sems, glu_send, glu_recv, two_send, two_recv, cot_send, cot_recv, stage_sems,
 ):
     shards, groups = glu.shape[0], glu.shape[1]
@@ -615,16 +639,16 @@
     cot_z = LineGather(at, cotangent, cots, cot_send, cot_recv, cot_send.shape[1])
     two_z = LineGather(at, normed2, held, two_send, two_recv, two_send.shape[1])
     sums = LineScatter(
-        at, own, other, heard, out, into, (sib_send, sib_recv, line_send, line_recv), line_send.shape[1]
+        at, own, other, heard, into, (sib_send, sib_recv, line_send, line_recv), line_send.shape[1]
     )
     for index in range(shards):
         glu_xy(index).start()
     cot_z.start()
 
     def split(chip, columns, value, mine, theirs):
-        tile[...] = value.reshape(2, block, value.shape[1])
-        mine[chip, :, columns] = tile[at.c].astype(mine.dtype)
-        theirs[chip, :, columns] = tile[1 - at.c].astype(theirs.dtype)
+        first = at.c == 0
+        mine[chip, :, columns] = jnp.where(first, value[:block], value[block:]).astype(mine.dtype)
+        theirs[chip, :, columns] = jnp.where(first, value[block:], value[:block]).astype(theirs.dtype)
 
     def columns_of(j):
         return pl.ds(pl.multiple_of(j * 256, 256), 256)
@@ -643,8 +667,12 @@
     for k in range(at.line // 2):
         project(at.line - 1 - k)
         project(k)
-        sums.step(k)
-    sums.steps(at.line // 2)
+        sums.push(at.line - 1 - k)
+        sums.push(k)
+    cot_z.pass_on(1)
+    sums.join()
+    for d in range(2, at.line):
+        cot_z.pass_on(d)
 
     def to_middle(here, total):
         values = total + tokens[here, :].astype(WIDE)
@@ -701,30 +729,9 @@
         def _(j):
             split(chip, columns_of(j), dot(hidden[here, :], down[:, columns_of(j)]), fed_own, fed_other)
 
-    two_z.settle(at.z)
-    cot_z.settle(at.z)
-    feed(at.z)
-
-    @pl.loop(1, at.line)
-    def _(d):
-        for gather in (two_z, cot_z):
-            @pl.when(at.z - d >= 0)
-            def _():
-                gather.arrive(at.z - d)
-
-            @pl.when(at.z + d < at.line)
-            def _():
-                gather.arrive(at.z + d)
-
-        @pl.loop(0, 2)
-        def _(side):
-            chip = at.z - d + 2 * d * side
-
-            @pl.when((chip >= 0) & (chip < at.line))
-            def _():
-                two_z.settle(chip)
-                cot_z.settle(chip)
-                feed(chip)
+    for chip in range(at.line):
+        cot_z.settle(chip)
+    two_z.distances(feed)
 
     def glu_out(j):
         return pltpu.make_async_copy(
@@ -758,12 +765,11 @@
             down_staged[lax.rem(j, 2)] = outer_sum(hidden[:, columns_of(j)], grads).astype(LOW)
             down_out(j).start()
 
-    sums.step(0)
+    for n in range(at.line - 1, 0, -1):
+        sums.push(at.nearest(n))
     down_sums()
-    for k in range(1, at.line - 1):
-        sums.step(k)
-        glu_sums((k - 1) * shards // (at.line - 1), k * shards // (at.line - 1))
-    glu_sums((at.line - 2) * shards // (at.line - 1), shards)
+    sums.join()
+    glu_sums(0, shards)
     gain_sums[...] = jnp.zeros_like(gain_sums)
 
     def back(here, grad):
@@ -790,7 +796,7 @@
     shards, rows, both = glu_mine.shape
     block, width = tokens.shape
     units = both // 2
-    line, pieces, thirds = shards // 2, 2, 4
+    line, pieces, thirds = shards // 2, 2, 2
     own = jax.ShapeDtypeStruct((block, width), WIDE)
     low = jax.ShapeDtypeStruct((line, block, width), LOW)
     outs = [
@@ -813,7 +819,6 @@
             pltpu.VMEM((shards * block, units), LOW),
             pltpu.VMEM((2 * block, both), WIDE),
             pltpu.VMEM((2 * block, units), WIDE),
-            pltpu.VMEM((2, block, 256), WIDE),
             pltpu.VMEM((block, width), LOW),
             pltpu.VMEM((2, groups, rows, both), LOW),
             pltpu.VMEM((2, 256, width), LOW),
@@ -831,21 +836,24 @@
 
 
 def back_kernel(
-    mixed, fed_own, fed_other, middle, middle_grad, tokens, gains, par_ref, wr_ref, wi_ref,
+    mixed, fed_own, fed_far, middle, middle_grad, tokens, gains, par_ref, wr_ref, wi_ref,
     out_far, in_far, normed_far, product_far, ext_far, pre_far, conv_far, r_far, i_far, st_far,
-    glu_grad, down_grad,
-    result, tokens_grad, gain_sums, wr_grad, wi_grad, sums_ref, out_grad, in_grad, glu_heard, down_heard,
+    glu_grad, down_grad, mlp_parts,
+    result, tokens_grad, glu_out, in_out, out_heard, small_heard, gain_out, glu_heard, down_heard, in_grad,
     held, in_whole, out_whole, product, ext, pre, conv_ref, r_ref, i_ref, st_ref,
-    both, pair_grad, tile, staged, factors, adj, prod, cg, carries, wr_sum, wi_sum,
-    fed_heard, fed_out, fed_into, fed_sib_send, fed_sib_recv, fed_send, fed_recv,
-    own, other, heard, out, into, sib_send, sib_recv, line_send, line_recv,
-    local_sems, held_send, held_recv, glu_sems, down_sems, stage_sems,
+    both, pair_grad, staged, factors, adj, prod, cg, carries, wr_sum, wi_sum,
+    out_sum, out_grad, small, gain_row, gain_parts, gain_heard, gain_sum, glu_parts, glu_sum, in_heard, in_sum,
+    fed_other, fed_heard, fed_into, fed_sib_send, fed_sib_recv, fed_send, fed_recv,
+    own, other, heard, into, sib_send, sib_recv, line_send, line_recv,
+    local_sems, held_send, held_recv, glu_xy_sems, down_sems, stage_sems, in_xy_sems, out_sems,
+    small_sems, gain_xy_sems, glu_sems, in_sems, gain_sems,
 ):
     shards, groups = in_whole.shape[0], in_whole.shape[1]
     at = Place(shards, groups)
     s, f = at.s, at.f
     block, width = tokens.shape
     positions, channels = product.shape
+    rows = in_whole.shape[2]
     pair = 2 * block
     segment = positions // 8
     chunks = positions // CHUNK
@@ -853,32 +861,44 @@
     keep = [
         (mixed, held.at[s]), (out_far, out_whole), (pre_far, pre), (st_far, st_ref),
         (product_far, product), (r_far, r_ref), (i_far, i_ref), (conv_far, conv_ref),
-        (ext_far, ext), (in_far, in_whole), (glu_grad.at[f], glu_heard.at[f]),
-        (down_grad.at[f], down_heard.at[f]), (normed_far, held),
+        (ext_far, ext), (in_far, in_whole), (fed_far, fed_other), (normed_far, held),
     ]
     keep = [pltpu.make_async_copy(a, b, local_sems.at[n]) for n, (a, b) in enumerate(keep)]
     for copy in keep[:-1]:
         copy.start()
     at.enter()
-    glu_xy = Spread(
-        at, lambda peer: glu_grad.at[peer], lambda origin: glu_heard.at[origin],
-        glu_sems.at[0], glu_sems.at[1],
-    )
-    down_xy = Spread(
-        at, lambda peer: down_grad.at[peer], lambda origin: down_heard.at[origin],
-        down_sems.at[0], down_sems.at[1],
-    )
+
+    def over_fsdp(src, dst, sems):
+        return Spread(
+            at, lambda peer: src.at[peer], lambda origin: dst.at[origin], sems.at[0], sems.at[1]
+        )
+
+    def over_seq(src, dst, sems):
+        return Spread(
+            at, lambda peer: src.at[peer], lambda origin: dst.at[origin], sems.at[0], sems.at[1], "seq"
+        )
+
+    glu_xy = over_fsdp(glu_grad, glu_heard, glu_xy_sems)
+    down_xy = over_fsdp(down_grad, down_heard, down_sems)
+    in_xy = over_fsdp(in_grad, in_heard, in_xy_sems)
+    out_xy = over_fsdp(out_grad, out_heard, out_sems)
+    small_xy = over_fsdp(small, small_heard, small_sems)
+    gain_xy = over_fsdp(gain_parts, gain_heard, gain_xy_sems)
+    glu_z = over_seq(glu_sum, glu_out, glu_sems)
+    in_z = over_seq(in_sum, in_out, in_sems)
+    gain_z = over_seq(gain_sum, gain_out, gain_sems)
     mixed_z = LineGather(at, mixed, held, held_send, held_recv, held_send.shape[1])
     fed = LineScatter(
-        at, fed_own, fed_other, fed_heard, fed_out, fed_into,
+        at, fed_own, fed_other, fed_heard, fed_into,
         (fed_sib_send, fed_sib_recv, fed_send, fed_recv), fed_send.shape[1],
     )
     sums = LineScatter(
-        at, own, other, heard, out, into, (sib_send, sib_recv, line_send, line_recv), line_send.shape[1]
+        at, own, other, heard, into, (sib_send, sib_recv, line_send, line_recv), line_send.shape[1]
     )
     mixed_z.start()
-    down_xy.start()
     glu_xy.start()
+    out_sum[...] = jnp.zeros_like(out_sum)
+    keep[10].wait()
     for k in range(at.line // 2):
         fed.across(at.line - 1 - k).start()
         fed.across(k).start()
@@ -886,9 +906,8 @@
     def columns_of(j):
         return pl.ds(pl.multiple_of(j * 256, 256), 256)
 
-    for n in (1, 2, 3):
+    for n in (0, 1, 2, 3, 4):
         keep[n].wait()
-    keep[0].wait()
 
     def mixed_back(chip):
         rows = held[pl.ds(2 * chip, 2), :, :].reshape(pair, width)
@@ -904,8 +923,22 @@
             put(adj, here, (grad * opened).astype(LOW).astype(WIDE))
             both[here, channels:] = (grad * states * slope).astype(LOW)
 
-    mixed_z.distances(mixed_back)
-    fed.step(0)
+        there = pl.ds(pl.multiple_of(chip * pair, pair), pair)
+
+        @pl.loop(0, width // 256)
+        def _(j):
+            part = held[pl.ds(2 * chip, 2), :, columns_of(j)].reshape(pair, 256)
+            out_sum[:, columns_of(j)] += outer_sum(product[there, :], part)
+
+    for n in range(at.line - 1, 0, -1):
+        fed.push(at.nearest(n))
+
+    def fed_beside(n):
+        @pl.when(n == 1)
+        def _():
+            fed.join()
+
+    mixed_z.distances(mixed_back, fed_beside)
     keep[5].wait()
 
     @pl.loop(0, chunks)
@@ -927,7 +960,6 @@
     for k in range(7, -1, -1):
         carries[k : k + 1, :] = carry
         carry = flow[k : k + 1] + through[k : k + 1] * carry
-    fed.step(1)
     for n in (6, 7, 8):
         keep[n].wait()
     cg[pl.ds(positions, 8), :] = jnp.zeros((8, channels), WIDE)
@@ -968,14 +1000,6 @@
 
     zero = jnp.zeros((1, channels), WIDE)
     totals = lax.fori_loop(0, chunks, grads, (zero,) * 8)
-    for k in range(8):
-        sums_ref[k : k + 1, :] = totals[k]
-    size = wr_grad.shape[1]
-    for n in range(channels // size):
-        part = slice(n * size, (n + 1) * size)
-        wr_grad[part, :] = wr_sum[part, part]
-        wi_grad[part, :] = wi_sum[part, part]
-
     @pl.loop(0, chunks)
     def _(c):
         base = pl.multiple_of(c * CHUNK, CHUNK)
@@ -985,7 +1009,6 @@
             total = total + par_ref[k : k + 1, :] * near[k : k + CHUNK]
         both[pl.ds(base, CHUNK), :channels] = total.astype(LOW)
 
-    fed.steps(2)
     keep[9].wait()
 
     def project(chip):
@@ -994,35 +1017,35 @@
         @pl.loop(0, shards)
         def _(j):
             value = times_transpose(rows, in_whole[j].reshape(width // shards, 2 * channels))
-            tile[...] = value.reshape(2, block, value.shape[1])
-            own[chip, :, columns_of(j)] = tile[at.c]
-            other[chip, :, columns_of(j)] = tile[1 - at.c].astype(LOW)
+            first = at.c == 0
+            own[chip, :, columns_of(j)] = jnp.where(first, value[:block], value[block:]).astype(LOW)
+            other[chip, :, columns_of(j)] = jnp.where(first, value[block:], value[:block]).astype(LOW)
 
         sums.across(chip).start()
 
     for k in range(at.line // 2):
         project(at.line - 1 - k)
         project(k)
-        sums.step(k)
-    keep[4].wait()
-
-    @pl.loop(0, width // 256)
-    def _(j):
-        columns = columns_of(j)
-        grads = held[:, :, columns].reshape(positions, 256)
-        out_grad[:, columns] = outer_sum(product[...], grads).astype(LOW)
-
+        sums.push(at.line - 1 - k)
+        sums.push(k)
     mixed_z.sent()
-    keep[12].start()
-
-    def store_result(here, total):
-        result[here, :] = (middle[here, :] + total).astype(LOW)
-
-    fed.finish(store_result)
-    sums.steps(at.line // 2)
-    keep[12].wait()
-
-    def in_out(j):
+    keep[11].start()
+    local = small.shape[1] - 8
+    size = small.shape[2] // 2
+    for n in range(channels // size):
+        part = slice(n * size, (n + 1) * size)
+        wr_sum[part, :size] = wr_sum[part, part]
+        wi_sum[part, :size] = wi_sum[part, part]
+    for group in range(groups):
+        part = slice(group * local, (group + 1) * local)
+        small[group, :local, :size] = wr_sum[part, :size]
+        small[group, :local, size:] = wi_sum[part, :size]
+        for k in range(8):
+            small[group, local + k : local + k + 1, :local] = totals[k][:, part]
+    small_xy.start()
+    keep[11].wait()
+
+    def in_done(j):
         return pltpu.make_async_copy(
             staged.at[lax.rem(j, 2)], in_grad.at[:, j], stage_sems.at[lax.rem(j, 2)]
         )
@@ -1031,13 +1054,75 @@
     def _(j):
         @pl.when(j >= 2)
         def _():
-            in_out(j - 2).wait()
-
-        rows = held[:, :, columns_of(j)].reshape(positions, 256)
-        staged[lax.rem(j, 2)] = outer_sum(rows, both[...]).astype(LOW).reshape(staged.shape[1:])
-        in_out(j).start()
-
-    gain_sums[...] = jnp.zeros_like(gain_sums)
+            in_done(j - 2).wait()
+
+        part = held[:, :, columns_of(j)].reshape(positions, 256)
+        staged[lax.rem(j, 2)] = outer_sum(part, both[...]).astype(LOW).reshape(staged.shape[1:])
+        in_done(j).start()
+
+    for j in range(shards - 2, shards):
+        in_done(j).wait()
+    in_xy.start()
+    in_own = pltpu.make_async_copy(in_grad.at[f], in_heard.at[f], local_sems.at[12])
+    in_own.start()
+    sums.join()
+    glu_xy.finish()
+    down_xy.start()
+
+    def glu_load(d, origin):
+        peer = lax.rem(s + d, shards)
+        half = lax.rem(d, 2)
+        return pltpu.make_async_copy(
+            glu_heard.at[origin, peer], glu_parts.at[half, origin], glu_sems.at[2 + half, origin]
+        )
+
+    def glu_load_own(d):
+        peer = lax.rem(s + d, shards)
+        half = lax.rem(d, 2)
+        return pltpu.make_async_copy(
+            glu_grad.at[f, peer], glu_parts.at[half, f], glu_sems.at[2 + half, f]
+        )
+
+    def glu_loads(d):
+        glu_load_own(d).start()
+        for hop in range(1, groups):
+            glu_load(d, lax.rem(f + hop, groups)).start()
+
+    def add(parts, total, peer):
+        @pl.loop(0, total.shape[1] // 16)
+        def _(n):
+            here = pl.ds(pl.multiple_of(n * 16, 16), 16)
+            value = parts[0, here, :].astype(WIDE)
+            for origin in range(1, groups):
+                value = value + parts[origin, here, :].astype(WIDE)
+            total[peer, here, :] = value.astype(total.dtype)
+
+    glu_loads(1)
+
+    @pl.loop(1, shards + 1)
+    def _(d):
+        @pl.when(d < shards)
+        def _():
+            glu_loads(d + 1)
+
+        for origin in range(groups):
+            glu_load(d, origin).wait()
+        add(glu_parts.at[lax.rem(d, 2)], glu_sum, lax.rem(s + d, shards))
+
+        @pl.when(d < shards)
+        def _():
+            glu_z.copy(d).start()
+
+    glu_own = pltpu.make_async_copy(glu_sum.at[s], glu_out.at[s], local_sems.at[13])
+    glu_own.start()
+    out_grad[...] = out_sum[...].astype(LOW).reshape(out_grad.shape)
+    out_xy.start()
+    gain_row[...] = jnp.zeros_like(gain_row)
+
+    def store_result(here, total):
+        result[here, :] = (middle[here, :] + total).astype(LOW)
+
+    fed.finish(store_result)
 
     def back(here, grad):
         values = tokens[here, :].astype(WIDE)
@@ -1046,60 +1131,108 @@
         along = jnp.mean(scaled * values, axis=-1, keepdims=True)
         total = middle_grad[here, :] + scale * scaled - values * (scale * scale * scale * along)
         tokens_grad[here, :] = total.astype(LOW)
-        gain_sums[0:1, :] += jnp.sum(grad * values * scale, axis=0, keepdims=True)
+        gain_row[0:1, :] += jnp.sum(grad * values * scale, axis=0, keepdims=True)
 
     sums.finish(back)
-    for j in range(shards - 2, shards):
-        in_out(j).wait()
+    for group in range(groups):
+        for shard in range(shards):
+            first = (shard * groups + group) * rows
+            gain_parts[group, shard, 0:1, :] = gain_row[0:1, first : first + rows]
+            gain_parts[group, shard, 1:2, :] = mlp_parts[0:1, first : first + rows]
+    gain_xy.start()
+    in_own.wait()
+    in_xy.finish()
+
+    @pl.loop(1, shards + 1)
+    def _(d):
+        peer = lax.rem(s + d, shards)
+        add(in_heard.at[:, peer], in_sum, peer)
+
+        @pl.when(d < shards)
+        def _():
+            in_z.copy(d).start()
+
+    last = [
+        pltpu.make_async_copy(in_sum.at[s], in_out.at[s], local_sems.at[14]),
+        pltpu.make_async_copy(out_grad.at[f], out_heard.at[f], local_sems.at[15]),
+        pltpu.make_async_copy(small.at[f], small_heard.at[f], local_sems.at[16]),
+    ]
+    for copy in last:
+        copy.start()
+    gain_xy.finish()
+    total = gain_parts[f]
+    for d in range(1, groups):
+        total = total + gain_heard[lax.rem(f + d, groups)]
+    gain_sum[...] = total
+    gain_z.start()
+    gain_own = pltpu.make_async_copy(gain_sum.at[s], gain_out.at[s], local_sems.at[17])
+    gain_own.start()
     fed.sent()
     sums.sent()
-    keep[10].wait()
-    keep[11].wait()
-    down_xy.finish()
-    glu_xy.finish()
+    for spread in (down_xy, small_xy, out_xy, glu_z, gain_z, in_z):
+        spread.finish()
+    for copy in (glu_own, gain_own, *last):
+        copy.wait()
 
 
 def back(
     mixed, fed_own, fed_other, middle, middle_grad, tokens, gains, par, wr, wi,
-    out_whole, in_whole, normed, product, ext, pre, conv, r, i, st, glu_grad, down_grad, size,
+    out_whole, in_whole, normed, product, ext, pre, conv, r, i, st, glu_grad, down_grad, mlp_sums, size,
 ):
     shards, groups, rows, both = in_whole.shape
     block, width = tokens.shape
     positions, channels = product.shape
-    line, pieces, thirds = shards // 2, 2, 4
+    line, pieces, halves = shards // 2, 2, 2
+    local = channels // groups
     low = pltpu.VMEM((line, block, width), LOW)
     short = jax.ShapeDtypeStruct((block, width), LOW)
-    square = jax.ShapeDtypeStruct((channels, size), WIDE)
+    glu_shape = glu_grad.shape[1:]
+    in_shape = (groups, shards, rows, both)
     outs = [
-        short, short, jax.ShapeDtypeStruct((8, width), WIDE), square, square,
-        jax.ShapeDtypeStruct((8, channels), WIDE),
-        jax.ShapeDtypeStruct((channels, width), LOW),
-        jax.ShapeDtypeStruct((groups, shards, rows, both), LOW),
-        jax.ShapeDtypeStruct(glu_grad.shape, LOW),
-        jax.ShapeDtypeStruct(down_grad.shape, LOW),
+        short, short, jax.ShapeDtypeStruct(glu_shape, LOW), jax.ShapeDtypeStruct(in_shape[1:], LOW),
+        jax.ShapeDtypeStruct((groups, local, width), LOW),
+        jax.ShapeDtypeStruct((groups, local + 8, 2 * size), WIDE),
+        jax.ShapeDtypeStruct((shards, 8, rows), WIDE),
+        jax.ShapeDtypeStruct(glu_grad.shape, LOW), jax.ShapeDtypeStruct(down_grad.shape, LOW),
+        jax.ShapeDtypeStruct(in_shape, LOW),
     ]
     far = [out_whole, in_whole, normed, product, ext, pre, conv, r, i, st]
     near = [in_whole, out_whole, product, ext, pre, conv, r, i, st]
     return pl.pallas_call(
         back_kernel,
         out_shape=outs,
-        in_specs=[HELD, HELD, ANY] + [HELD] * 7 + [ANY] * (len(far) + 2),
-        out_specs=[HELD] * 7 + [ANY] * 3,
+        in_specs=[HELD, HELD, ANY] + [HELD] * 7 + [ANY] * (len(far) + 2) + [HELD],
+        out_specs=[HELD] * 2 + [ANY] * 8,
         scratch_shapes=[pltpu.VMEM((shards, block, width), LOW)]
         + [pltpu.VMEM(member.shape, member.dtype) for member in near]
         + [
             pltpu.VMEM((positions, 2 * channels), LOW),
             pltpu.VMEM((2 * block, channels), WIDE),
-            pltpu.VMEM((2, block, 256), WIDE),
             pltpu.VMEM((2, groups, rows, both), LOW),
         ]
         + [pltpu.VMEM((lane_tiles(channels), positions, 128), WIDE)] * 3
         + [pltpu.VMEM((positions + 8, channels), WIDE), pltpu.VMEM((8, channels), WIDE)]
         + [pltpu.VMEM((channels, channels), WIDE)] * 2
-        + LineScatter.scratch(line, block, width, thirds)[2:]
-        + LineScatter.scratch(line, block, width, thirds)
         + [
-            dma(13), dma(shards, pieces, 3), dma(shards, pieces), dma(2, groups), dma(2, groups), dma(2),
+            pltpu.VMEM((channels, width), WIDE),
+            pltpu.VMEM((groups, local, width), LOW),
+            pltpu.VMEM((groups, local + 8, 2 * size), WIDE),
+            pltpu.VMEM((8, width), WIDE),
+            pltpu.VMEM((groups, shards, 8, rows), WIDE),
+            pltpu.VMEM((groups, shards, 8, rows), WIDE),
+            pltpu.VMEM((shards, 8, rows), WIDE),
+            pltpu.VMEM((2, groups) + glu_shape[1:], LOW),
+            pltpu.VMEM(glu_shape, LOW),
+            pltpu.VMEM(in_shape, LOW),
+            pltpu.VMEM(in_shape[1:], LOW),
+        ]
+        + LineScatter.scratch(line, block, width, halves)[1:]
+        + [low]
+        + LineScatter.scratch(line, block, width, halves)[1:]
+        + [
+            dma(18), dma(shards, pieces, 3), dma(shards, pieces), dma(2, groups), dma(2, groups), dma(2),
+            dma(2, groups), dma(2, groups), dma(2, groups), dma(2, groups),
+            dma(4, shards), dma(2, shards), dma(2, shards),
         ],
         compiler_params=pltpu.CompilerParams(
             collective_id=3, has_side_effects=True, vmem_limit_bytes=VMEM_BYTES
@@ -1107,119 +1240,8 @@
         name="back",
     )(
         mixed, fed_own, fed_other, middle, middle_grad, tokens, gains, par, wr, wi, *far,
-        glu_grad, down_grad,
-    )
-
-
-def tail_kernel(
-    glu_far, in_grad, out_grad, small, gain_parts,
-    glu_out, in_out, out_heard, small_heard, gain_out,
-    glu_heard, glu_sum, in_heard, in_sum, gain_heard, gain_sum,
-    local_sems, in_xy_sems, out_sems, small_sems, gain_xy_sems, glu_sems, in_sems, gain_sems,
-):
-    groups, shards = glu_far.shape[0], glu_far.shape[1]
-    at = Place(shards, groups)
-    s, f = at.s, at.f
-    keep = [
-        (glu_far, glu_heard), (in_grad.at[f], in_heard.at[f]), (out_grad.at[f], out_heard.at[f]),
-        (small.at[f], small_heard.at[f]), (gain_parts.at[f], gain_heard.at[f]),
-    ]
-    keep = [pltpu.make_async_copy(a, b, local_sems.at[n]) for n, (a, b) in enumerate(keep)]
-    for copy in keep:
-        copy.start()
-    at.enter()
-
-    def over_fsdp(src, dst, sems):
-        return Spread(
-            at, lambda peer: src.at[peer], lambda origin: dst.at[origin], sems.at[0], sems.at[1]
-        )
-
-    def over_seq(src, dst, sems):
-        return Spread(
-            at, lambda peer: src.at[peer], lambda origin: dst.at[origin], sems.at[0], sems.at[1], "seq"
-        )
-
-    gain_xy = over_fsdp(gain_parts, gain_heard, gain_xy_sems)
-    in_xy = over_fsdp(in_grad, in_heard, in_xy_sems)
-    small_xy = over_fsdp(small, small_heard, small_sems)
-    out_xy = over_fsdp(out_grad, out_heard, out_sems)
-    glu_z = over_seq(glu_sum, glu_out, glu_sems)
-    in_z = over_seq(in_sum, in_out, in_sems)
-    gain_z = over_seq(gain_sum, gain_out, gain_sems)
-    for spread in (gain_xy, in_xy, small_xy, out_xy):
-        spread.start()
-
-    def add(parts, total, peer):
-        @pl.loop(0, total.shape[1] // 16)
-        def _(n):
-            here = pl.ds(pl.multiple_of(n * 16, 16), 16)
-            value = parts[0, peer, here, :].astype(WIDE)
-            for origin in range(1, groups):
-                value = value + parts[origin, peer, here, :].astype(WIDE)
-            total[peer, here, :] = value.astype(total.dtype)
-
-    def swap(parts, total, spread, into, sem):
-        @pl.loop(1, shards)
-        def _(d):
-            peer = lax.rem(s + d, shards)
-            add(parts, total, peer)
-            spread.copy(d).start()
-
-        add(parts, total, s)
-        mine = pltpu.make_async_copy(total.at[s], into.at[s], sem)
-        mine.start()
-        return mine
-
-    keep[0].wait()
-    glu_own = swap(glu_heard, glu_sum, glu_z, glu_out, local_sems.at[5])
-    gain_xy.finish()
-    keep[4].wait()
-    total = gain_heard[0]
-    for origin in range(1, groups):
-        total = total + gain_heard[origin]
-    gain_sum[...] = total
-    gain_z.start()
-    gain_own = pltpu.make_async_copy(gain_sum.at[s], gain_out.at[s], local_sems.at[6])
-    gain_own.start()
-    in_xy.finish()
-    keep[1].wait()
-    in_own = swap(in_heard, in_sum, in_z, in_out, local_sems.at[7])
-    for spread in (gain_z, small_xy, out_xy, glu_z, in_z):
-        spread.finish()
-    for copy in (keep[2], keep[3], glu_own, gain_own, in_own):
-        copy.wait()
-
-
-def tail(glu_heard, in_grad, out_grad, small, gain_parts):
-    groups, shards, rows, both = glu_heard.shape
-    wide = in_grad.shape[3]
-    outs = [
-        jax.ShapeDtypeStruct((shards, rows, both), LOW),
-        jax.ShapeDtypeStruct((shards, rows, wide), LOW),
-        jax.ShapeDtypeStruct(out_grad.shape, LOW),
-        jax.ShapeDtypeStruct(small.shape, WIDE),
-        jax.ShapeDtypeStruct(gain_parts.shape[1:], WIDE),
-    ]
-    return pl.pallas_call(
-        tail_kernel,
-        out_shape=outs,
-        in_specs=[ANY] * 5,
-        out_specs=[ANY] * 5,
-        scratch_shapes=[
-            pltpu.VMEM(glu_heard.shape, LOW),
-            pltpu.VMEM((shards, rows, both), LOW),
-            pltpu.VMEM(in_grad.shape, LOW),
-            pltpu.VMEM((shards, rows, wide), LOW),
-            pltpu.VMEM(gain_parts.shape, WIDE),
-            pltpu.VMEM(gain_parts.shape[1:], WIDE),
-            dma(8), dma(2, groups), dma(2, groups), dma(2, groups), dma(2, groups),
-            dma(2, shards), dma(2, shards), dma(2, shards),
-        ],
-        compiler_params=pltpu.CompilerParams(
-            collective_id=4, has_side_effects=True, vmem_limit_bytes=VMEM_BYTES
-        ),
-        name="tail",
-    )(glu_heard, in_grad, out_grad, small, gain_parts)
+        glu_grad, down_grad, mlp_sums,
+    )
 
 
 def mixer_forward_kernel(
@@ -1625,27 +1647,17 @@
     middle, middle_grad, mixed_low, mlp_sums, fed_own, fed_other, glu_grad, down_grad = feed(
         product, out_whole, glu_mine, down_whole.reshape(-1, width), grad_low, tokens_low, gains, groups
     )
+    down_grad = down_grad.reshape(groups, -1, width)
     (
-        result, tokens_grad, mix_sums, wr_grad, wi_grad, sums, out_grad, in_grad, glu_heard, down_heard,
+        result, tokens_grad, glu_out, in_out, out_heard, small_heard, gain_out, unused, down_heard, unused,
     ) = back(
         mixed_low, fed_own, fed_other, middle, middle_grad, tokens_low, gains, par, wr, wi,
         out_whole, in_whole, normed, product, ext, branch_pre, conv_low, recur_gate, input_gate, states,
-        glu_grad, down_grad.reshape(groups, -1, width), size,
+        glu_grad, down_grad, mlp_sums, size,
     )
     small_rows = recurrence_weight.shape[0]
-    vector_parts = sums.reshape(8, groups, small_rows).transpose(1, 0, 2)
-    small = jnp.concatenate(
-        [
-            jnp.concatenate([wr_grad, wi_grad], axis=1).reshape(groups, small_rows, 2 * size),
-            jnp.pad(vector_parts, ((0, 0), (0, 0), (0, 2 * size - small_rows))),
-        ],
-        axis=1,
-    )
-    gain_parts = jnp.stack([mix_sums[0], mlp_sums[0]]).reshape(2, shards, groups, rows)
-    gain_parts = jnp.pad(gain_parts.transpose(2, 1, 0, 3), ((0, 0), (0, 0), (0, 6), (0, 0)))
-    glu_out, in_out, out_heard, small_heard, gain_out = tail(
-        glu_heard, in_grad, out_grad.reshape(groups, -1, width), small, gain_parts
-    )
+    mine = jnp.arange(groups)[:, None, None] == lax.axis_index("fsdp")
+    down_heard = jnp.where(mine, down_grad, down_heard)
 
     def rows_of(parts, first, size):
         return parts[:, :, first : first + size].astype(WIDE).transpose(1, 0, 2).reshape(rows, -1)

time: 554 us -> 498 us (0.90)
  Pallas kernels: 521 us -> 473 us
    pallas_call x2 -> x1, Pallas kernels: 195 us -> 113 us  [mix_in(): pl.pallas_call(mix_in_kernel, out_shape=held + far, in_specs=[HELD] * 5 +...]
    pallas_call x1, Pallas kernels: 139 us -> 196 us  [back(): pl.pallas_call(back_kernel, out_shape=outs, in_specs=[HELD, HELD, ANY] +...]
    pallas_call x1, Pallas kernels: 187 us -> 164 us  [feed(): pl.pallas_call(feed_kernel, out_shape=outs, in_specs=[HELD, HELD, ANY, AN...]
where the time goes in v4:
time: 498 us
  Pallas kernels  473 us (95%)
  other arithmetic  12 us (2%)
  local copies, waits for them, and re-layouts  11.8 us (2%)
    pallas_call x1, Pallas kernels, back(): pl.pallas_call(back_kernel, out_shape=outs, in_specs=[HELD, HELD, ANY] +...  196 us
    pallas_call x1, Pallas kernels, feed(): pl.pallas_call(feed_kernel, out_shape=outs, in_specs=[HELD, HELD, ANY, AN...  164 us
    pallas_call x1, Pallas kernels, mix_in(): pl.pallas_call(mix_in_kernel, out_shape=held + far, in_specs=[HELD] * 5 +...  113 us

profile of v4, /device:TPU:0, one launch (start us, length us, event | category | flops | bytes accessed | tf_op | source)
XLA Modules:
  0.0 497.7 jit_solution(12801929924206906031)
XLA Ops:
  0.7 1.5 copy_bitcast_fusion
  2.2 0.0 copy-start.6
  2.2 0.0 copy-start.7
  2.2 1.3 maximum_bitcast_fusion.glu_shard
  3.5 0.0 copy-done.6
  3.5 0.3 reshape.100
  3.8 0.0 copy-done.7
  3.8 0.0 copy-start.8
  3.9 0.0 copy-start.9
  3.9 0.0 copy-start.11
  3.9 0.0 copy-start.12
  3.9 0.0 copy-start.13
  3.9 0.0 copy-start.14
  3.9 0.0 copy-start.17
  3.9 0.0 copy-start.15
  3.9 0.0 copy-start.16
  4.0 0.3 reshape.101
  4.3 1.0 maximum_bitcast_fusion.1.in_shard
  5.4 0.0 copy-done.8
  5.4 0.0 copy-done.9
  5.4 0.7 pad_maximum_fusion.small
  6.1 0.0 copy-done.11
  6.1 0.0 copy-done.12
  6.1 0.0 copy-done.13
  6.1 0.0 copy-done.14
  6.1 0.0 copy-done.17
  6.1 0.6 pad_maximum_fusion.1.vecs
  6.8 0.0 copy-done.15
  6.8 0.0 copy-done.16
  6.8 0.6 fusion.3.gain_shard
  7.4 112.8 %mix_in.1 = (bf16[8,128,2048]{2,1,0:T(8,128)(2,1)}, bf16[8,4,64,640]{3,2,1,0:T(8,128)(2,1)}, f32[1032,320]{1,0:T(8,128)}, f32[1024,320]{1,0:T(8,128)}, bf16[1024...) custom-call(bf16[128,2048]{1,0:T(8,128)(2,1)} %bitcast.58, ...), custom_call_target="tpu_custom_call" | custom-call | tf_op jit(solution)/shard_map/mix_in/pallas_call | solution.py:591
  120.2 163.7 %feed.1 = (f32[128,2048]{1,0:T(8,128)}, f32[128,2048]{1,0:T(8,128)}, bf16[128,2048]{1,0:T(8,128)(2,1)}, f32[8,2048]{1,0:T(8,128)}, bf16[4,128,2048]{2,1,0:T(8,12...) custom-call(bf16[1024,320]{1,0:T(8,128)(2,1)} %get-tuple-element.49.product.prod, ...), custom_call_target="tpu_custom_call" | custom-call | tf_op jit(solution)/shard_map/feed/pallas_call | solution.py:809
  283.9 196.5 %back.1 = (bf16[128,2048]{1,0:T(8,128)(2,1)}, bf16[128,2048]{1,0:T(8,128)(2,1)}, bf16[8,64,1536]{2,1,0:T(8,128)(2,1)}, bf16[8,64,640]{2,1,0:T(8,128)(2,1)}, bf16...) custom-call(bf16[128,2048]{1,0:T(8,128)(2,1)} %get-tuple-element.54., ...), custom_call_target="tpu_custom_call" | custom-call | tf_op jit(solution)/shard_map/back/pallas_call | solution.py:1201
  480.4 0.0 copy-start
  480.4 5.6 %convert_reduce_fusion = f32[192,2048]{1,0:T(8,128)} fusion(bf16[4,192,2048]{2,1,0:T(8,128)(2,1)} %bitcast.55, bf16[4,192,2048]{2,1,0:T(8,128)(2,1)} %get-tuple-element.80, pred[4]{0:T(512)(128)(4,1)S(1)} %iota_compare_fusion.1), kind=kLoop, calls=%fused_computation | loop fusion | flops 4325376 | bytes 7864324 | tf_op jit(solution)/shard_map/reduce_sum | solution.py:1685
  486.0 0.0 copy-done
  486.0 0.3 convert_bitcast_fusion
  486.3 1.3 copy.44
  487.6 0.0 copy-start.2
  487.6 1.3 copy.45
  488.9 0.0 copy-done.2
  488.9 0.2 convert_bitcast_fusion.2
  489.1 0.5 copy.38
  489.6 1.0 reshape.119
  490.6 0.0 copy-start.1
  490.6 0.5 copy.39
  491.1 0.0 copy-start.3
  491.1 1.0 reshape.121
  492.1 0.0 copy-start.10
  492.1 0.0 copy-start.5
  492.1 0.0 copy-done.1
  492.1 0.0 copy-start.4
  492.1 1.0 convert_reduce_fusion.1
  493.2 0.0 copy-done.3
  493.2 0.7 fusion.7
  493.9 0.6 slice_bitcast_fusion
  494.5 0.5 slice_bitcast_fusion.1
  495.0 0.5 divide_multiply_fusion
  495.6 0.0 copy-done.10
  495.6 0.5 slice_bitcast_fusion.4
  496.1 0.0 copy-done.5
  496.1 0.8 copy.50
  496.9 0.0 copy-done.4
  496.9 0.8 copy.51
  (8 shorter events, 0.2 us)
Async XLA Ops:
  2.2 1.3 copy-start.6
  2.2 1.6 copy-start.7
  3.8 1.5 copy-start.8
  3.9 1.5 copy-start.9
  3.9 2.2 copy-start.11
  3.9 2.2 copy-start.12
  3.9 2.2 copy-start.13
  3.9 2.2 copy-start.14
  3.9 2.2 copy-start.17
  3.9 2.8 copy-start.15
  3.9 2.8 copy-start.16
  480.4 5.6 %copy-start = (bf16[8,64,1536]{2,1,0:T(8,128)(2,1)S(1)}, bf16[8,64,1536]{2,1,0:T(8,128)(2,1)}, u32[]{:S(2)}) copy-start(bf16[8,64,1536]{2,1,0:T(8,128)(2,1)} %get-tuple-element.79) | copy-start | bytes 4718596
  487.6 1.3 copy-start.2
  490.6 1.5 copy-start.1
  491.1 2.1 copy-start.3
  492.1 3.4 copy-start.10
  492.1 4.0 copy-start.5
  492.1 4.8 copy-start.4

commit v5 on v4

--- a/solution.py
+++ b/solution.py
@@ -319,13 +319,28 @@
 
         return store
 
+    def goes(self, chip):
+        goes = chip != self.at.z
+        return goes & jnp.logical_not(self.joined(chip)) if self.at.line >= 4 else goes
+
+    def prepare(self, chip):
+        @pl.when(self.goes(chip))
+        def _():
+            self.across(chip).wait()
+
+            @pl.loop(0, self.pieces)
+            def _(piece):
+                self.add(chip, piece, [], self.store_out(chip))
+
+    def launch(self, chip):
+        @pl.when(self.goes(chip))
+        def _():
+            @pl.loop(0, self.pieces)
+            def _(piece):
+                self.along(chip, piece).start()
+
     def push(self, chip):
-        at = self.at
-        goes = chip != at.z
-        if at.line >= 4:
-            goes = goes & jnp.logical_not(self.joined(chip))
-
-        @pl.when(goes)
+        @pl.when(self.goes(chip))
         def _():
             self.across(chip).wait()
 
@@ -393,10 +408,11 @@
 
 def mix_in_kernel(
     tokens, in_shard, glu_shard, out_shard, down_shard, small, vecs, gain_shard,
-    normed, in_whole, ext, pre_ref, conv_ref, r_ref, i_ref, st_ref,
-    product_ref, par_ref, wr_ref, wi_ref, gains, glu_mine, out_whole, down_whole,
+    normed_far, in_far, ext_far, pre_far, conv_far, r_far, i_far, st_far,
+    product_far, par_ref, wr_ref, wi_ref, gains, glu_mine, out_whole, down_whole,
+    normed, in_whole, ext, pre_ref, conv_ref, r_ref, i_ref, st_ref, product_ref,
     held, small_all, vecs_all, gain_all, factors, drive, prod,
-    local_sems, tok_send, tok_recv, in_sems, in_xy_send, in_xy_recv, glu_sems, xy_sems, gain_sems,
+    local_sems, tok_send, tok_recv, in_sems, in_xy_send, in_xy_recv, glu_sems, xy_sems, gain_sems, leave_sems,
 ):
     groups, shards = in_whole.shape[1], in_whole.shape[0]
     at = Place(shards, groups)
@@ -407,6 +423,11 @@
     segment = positions // 8
     chunks = positions // CHUNK
 
+    leaving = [
+        (normed, normed_far), (in_whole, in_far), (ext, ext_far), (pre_ref, pre_far), (conv_ref, conv_far),
+        (r_ref, r_far), (i_ref, i_far), (st_ref, st_far), (product_ref, product_far),
+    ]
+    leaving = [pltpu.make_async_copy(a, b, leave_sems.at[n]) for n, (a, b) in enumerate(leaving)]
     keep = [
         (tokens, held.at[s]), (in_shard.at[s], in_whole.at[s, f]), (glu_shard.at[s], glu_mine.at[s]),
         (out_shard, out_whole.at[f]), (down_shard, down_whole.at[f]), (small, small_all.at[f]),
@@ -483,6 +504,7 @@
             )
 
     gather.distances(take)
+    leaving[0].start()
     keep[6].wait()
     vecs_xy.finish()
     keep[5].wait()
@@ -503,6 +525,7 @@
     for index in range(shards):
         for d in range(1, groups):
             in_xy(index).arrive(d)
+    leaving[1].start()
     @pl.loop(0, at.line)
     def _(chip):
         pair = normed[pl.ds(2 * chip, 2), :, :].reshape(2 * tokens.shape[0], width)
@@ -532,6 +555,9 @@
         put(factors, here, factor)
         put(drive, here, m * gate * conv_low.astype(WIDE))
 
+    for n in range(2, 7):
+        leaving[n].start()
+
     def step(i, n, state, product):
         here = pl.ds(i, 8, stride=segment)
         factor = factors[n, here, :]
@@ -555,6 +581,8 @@
             ).astype(LOW)
         carry = state[k : k + 1] + product[k : k + 1] * carry
 
+    leaving[7].start()
+    leaving[8].start()
     glu_z.finish()
     out_xy.finish()
     down_xy.finish()
@@ -564,6 +592,8 @@
         in_xy(index).sent()
     for n in (2, 3, 4):
         keep[n].wait()
+    for copy in leaving:
+        copy.wait()
 
 
 def mix_in(tokens, in_shard, glu_shard, out_shard, down_shard, small, vecs, gain_shard, groups):
@@ -576,12 +606,14 @@
     low = jax.ShapeDtypeStruct((positions, channels), LOW)
     longer = jax.ShapeDtypeStruct((positions + 8, channels), WIDE)
     square = jax.ShapeDtypeStruct((channels, channels), LOW)
-    held = [
+    saved = [
         jax.ShapeDtypeStruct((shards, block, width), LOW),
         jax.ShapeDtypeStruct((shards, groups, rows, both), LOW),
         longer, wide, low, wide, wide, longer,
-        low, jax.ShapeDtypeStruct((8, channels), WIDE), square, square,
-        jax.ShapeDtypeStruct((8, width), WIDE),
+        low,
+    ]
+    held = [
+        jax.ShapeDtypeStruct((8, channels), WIDE), square, square, jax.ShapeDtypeStruct((8, width), WIDE),
     ]
     far = [
         jax.ShapeDtypeStruct((shards, rows, glu_shard.shape[2]), LOW),
@@ -590,10 +622,11 @@
     ]
     return pl.pallas_call(
         mix_in_kernel,
-        out_shape=held + far,
+        out_shape=saved + held + far,
         in_specs=[HELD] * 5 + [ANY] * 3,
-        out_specs=[HELD] * len(held) + [ANY] * len(far),
-        scratch_shapes=[
+        out_specs=[ANY] * len(saved) + [HELD] * len(held) + [ANY] * len(far),
+        scratch_shapes=[pltpu.VMEM(member.shape, member.dtype) for member in saved]
+        + [
             pltpu.VMEM((shards, block, width), LOW),
             pltpu.VMEM((groups,) + small.shape, LOW),
             pltpu.VMEM((groups,) + vecs.shape, WIDE),
@@ -602,7 +635,7 @@
         + [pltpu.VMEM((lane_tiles(channels), positions, 128), WIDE)] * 3
         + [
             dma(8), dma(shards, pieces, 3), dma(shards, pieces), dma(2, shards), dma(shards, groups),
-            dma(shards, groups), dma(2, shards), dma(5, 2, groups), dma(2, shards),
+            dma(shards, groups), dma(2, shards), dma(5, 2, groups), dma(2, shards), dma(9),
         ],
         compiler_params=pltpu.CompilerParams(
             collective_id=1, has_side_effects=True, vmem_limit_bytes=VMEM_BYTES
@@ -612,9 +645,9 @@
 
 
 def feed_kernel(
-    product, out_whole, glu_mine, down_in, cotangent, tokens, gains,
-    middle, middle_grad, mixed_low, gain_sums, fed_own, fed_other, glu_grad, down_grad,
-    held, cots, glu, down, both, hidden, wide_pair, hidden_pair, normed2, staged, down_staged,
+    product_far, out_far, glu_mine, down_in, cotangent, tokens, gains,
+    middle, middle_grad, mixed_low, gain_sums, fed_own_far, fed_other_far, glu_grad, down_grad,
+    product, out_whole, fed_own, fed_other, held, cots, glu, down, both, hidden, wide_pair, hidden_pair, normed2, staged, down_staged,
     own, other, heard, into, sib_send, sib_recv, line_send, line_recv,
     local_sems, glu_send, glu_recv, two_send, two_recv, cot_send, cot_recv, stage_sems,
 ):
@@ -626,6 +659,7 @@
     pair = 2 * block
 
     keep = [(glu_mine, glu.at[:, f]), (down_in, down), (cotangent, cots.at[s])]
+    keep += [(product_far, product), (out_far, out_whole)]
     keep = [pltpu.make_async_copy(a, b, local_sems.at[n]) for n, (a, b) in enumerate(keep)]
     for copy in keep:
         copy.start()
@@ -656,6 +690,9 @@
     def pair_rows(chip):
         return pl.ds(pl.multiple_of(chip * pair, pair), pair)
 
+    keep[3].wait()
+    keep[4].wait()
+
     def project(chip):
         @pl.loop(0, width // 256)
         def _(j):
@@ -669,10 +706,8 @@
         project(k)
         sums.push(at.line - 1 - k)
         sums.push(k)
+    sums.join()
     cot_z.pass_on(1)
-    sums.join()
-    for d in range(2, at.line):
-        cot_z.pass_on(d)
 
     def to_middle(here, total):
         values = total + tokens[here, :].astype(WIDE)
@@ -682,18 +717,19 @@
 
     sums.finish(to_middle)
     two_z.start()
-    own_copy = pltpu.make_async_copy(normed2, held.at[s], local_sems.at[3])
+    own_copy = pltpu.make_async_copy(normed2, held.at[s], local_sems.at[5])
     own_copy.start()
     keep[0].wait()
     keep[1].wait()
     keep[2].wait()
     sums.sent()
     own_copy.wait()
+    for d in range(2, at.line):
+        cot_z.pass_on(d)
     for index in range(shards):
         glu_xy(index).finish()
 
-    def feed(chip):
-        here = pair_rows(chip)
+    def open_up(chip):
         rows = held[pl.ds(2 * chip, 2), :, :].reshape(pair, width)
         grads = cots[pl.ds(2 * chip, 2), :, :].reshape(pair, width)
 
@@ -718,20 +754,44 @@
             both[there, :units] = (grad * up * slope).astype(LOW)
             both[there, units:] = (grad * opened).astype(LOW)
 
+    def to_normed2(chip):
         @pl.loop(0, shards)
         def _(j):
-            value = times_transpose(both[here, :], glu[j].reshape(width // shards, 2 * units))
+            value = times_transpose(
+                both[pair_rows(chip), :], glu[j].reshape(width // shards, 2 * units)
+            )
             split(chip, columns_of(j), value, own, other)
 
         sums.across(chip).start()
 
+    def to_fed(chip):
         @pl.loop(0, width // 256)
         def _(j):
-            split(chip, columns_of(j), dot(hidden[here, :], down[:, columns_of(j)]), fed_own, fed_other)
-
-    for chip in range(at.line):
-        cot_z.settle(chip)
-    two_z.distances(feed)
+            value = dot(hidden[pair_rows(chip), :], down[:, columns_of(j)])
+            split(chip, columns_of(j), value, fed_own, fed_other)
+
+    cot_z.settle(at.z)
+    two_z.settle(at.z)
+
+    @pl.loop(1, at.line + 1)
+    def _(n):
+        chip = at.nearest(lax.rem(n, at.line))
+
+        @pl.when(n < at.line)
+        def _():
+            two_z.pass_on(n)
+            two_z.settle(chip)
+            cot_z.settle(chip)
+
+        open_up(chip)
+
+        @pl.when(n > 1)
+        def _():
+            sums.push(at.nearest(n - 1))
+
+        to_normed2(chip)
+
+    sums.join()
 
     def glu_out(j):
         return pltpu.make_async_copy(
@@ -765,11 +825,19 @@
             down_staged[lax.rem(j, 2)] = outer_sum(hidden[:, columns_of(j)], grads).astype(LOW)
             down_out(j).start()
 
-    for n in range(at.line - 1, 0, -1):
-        sums.push(at.nearest(n))
     down_sums()
-    sums.join()
-    glu_sums(0, shards)
+
+    @pl.loop(0, at.line)
+    def _(chip):
+        to_fed(chip)
+
+    fed_leave = [
+        pltpu.make_async_copy(fed_own, fed_own_far, local_sems.at[6]),
+        pltpu.make_async_copy(fed_other, fed_other_far, local_sems.at[7]),
+    ]
+    for copy in fed_leave:
+        copy.start()
+
     gain_sums[...] = jnp.zeros_like(gain_sums)
 
     def back(here, grad):
@@ -777,16 +845,19 @@
         scale = lax.rsqrt(jnp.mean(values * values, axis=-1, keepdims=True) + EPSILON)
         scaled = grad * gains[1:2, :]
         along = jnp.mean(scaled * values, axis=-1, keepdims=True)
-        total = cotangent[here, :].astype(WIDE) + scale * scaled - values * (scale * scale * scale * along)
+        total = cots[at.s, here, :].astype(WIDE) + scale * scaled - values * (scale * scale * scale * along)
         middle_grad[here, :] = total
         mixed_low[here, :] = total.astype(LOW)
         gain_sums[0:1, :] += jnp.sum(grad * values * scale, axis=0, keepdims=True)
 
     sums.finish(back)
+    glu_sums(0, shards)
     for j in range(shards - 2, shards):
         glu_out(j).wait()
     for j in range(max(units // 256 - 2, 0), units // 256):
         down_out(j).wait()
+    for copy in fed_leave:
+        copy.wait()
     sums.sent()
     two_z.sent()
     cot_z.sent()
@@ -809,10 +880,11 @@
     return pl.pallas_call(
         feed_kernel,
         out_shape=outs,
-        in_specs=[HELD, HELD, ANY, ANY, HELD, HELD, HELD],
-        out_specs=[HELD] * 6 + [ANY] * 2,
+        in_specs=[ANY] * 5 + [HELD] * 2,
+        out_specs=[HELD] * 4 + [ANY] * 4,
         scratch_shapes=[
-            gathered, gathered,
+            pltpu.VMEM(product.shape, LOW), pltpu.VMEM(out_whole.shape, LOW),
+            pltpu.VMEM(low.shape, LOW), pltpu.VMEM(low.shape, LOW), gathered, gathered,
             pltpu.VMEM((shards, groups, rows, both), LOW),
             pltpu.VMEM((units, width), LOW),
             pltpu.VMEM((shards * block, both), LOW),
@@ -825,7 +897,7 @@
         ]
         + LineScatter.scratch(line, block, width, thirds)
         + [
-            dma(4), dma(shards, groups), dma(shards, groups), dma(shards, pieces, 3), dma(shards, pieces),
+            dma(8), dma(shards, groups), dma(shards, groups), dma(shards, pieces, 3), dma(shards, pieces),
             dma(shards, pieces, 3), dma(shards, pieces), dma(4),
         ],
         compiler_params=pltpu.CompilerParams(
@@ -836,11 +908,11 @@
 
 
 def back_kernel(
-    mixed, fed_own, fed_far, middle, middle_grad, tokens, gains, par_ref, wr_ref, wi_ref,
+    mixed, fed_own_far, fed_far, middle_far, middle_grad_far, tokens_far, gains, par_ref, wr_ref, wi_ref,
     out_far, in_far, normed_far, product_far, ext_far, pre_far, conv_far, r_far, i_far, st_far,
     glu_grad, down_grad, mlp_parts,
-    result, tokens_grad, glu_out, in_out, out_heard, small_heard, gain_out, glu_heard, down_heard, in_grad,
-    held, in_whole, out_whole, product, ext, pre, conv_ref, r_ref, i_ref, st_ref,
+    result, tokens_grad, glu_out, in_out, out_heard, small_heard, gain_out, glu_heard, in_grad, down_heard,
+    fed_own, middle, middle_grad, tokens, held, in_whole, out_whole, product, ext, pre, conv_ref, r_ref, i_ref, st_ref,
     both, pair_grad, staged, factors, adj, prod, cg, carries, wr_sum, wi_sum,
     out_sum, out_grad, small, gain_row, gain_parts, gain_heard, gain_sum, glu_parts, glu_sum, in_heard, in_sum,
     fed_other, fed_heard, fed_into, fed_sib_send, fed_sib_recv, fed_send, fed_recv,
@@ -861,10 +933,11 @@
     keep = [
         (mixed, held.at[s]), (out_far, out_whole), (pre_far, pre), (st_far, st_ref),
         (product_far, product), (r_far, r_ref), (i_far, i_ref), (conv_far, conv_ref),
-        (ext_far, ext), (in_far, in_whole), (fed_far, fed_other), (normed_far, held),
+        (ext_far, ext), (in_far, in_whole), (fed_far, fed_other), (normed_far, held), (fed_own_far, fed_own),
+        (middle_far, middle), (middle_grad_far, middle_grad), (tokens_far, tokens),
     ]
     keep = [pltpu.make_async_copy(a, b, local_sems.at[n]) for n, (a, b) in enumerate(keep)]
-    for copy in keep[:-1]:
+    for copy in keep[:11] + keep[12:]:
         copy.start()
     at.enter()
 
@@ -879,9 +952,9 @@
         )
 
     glu_xy = over_fsdp(glu_grad, glu_heard, glu_xy_sems)
-    down_xy = over_fsdp(down_grad, down_heard, down_sems)
     in_xy = over_fsdp(in_grad, in_heard, in_xy_sems)
     out_xy = over_fsdp(out_grad, out_heard, out_sems)
+    down_xy = over_fsdp(down_grad, down_heard, down_sems)
     small_xy = over_fsdp(small, small_heard, small_sems)
     gain_xy = over_fsdp(gain_parts, gain_heard, gain_xy_sems)
     glu_z = over_seq(glu_sum, glu_out, glu_sems)
@@ -899,6 +972,7 @@
     glu_xy.start()
     out_sum[...] = jnp.zeros_like(out_sum)
     keep[10].wait()
+    keep[12].wait()
     for k in range(at.line // 2):
         fed.across(at.line - 1 - k).start()
         fed.across(k).start()
@@ -931,14 +1005,11 @@
             out_sum[:, columns_of(j)] += outer_sum(product[there, :], part)
 
     for n in range(at.line - 1, 0, -1):
-        fed.push(at.nearest(n))
-
-    def fed_beside(n):
-        @pl.when(n == 1)
-        def _():
-            fed.join()
-
-    mixed_z.distances(mixed_back, fed_beside)
+        fed.prepare(at.nearest(n))
+
+    mixed_z.distances(mixed_back)
+    for n in range(at.line - 1, 0, -1):
+        fed.launch(at.nearest(n))
     keep[5].wait()
 
     @pl.loop(0, chunks)
@@ -1009,6 +1080,7 @@
             total = total + par_ref[k : k + 1, :] * near[k : k + CHUNK]
         both[pl.ds(base, CHUNK), :channels] = total.astype(LOW)
 
+    fed.join()
     keep[9].wait()
 
     def project(chip):
@@ -1063,11 +1135,10 @@
     for j in range(shards - 2, shards):
         in_done(j).wait()
     in_xy.start()
-    in_own = pltpu.make_async_copy(in_grad.at[f], in_heard.at[f], local_sems.at[12])
+    in_own = pltpu.make_async_copy(in_grad.at[f], in_heard.at[f], local_sems.at[16])
     in_own.start()
     sums.join()
     glu_xy.finish()
-    down_xy.start()
 
     def glu_load(d, origin):
         peer = lax.rem(s + d, shards)
@@ -1113,11 +1184,14 @@
         def _():
             glu_z.copy(d).start()
 
-    glu_own = pltpu.make_async_copy(glu_sum.at[s], glu_out.at[s], local_sems.at[13])
+    glu_own = pltpu.make_async_copy(glu_sum.at[s], glu_out.at[s], local_sems.at[17])
     glu_own.start()
     out_grad[...] = out_sum[...].astype(LOW).reshape(out_grad.shape)
     out_xy.start()
     gain_row[...] = jnp.zeros_like(gain_row)
+
+    for n in (13, 14, 15):
+        keep[n].wait()
 
     def store_result(here, total):
         result[here, :] = (middle[here, :] + total).astype(LOW)
@@ -1142,6 +1216,7 @@
     gain_xy.start()
     in_own.wait()
     in_xy.finish()
+    down_xy.start()
 
     @pl.loop(1, shards + 1)
     def _(d):
@@ -1153,9 +1228,9 @@
             in_z.copy(d).start()
 
     last = [
-        pltpu.make_async_copy(in_sum.at[s], in_out.at[s], local_sems.at[14]),
-        pltpu.make_async_copy(out_grad.at[f], out_heard.at[f], local_sems.at[15]),
-        pltpu.make_async_copy(small.at[f], small_heard.at[f], local_sems.at[16]),
+        pltpu.make_async_copy(in_sum.at[s], in_out.at[s], local_sems.at[18]),
+        pltpu.make_async_copy(out_grad.at[f], out_heard.at[f], local_sems.at[19]),
+        pltpu.make_async_copy(small.at[f], small_heard.at[f], local_sems.at[20]),
     ]
     for copy in last:
         copy.start()
@@ -1165,11 +1240,11 @@
         total = total + gain_heard[lax.rem(f + d, groups)]
     gain_sum[...] = total
     gain_z.start()
-    gain_own = pltpu.make_async_copy(gain_sum.at[s], gain_out.at[s], local_sems.at[17])
+    gain_own = pltpu.make_async_copy(gain_sum.at[s], gain_out.at[s], local_sems.at[21])
     gain_own.start()
     fed.sent()
     sums.sent()
-    for spread in (down_xy, small_xy, out_xy, glu_z, gain_z, in_z):
+    for spread in (small_xy, out_xy, down_xy, glu_z, gain_z, in_z):
         spread.finish()
     for copy in (glu_own, gain_own, *last):
         copy.wait()
@@ -1193,17 +1268,19 @@
         jax.ShapeDtypeStruct((groups, local, width), LOW),
         jax.ShapeDtypeStruct((groups, local + 8, 2 * size), WIDE),
         jax.ShapeDtypeStruct((shards, 8, rows), WIDE),
-        jax.ShapeDtypeStruct(glu_grad.shape, LOW), jax.ShapeDtypeStruct(down_grad.shape, LOW),
-        jax.ShapeDtypeStruct(in_shape, LOW),
+        jax.ShapeDtypeStruct(glu_grad.shape, LOW), jax.ShapeDtypeStruct(in_shape, LOW),
+        jax.ShapeDtypeStruct(down_grad.shape, LOW),
     ]
+    late = [fed_own, middle, middle_grad, tokens]
     far = [out_whole, in_whole, normed, product, ext, pre, conv, r, i, st]
     near = [in_whole, out_whole, product, ext, pre, conv, r, i, st]
     return pl.pallas_call(
         back_kernel,
         out_shape=outs,
-        in_specs=[HELD, HELD, ANY] + [HELD] * 7 + [ANY] * (len(far) + 2) + [HELD],
+        in_specs=[ANY] * 6 + [HELD] * 4 + [ANY] * (len(far) + 2) + [HELD],
         out_specs=[HELD] * 2 + [ANY] * 8,
-        scratch_shapes=[pltpu.VMEM((shards, block, width), LOW)]
+        scratch_shapes=[pltpu.VMEM(member.shape, member.dtype) for member in late]
+        + [pltpu.VMEM((shards, block, width), LOW)]
         + [pltpu.VMEM(member.shape, member.dtype) for member in near]
         + [
             pltpu.VMEM((positions, 2 * channels), LOW),
@@ -1230,7 +1307,7 @@
         + [low]
         + LineScatter.scratch(line, block, width, halves)[1:]
         + [
-            dma(18), dma(shards, pieces, 3), dma(shards, pieces), dma(2, groups), dma(2, groups), dma(2),
+            dma(22), dma(shards, pieces, 3), dma(shards, pieces), dma(2, groups), dma(2, groups), dma(2),
             dma(2, groups), dma(2, groups), dma(2, groups), dma(2, groups),
             dma(4, shards), dma(2, shards), dma(2, shards),
         ],
@@ -1649,7 +1726,7 @@
     )
     down_grad = down_grad.reshape(groups, -1, width)
     (
-        result, tokens_grad, glu_out, in_out, out_heard, small_heard, gain_out, unused, down_heard, unused,
+        result, tokens_grad, glu_out, in_out, out_heard, small_heard, gain_out, unused, unused, down_heard,
     ) = back(
         mixed_low, fed_own, fed_other, middle, middle_grad, tokens_low, gains, par, wr, wi,
         out_whole, in_whole, normed, product, ext, branch_pre, conv_low, recur_gate, input_gate, states,

time: 498 us -> 455 us (0.914)
  Pallas kernels: 473 us -> 430 us
    pallas_call x3, Pallas kernels: 473 us -> 430 us  [the longest x1 169 us: back(): pl.pallas_call(back_kernel, out_shape=outs, in_specs=[ANY] * 6 + [HELD] *...]
where the time goes in v5:
time: 455 us
  Pallas kernels  430 us (95%)
  other arithmetic  12 us (3%)
  local copies, waits for them, and re-layouts  11.8 us (3%)
    pallas_call x1, Pallas kernels, back(): pl.pallas_call(back_kernel, out_shape=outs, in_specs=[ANY] * 6 + [HELD] *...  169 us
    pallas_call x1, Pallas kernels, feed(): pl.pallas_call(feed_kernel, out_shape=outs, in_specs=[ANY] * 5 + [HELD] *...  152 us
    pallas_call x1, Pallas kernels, mix_in(): pl.pallas_call(mix_in_kernel, out_shape=saved + held + far, in_specs=[HEL...  109 us

profile of v5, /device:TPU:0, one launch (start us, length us, event | category | flops | bytes accessed | tf_op | source)
XLA Modules:
  0.0 454.8 jit_solution(6299089425075143459)
XLA Ops:
  0.7 1.5 copy_bitcast_fusion
  2.2 0.0 copy-start.6
  2.2 0.0 copy-start.7
  2.2 1.3 maximum_bitcast_fusion.glu_shard
  3.5 0.0 copy-done.6
  3.5 0.3 reshape.100
  3.8 0.0 copy-done.7
  3.8 0.0 copy-start.8
  3.9 0.0 copy-start.9
  3.9 0.0 copy-start.11
  3.9 0.0 copy-start.12
  3.9 0.0 copy-start.13
  3.9 0.0 copy-start.14
  3.9 0.0 copy-start.17
  3.9 0.0 copy-start.15
  3.9 0.0 copy-start.16
  4.0 0.3 reshape.101
  4.3 1.0 maximum_bitcast_fusion.1.in_shard
  5.4 0.0 copy-done.8
  5.4 0.0 copy-done.9
  5.4 0.7 pad_maximum_fusion.small
  6.1 0.0 copy-done.11
  6.1 0.0 copy-done.12
  6.1 0.0 copy-done.13
  6.1 0.0 copy-done.14
  6.1 0.0 copy-done.17
  6.1 0.6 pad_maximum_fusion.1.vecs
  6.8 0.0 copy-done.15
  6.8 0.0 copy-done.16
  6.8 0.6 fusion.3.gain_shard
  7.4 108.6 %mix_in.1 = (bf16[8,128,2048]{2,1,0:T(8,128)(2,1)}, bf16[8,4,64,640]{3,2,1,0:T(8,128)(2,1)}, f32[1032,320]{1,0:T(8,128)}, f32[1024,320]{1,0:T(8,128)}, bf16[1024...) custom-call(bf16[128,2048]{1,0:T(8,128)(2,1)} %bitcast.58, ...), custom_call_target="tpu_custom_call" | custom-call | tf_op jit(solution)/shard_map/mix_in/pallas_call | solution.py:623
  116.0 152.3 %feed.1 = (f32[128,2048]{1,0:T(8,128)}, f32[128,2048]{1,0:T(8,128)}, bf16[128,2048]{1,0:T(8,128)(2,1)}, f32[8,2048]{1,0:T(8,128)}, bf16[4,128,2048]{2,1,0:T(8,12...) custom-call(bf16[1024,320]{1,0:T(8,128)(2,1)} %get-tuple-element.49.product_far,, ...), custom_call_target="tpu_custom_call" | custom-call | tf_op jit(solution)/shard_map/feed/pallas_call | solution.py:880
  268.3 169.2 %back.1 = (bf16[128,2048]{1,0:T(8,128)(2,1)}, bf16[128,2048]{1,0:T(8,128)(2,1)}, bf16[8,64,1536]{2,1,0:T(8,128)(2,1)}, bf16[8,64,640]{2,1,0:T(8,128)(2,1)}, bf16...) custom-call(bf16[128,2048]{1,0:T(8,128)(2,1)} %get-tuple-element.54., ...), custom_call_target="tpu_custom_call" | custom-call | tf_op jit(solution)/shard_map/back/pallas_call | solution.py:1277
  437.5 0.0 copy-start
  437.5 5.6 %convert_reduce_fusion = f32[192,2048]{1,0:T(8,128)} fusion(bf16[4,192,2048]{2,1,0:T(8,128)(2,1)} %bitcast.55, bf16[4,192,2048]{2,1,0:T(8,128)(2,1)} %get-tuple-element.80, pred[4]{0:T(512)(128)(4,1)S(1)} %iota_compare_fusion.1), kind=kLoop, calls=%fused_computation | loop fusion | flops 4325376 | bytes 7864324 | tf_op jit(solution)/shard_map/reduce_sum | solution.py:1762
  443.1 0.0 copy-done
  443.1 0.3 convert_bitcast_fusion
  443.4 1.3 copy.44
  444.7 0.0 copy-start.2
  444.7 1.3 copy.45
  446.0 0.0 copy-done.2
  446.0 0.2 convert_bitcast_fusion.2
  446.2 0.5 copy.38
  446.7 1.0 reshape.119
  447.7 0.0 copy-start.1
  447.7 0.5 copy.39
  448.2 0.0 copy-start.3
  448.2 1.0 reshape.121
  449.2 0.0 copy-start.10
  449.2 0.0 copy-start.5
  449.2 0.0 copy-done.1
  449.2 0.0 copy-start.4
  449.2 1.0 convert_reduce_fusion.1
  450.3 0.0 copy-done.3
  450.3 0.7 fusion.7
  451.0 0.6 slice_bitcast_fusion
  451.6 0.5 slice_bitcast_fusion.1
  452.1 0.5 divide_multiply_fusion
  452.6 0.0 copy-done.10
  452.7 0.5 slice_bitcast_fusion.4
  453.2 0.0 copy-done.5
  453.2 0.8 copy.50
  454.0 0.0 copy-done.4
  454.0 0.8 copy.51
  (8 shorter events, 0.2 us)
Async XLA Ops:
  2.2 1.3 copy-start.6
  2.2 1.6 copy-start.7
  3.8 1.5 copy-start.8
  3.9 1.5 copy-start.9
  3.9 2.2 copy-start.11
  3.9 2.2 copy-start.12
  3.9 2.2 copy-start.13
  3.9 2.2 copy-start.14
  3.9 2.2 copy-start.17
  3.9 2.8 copy-start.15
  3.9 2.8 copy-start.16
  437.5 5.6 %copy-start = (bf16[8,64,1536]{2,1,0:T(8,128)(2,1)S(1)}, bf16[8,64,1536]{2,1,0:T(8,128)(2,1)}, u32[]{:S(2)}) copy-start(bf16[8,64,1536]{2,1,0:T(8,128)(2,1)} %get-tuple-element.79) | copy-start | bytes 4718596
  444.7 1.3 copy-start.2
  447.7 1.5 copy-start.1
  448.2 2.1 copy-start.3
  449.2 3.4 copy-start.10
  449.2 4.0 copy-start.5
  449.2 4.8 %copy-start.4 = (bf16[128,2048]{1,0:T(8,128)(2,1)S(1)}, bf16[128,2048]{1,0:T(8,128)(2,1)}, u32[]{:S(2)}) copy-start(bf16[128,2048]{1,0:T(8,128)(2,1)} %get-tuple-element.74) | copy-start | bytes 1572868

commit v6 on v5

--- a/solution.py
+++ b/solution.py
@@ -180,9 +180,9 @@
             self.send.at[slot, piece, kind], self.recv.at[slot, piece], "seq", peer,
         )
 
-    def start(self):
+    def start(self, first=0, last=None):
         at = self.at
-        for piece in range(self.pieces):
+        for piece in range(first, self.pieces if last is None else last):
             @pl.when(at.z + 1 < at.line)
             def _():
                 self.copy(at.s, piece, 1, True).start()
@@ -252,23 +252,23 @@
 
 
 class LineScatter:
-    def __init__(self, at, own, other, heard, into, sems, pieces):
-        self.at, self.own, self.other, self.heard, self.into = at, own, other, heard, into
+    def __init__(self, at, parts, heard, into, sems, pieces):
+        self.at, self.parts, self.heard, self.into = at, parts, heard, into
         self.sib_send, self.sib_recv, self.send, self.recv = sems
         self.pieces = pieces
-        self.rows = own.shape[1] // pieces
+        self.rows = parts.shape[2] // pieces
 
     @staticmethod
     def scratch(line, rows, width, pieces):
         low = pltpu.VMEM((line, rows, width), LOW)
         return [
-            pltpu.VMEM((line, rows, width), WIDE), low, low, low,
+            pltpu.VMEM((line, 2, rows, width), LOW), low, low,
             dma(line), dma(line), dma(line, pieces), dma(line, pieces),
         ]
 
     def across(self, chip):
         return remote(
-            self.other.at[chip], self.heard.at[chip], self.sib_send.at[chip],
+            self.parts.at[chip, 1 - self.at.c], self.heard.at[chip], self.sib_send.at[chip],
             self.sib_recv.at[chip], "seq", self.at.sibling,
         )
 
@@ -292,7 +292,7 @@
             target = jnp.where(self.whole_way(chip, at.z), stop, chip)
             slot = jnp.where(self.whole_way(chip, at.z), stop, at.z)
         return remote(
-            self.other.at[chip, rows], self.into.at[slot, rows], self.send.at[chip, piece],
+            self.parts.at[chip, 1 - at.c, rows], self.into.at[slot, rows], self.send.at[chip, piece],
             self.recv.at[slot, piece], "seq", 2 * target + at.c,
         )
 
@@ -307,7 +307,7 @@
         @pl.loop(0, self.rows // 16)
         def _(block):
             rows = pl.ds(pl.multiple_of(piece * self.rows + block * 16, 16), 16)
-            total = self.own[chip, rows, :].astype(WIDE) + self.heard[chip, rows, :].astype(WIDE)
+            total = self.parts[chip, self.at.c, rows, :].astype(WIDE) + self.heard[chip, rows, :].astype(WIDE)
             for known, slot in extras:
                 here = self.into[slot, rows, :].astype(WIDE)
                 total = total + (here if known is True else jnp.where(known, here, 0.0))
@@ -315,7 +315,7 @@
 
     def store_out(self, chip):
         def store(rows, total):
-            self.other[chip, rows, :] = total.astype(LOW)
+            self.parts[chip, 1 - self.at.c, rows, :] = total.astype(LOW)
 
         return store
 
@@ -323,33 +323,18 @@
         goes = chip != self.at.z
         return goes & jnp.logical_not(self.joined(chip)) if self.at.line >= 4 else goes
 
-    def prepare(self, chip):
+    def push(self, chip, first=0, last=None):
         @pl.when(self.goes(chip))
         def _():
-            self.across(chip).wait()
-
-            @pl.loop(0, self.pieces)
-            def _(piece):
-                self.add(chip, piece, [], self.store_out(chip))
-
-    def launch(self, chip):
-        @pl.when(self.goes(chip))
-        def _():
-            @pl.loop(0, self.pieces)
-            def _(piece):
-                self.along(chip, piece).start()
-
-    def push(self, chip):
-        @pl.when(self.goes(chip))
-        def _():
-            self.across(chip).wait()
-
-            @pl.loop(0, self.pieces)
+            if first == 0:
+                self.across(chip).wait()
+
+            @pl.loop(first, self.pieces if last is None else last)
             def _(piece):
                 self.add(chip, piece, [], self.store_out(chip))
                 self.along(chip, piece).start()
 
-    def join(self):
+    def join(self, first=0, last=None):
         at = self.at
         if at.line < 4:
             return
@@ -357,23 +342,25 @@
         @pl.when((at.z == 1) | (at.z == at.line - 2))
         def _():
             chip = jnp.where(at.z == 1, at.line - 1, 0)
-            self.across(chip).wait()
-
-            @pl.loop(0, self.pieces)
+            if first == 0:
+                self.across(chip).wait()
+
+            @pl.loop(first, self.pieces if last is None else last)
             def _(piece):
                 self.landed(at.z, piece)
                 self.add(chip, piece, [(True, at.z)], self.store_out(chip))
                 self.along(chip, piece).start()
 
-    def finish(self, store):
+    def finish(self, store, first=0, last=None):
         at = self.at
-        self.across(at.z).wait_recv()
+        if first == 0:
+            self.across(at.z).wait_recv()
 
         def known(chip):
             heard = chip != at.z
             return heard & jnp.logical_not(self.whole_way(chip, at.z)) if at.line >= 4 else heard
 
-        @pl.loop(0, self.pieces)
+        @pl.loop(first, self.pieces if last is None else last)
         def _(piece):
             for chip in range(at.line):
                 @pl.when(known(chip))
@@ -407,11 +394,12 @@
 
 
 def mix_in_kernel(
-    tokens, in_shard, glu_shard, out_shard, down_shard, small, vecs, gain_shard,
+    tokens, lru_rows, gelu_rows, gate_rows, up_rows, out_shard, down_shard, gate_block, input_block,
+    vecs, gain_shard,
     normed_far, in_far, ext_far, pre_far, conv_far, r_far, i_far, st_far,
     product_far, par_ref, wr_ref, wi_ref, gains, glu_mine, out_whole, down_whole,
     normed, in_whole, ext, pre_ref, conv_ref, r_ref, i_ref, st_ref, product_ref,
-    held, small_all, vecs_all, gain_all, factors, drive, prod,
+    in_shard, glu_shard, small, held, small_all, vecs_all, gain_all, factors, drive, prod,
     local_sems, tok_send, tok_recv, in_sems, in_xy_send, in_xy_recv, glu_sems, xy_sems, gain_sems, leave_sems,
 ):
     groups, shards = in_whole.shape[1], in_whole.shape[0]
@@ -423,6 +411,17 @@
     segment = positions // 8
     chunks = positions // CHUNK
 
+    units = gate_rows.shape[1] // shards
+    for shard in range(shards):
+        part = slice(shard * units, (shard + 1) * units)
+        glu_shard[shard, :, :units] = gate_rows[:, part]
+        glu_shard[shard, :, units:] = up_rows[:, part]
+        part = slice(shard * channels, (shard + 1) * channels)
+        in_shard[shard, :, :channels] = lru_rows[:, part]
+        in_shard[shard, :, channels:] = gelu_rows[:, part]
+    size = gate_block.shape[1]
+    small[:, :size] = gate_block[...]
+    small[:, size:] = input_block[...]
     leaving = [
         (normed, normed_far), (in_whole, in_far), (ext, ext_far), (pre_ref, pre_far), (conv_ref, conv_far),
         (r_ref, r_far), (i_ref, i_far), (st_ref, st_far), (product_ref, product_far),
@@ -509,7 +508,6 @@
     vecs_xy.finish()
     keep[5].wait()
     small_xy.finish()
-    size = small.shape[1] // 2
     local = small.shape[0]
     wr_ref[...] = jnp.zeros_like(wr_ref)
     wi_ref[...] = jnp.zeros_like(wi_ref)
@@ -596,11 +594,17 @@
         copy.wait()
 
 
-def mix_in(tokens, in_shard, glu_shard, out_shard, down_shard, small, vecs, gain_shard, groups):
-    shards, rows, both = in_shard.shape
+def mix_in(
+    tokens, lru_rows, gelu_rows, gate_rows, up_rows, out_shard, down_shard, gate_block, input_block,
+    vecs, gain_shard, shards, groups,
+):
+    rows = lru_rows.shape[0]
     block, width = tokens.shape
-    positions, channels = shards * block, both // 2
-    local = small.shape[0]
+    positions, channels = shards * block, lru_rows.shape[1] // shards
+    both = 2 * channels
+    in_shape = (shards, rows, both)
+    glu_shape = (shards, rows, 2 * (gate_rows.shape[1] // shards))
+    small_shape = (gate_block.shape[0], 2 * gate_block.shape[1])
     pieces = 2
     wide = jax.ShapeDtypeStruct((positions, channels), WIDE)
     low = jax.ShapeDtypeStruct((positions, channels), LOW)
@@ -616,19 +620,20 @@
         jax.ShapeDtypeStruct((8, channels), WIDE), square, square, jax.ShapeDtypeStruct((8, width), WIDE),
     ]
     far = [
-        jax.ShapeDtypeStruct((shards, rows, glu_shard.shape[2]), LOW),
+        jax.ShapeDtypeStruct(glu_shape, LOW),
         jax.ShapeDtypeStruct((groups,) + out_shard.shape, LOW),
         jax.ShapeDtypeStruct((groups,) + down_shard.shape, LOW),
     ]
     return pl.pallas_call(
         mix_in_kernel,
         out_shape=saved + held + far,
-        in_specs=[HELD] * 5 + [ANY] * 3,
+        in_specs=[HELD] * 9 + [ANY] * 2,
         out_specs=[ANY] * len(saved) + [HELD] * len(held) + [ANY] * len(far),
         scratch_shapes=[pltpu.VMEM(member.shape, member.dtype) for member in saved]
         + [
+            pltpu.VMEM(in_shape, LOW), pltpu.VMEM(glu_shape, LOW), pltpu.VMEM(small_shape, LOW),
             pltpu.VMEM((shards, block, width), LOW),
-            pltpu.VMEM((groups,) + small.shape, LOW),
+            pltpu.VMEM((groups,) + small_shape, LOW),
             pltpu.VMEM((groups,) + vecs.shape, WIDE),
             pltpu.VMEM((shards, groups) + gain_shard.shape, WIDE),
         ]
@@ -641,14 +646,17 @@
             collective_id=1, has_side_effects=True, vmem_limit_bytes=VMEM_BYTES
         ),
         name="mix_in",
-    )(tokens, in_shard, glu_shard, out_shard, down_shard, small, vecs, gain_shard)
+    )(
+        tokens, lru_rows, gelu_rows, gate_rows, up_rows, out_shard, down_shard, gate_block, input_block,
+        vecs, gain_shard,
+    )
 
 
 def feed_kernel(
     product_far, out_far, glu_mine, down_in, cotangent, tokens, gains,
-    middle, middle_grad, mixed_low, gain_sums, fed_own_far, fed_other_far, glu_grad, down_grad,
-    product, out_whole, fed_own, fed_other, held, cots, glu, down, both, hidden, wide_pair, hidden_pair, normed2, staged, down_staged,
-    own, other, heard, into, sib_send, sib_recv, line_send, line_recv,
+    middle, middle_grad, mixed_low, gain_sums, hidden_far, glu_grad, down_grad,
+    product, out_whole, held, cots, glu, down, both, hidden, wide_pair, hidden_pair, normed2, staged, down_staged,
+    parts, heard, into, sib_send, sib_recv, line_send, line_recv,
     local_sems, glu_send, glu_recv, two_send, two_recv, cot_send, cot_recv, stage_sems,
 ):
     shards, groups = glu.shape[0], glu.shape[1]
@@ -673,16 +681,14 @@
     cot_z = LineGather(at, cotangent, cots, cot_send, cot_recv, cot_send.shape[1])
     two_z = LineGather(at, normed2, held, two_send, two_recv, two_send.shape[1])
     sums = LineScatter(
-        at, own, other, heard, into, (sib_send, sib_recv, line_send, line_recv), line_send.shape[1]
+        at, parts, heard, into, (sib_send, sib_recv, line_send, line_recv), line_send.shape[1]
     )
     for index in range(shards):
         glu_xy(index).start()
     cot_z.start()
 
-    def split(chip, columns, value, mine, theirs):
-        first = at.c == 0
-        mine[chip, :, columns] = jnp.where(first, value[:block], value[block:]).astype(mine.dtype)
-        theirs[chip, :, columns] = jnp.where(first, value[block:], value[:block]).astype(theirs.dtype)
+    def split(chip, columns, value, parts):
+        parts[chip, :, :, columns] = value.astype(LOW).reshape(2, block, value.shape[1])
 
     def columns_of(j):
         return pl.ds(pl.multiple_of(j * 256, 256), 256)
@@ -697,16 +703,19 @@
         @pl.loop(0, width // 256)
         def _(j):
             value = dot(product[pair_rows(chip), :], out_whole[:, columns_of(j)])
-            split(chip, columns_of(j), value, own, other)
+            split(chip, columns_of(j), value, parts)
 
         sums.across(chip).start()
 
     for k in range(at.line // 2):
         project(at.line - 1 - k)
         project(k)
-        sums.push(at.line - 1 - k)
-        sums.push(k)
-    sums.join()
+        sums.push(at.line - 1 - k, 0, 1)
+        sums.push(k, 0, 1)
+    for k in range(at.line // 2):
+        sums.push(at.line - 1 - k, 1)
+        sums.push(k, 1)
+    sums.join(0, 1)
     cot_z.pass_on(1)
 
     def to_middle(here, total):
@@ -715,8 +724,12 @@
         scale = lax.rsqrt(jnp.mean(values * values, axis=-1, keepdims=True) + EPSILON)
         normed2[here, :] = (values * scale * gains[1:2, :]).astype(LOW)
 
-    sums.finish(to_middle)
-    two_z.start()
+    sums.finish(to_middle, 0, 1)
+    two_z.start(0, 1)
+    cot_z.pass_on(2)
+    sums.join(1)
+    sums.finish(to_middle, 1)
+    two_z.start(1)
     own_copy = pltpu.make_async_copy(normed2, held.at[s], local_sems.at[5])
     own_copy.start()
     keep[0].wait()
@@ -724,7 +737,7 @@
     keep[2].wait()
     sums.sent()
     own_copy.wait()
-    for d in range(2, at.line):
+    for d in range(3, at.line):
         cot_z.pass_on(d)
     for index in range(shards):
         glu_xy(index).finish()
@@ -760,15 +773,9 @@
             value = times_transpose(
                 both[pair_rows(chip), :], glu[j].reshape(width // shards, 2 * units)
             )
-            split(chip, columns_of(j), value, own, other)
+            split(chip, columns_of(j), value, parts)
 
         sums.across(chip).start()
-
-    def to_fed(chip):
-        @pl.loop(0, width // 256)
-        def _(j):
-            value = dot(hidden[pair_rows(chip), :], down[:, columns_of(j)])
-            split(chip, columns_of(j), value, fed_own, fed_other)
 
     cot_z.settle(at.z)
     two_z.settle(at.z)
@@ -791,6 +798,8 @@
 
         to_normed2(chip)
 
+    hidden_leave = pltpu.make_async_copy(hidden, hidden_far, local_sems.at[6])
+    hidden_leave.start()
     sums.join()
 
     def glu_out(j):
@@ -826,18 +835,7 @@
             down_out(j).start()
 
     down_sums()
-
-    @pl.loop(0, at.line)
-    def _(chip):
-        to_fed(chip)
-
-    fed_leave = [
-        pltpu.make_async_copy(fed_own, fed_own_far, local_sems.at[6]),
-        pltpu.make_async_copy(fed_other, fed_other_far, local_sems.at[7]),
-    ]
-    for copy in fed_leave:
-        copy.start()
-
+    glu_sums(0, shards)
     gain_sums[...] = jnp.zeros_like(gain_sums)
 
     def back(here, grad):
@@ -851,13 +849,11 @@
         gain_sums[0:1, :] += jnp.sum(grad * values * scale, axis=0, keepdims=True)
 
     sums.finish(back)
-    glu_sums(0, shards)
     for j in range(shards - 2, shards):
         glu_out(j).wait()
     for j in range(max(units // 256 - 2, 0), units // 256):
         down_out(j).wait()
-    for copy in fed_leave:
-        copy.wait()
+    hidden_leave.wait()
     sums.sent()
     two_z.sent()
     cot_z.sent()
@@ -869,10 +865,9 @@
     units = both // 2
     line, pieces, thirds = shards // 2, 2, 2
     own = jax.ShapeDtypeStruct((block, width), WIDE)
-    low = jax.ShapeDtypeStruct((line, block, width), LOW)
     outs = [
         own, own, jax.ShapeDtypeStruct((block, width), LOW), jax.ShapeDtypeStruct((8, width), WIDE),
-        low, low,
+        jax.ShapeDtypeStruct((shards * block, units), LOW),
         jax.ShapeDtypeStruct((groups, shards, rows, both), LOW),
         jax.ShapeDtypeStruct((units, width), LOW),
     ]
@@ -881,10 +876,10 @@
         feed_kernel,
         out_shape=outs,
         in_specs=[ANY] * 5 + [HELD] * 2,
-        out_specs=[HELD] * 4 + [ANY] * 4,
+        out_specs=[HELD] * 4 + [ANY] * 3,
         scratch_shapes=[
             pltpu.VMEM(product.shape, LOW), pltpu.VMEM(out_whole.shape, LOW),
-            pltpu.VMEM(low.shape, LOW), pltpu.VMEM(low.shape, LOW), gathered, gathered,
+            gathered, gathered,
             pltpu.VMEM((shards, groups, rows, both), LOW),
             pltpu.VMEM((units, width), LOW),
             pltpu.VMEM((shards * block, both), LOW),
@@ -908,15 +903,15 @@
 
 
 def back_kernel(
-    mixed, fed_own_far, fed_far, middle_far, middle_grad_far, tokens_far, gains, par_ref, wr_ref, wi_ref,
+    mixed, hidden_far, down_far, middle_far, middle_grad_far, tokens_far, gains, par_ref, wr_ref, wi_ref,
     out_far, in_far, normed_far, product_far, ext_far, pre_far, conv_far, r_far, i_far, st_far,
     glu_grad, down_grad, mlp_parts,
     result, tokens_grad, glu_out, in_out, out_heard, small_heard, gain_out, glu_heard, in_grad, down_heard,
-    fed_own, middle, middle_grad, tokens, held, in_whole, out_whole, product, ext, pre, conv_ref, r_ref, i_ref, st_ref,
-    both, pair_grad, staged, factors, adj, prod, cg, carries, wr_sum, wi_sum,
+    middle, middle_grad, tokens, held, in_whole, out_whole, product, ext, pre, conv_ref, r_ref, i_ref, st_ref,
+    both, pair_grad, staged, adj, totals_ref, wr_sum, wi_sum,
     out_sum, out_grad, small, gain_row, gain_parts, gain_heard, gain_sum, glu_parts, glu_sum, in_heard, in_sum,
-    fed_other, fed_heard, fed_into, fed_sib_send, fed_sib_recv, fed_send, fed_recv,
-    own, other, heard, into, sib_send, sib_recv, line_send, line_recv,
+    fed_parts, fed_heard, fed_into, fed_sib_send, fed_sib_recv, fed_send, fed_recv,
+    parts, heard, into, sib_send, sib_recv, line_send, line_recv,
     local_sems, held_send, held_recv, glu_xy_sems, down_sems, stage_sems, in_xy_sems, out_sems,
     small_sems, gain_xy_sems, glu_sems, in_sems, gain_sems,
 ):
@@ -933,11 +928,11 @@
     keep = [
         (mixed, held.at[s]), (out_far, out_whole), (pre_far, pre), (st_far, st_ref),
         (product_far, product), (r_far, r_ref), (i_far, i_ref), (conv_far, conv_ref),
-        (ext_far, ext), (in_far, in_whole), (fed_far, fed_other), (normed_far, held), (fed_own_far, fed_own),
+        (ext_far, ext), (in_far, in_whole), (mixed, held.at[s]), (normed_far, held),
         (middle_far, middle), (middle_grad_far, middle_grad), (tokens_far, tokens),
     ]
     keep = [pltpu.make_async_copy(a, b, local_sems.at[n]) for n, (a, b) in enumerate(keep)]
-    for copy in keep[:11] + keep[12:]:
+    for copy in keep[:10] + keep[12:]:
         copy.start()
     at.enter()
 
@@ -962,24 +957,45 @@
     gain_z = over_seq(gain_sum, gain_out, gain_sems)
     mixed_z = LineGather(at, mixed, held, held_send, held_recv, held_send.shape[1])
     fed = LineScatter(
-        at, fed_own, fed_other, fed_heard, fed_into,
+        at, fed_parts, fed_heard, fed_into,
         (fed_sib_send, fed_sib_recv, fed_send, fed_recv), fed_send.shape[1],
     )
     sums = LineScatter(
-        at, own, other, heard, into, (sib_send, sib_recv, line_send, line_recv), line_send.shape[1]
+        at, parts, heard, into, (sib_send, sib_recv, line_send, line_recv), line_send.shape[1]
     )
     mixed_z.start()
     glu_xy.start()
     out_sum[...] = jnp.zeros_like(out_sum)
-    keep[10].wait()
-    keep[12].wait()
-    for k in range(at.line // 2):
-        fed.across(at.line - 1 - k).start()
-        fed.across(k).start()
 
     def columns_of(j):
         return pl.ds(pl.multiple_of(j * 256, 256), 256)
 
+    def feed_out(hidden, down, sems):
+        loads = [
+            pltpu.make_async_copy(hidden_far, hidden, sems.at[0]),
+            pltpu.make_async_copy(down_far, down, sems.at[1]),
+        ]
+        for load in loads:
+            load.start()
+        for load in loads:
+            load.wait()
+
+        def one(chip):
+            @pl.loop(0, width // 256)
+            def _(j):
+                there = pl.ds(pl.multiple_of(chip * pair, pair), pair)
+                value = dot(hidden[there, :], down[:, columns_of(j)])
+                fed_parts[chip, :, :, columns_of(j)] = value.astype(LOW).reshape(2, block, 256)
+
+            fed.across(chip).start()
+
+        for k in range(at.line // 2):
+            one(at.line - 1 - k)
+            one(k)
+
+    pl.run_scoped(
+        feed_out, pltpu.VMEM(hidden_far.shape, LOW), pltpu.VMEM(down_far.shape, LOW), dma(2)
+    )
     for n in (0, 1, 2, 3, 4):
         keep[n].wait()
 
@@ -1004,82 +1020,91 @@
             part = held[pl.ds(2 * chip, 2), :, columns_of(j)].reshape(pair, 256)
             out_sum[:, columns_of(j)] += outer_sum(product[there, :], part)
 
-    for n in range(at.line - 1, 0, -1):
-        fed.prepare(at.nearest(n))
-
-    mixed_z.distances(mixed_back)
-    for n in range(at.line - 1, 0, -1):
-        fed.launch(at.nearest(n))
-    keep[5].wait()
-
-    @pl.loop(0, chunks)
-    def _(n):
-        here = pl.ds(pl.multiple_of(n * CHUNK, CHUNK), CHUNK)
-        put(factors, here, jnp.exp(r_ref[here, :] * par_ref[7:8, :]))
-
-    def step(j, n, flow, product):
-        here = pl.ds(segment - 1 - j, 8, stride=segment)
-        factor = factors[n, here, :]
-        adjoint = adj[n, here, :] + flow
-        adj[n, here, :] = adjoint
-        prod[n, here, :] = product
-        return factor * adjoint, factor * product
-
-    flow, through = scan_segments(step, segment, lane_tiles(channels))
-    flow, through = flow[:, :channels], through[:, :channels]
-    carry = jnp.zeros((1, channels), WIDE)
-    for k in range(7, -1, -1):
-        carries[k : k + 1, :] = carry
-        carry = flow[k : k + 1] + through[k : k + 1] * carry
-    for n in (6, 7, 8):
-        keep[n].wait()
-    cg[pl.ds(positions, 8), :] = jnp.zeros((8, channels), WIDE)
-    wr_sum[...] = jnp.zeros_like(wr_sum)
-    wi_sum[...] = jnp.zeros_like(wi_sum)
-
-    def grads(c, sums):
-        base = pl.multiple_of(c * CHUNK, CHUNK)
-        rows = pl.ds(base, CHUNK)
-        adjoint = get(adj, rows, channels) + get(prod, rows, channels) * carries[pl.ds(base // segment, 1), :]
-        before = st_ref[pl.ds(base, CHUNK + 8), :][7 : 7 + CHUNK]
-        conv_low = conv_ref[rows, :]
-        conv = conv_low.astype(WIDE)
-        r = r_ref[rows, :]
-        gate = i_ref[rows, :]
-        factor = get(factors, rows, channels)
-        m = jnp.sqrt(one_minus_exp(-2.0 * (r * par_ref[7:8, :])))
-        driven = adjoint * gate
-        by_log = adjoint * before * factor - driven * conv * factor * factor / m
-        by_r = by_log * par_ref[7:8, :] * r * (1.0 - r)
-        by_i = adjoint * m * conv * gate * (1.0 - gate)
-        by_r_low = by_r.astype(LOW)
-        by_i_low = by_i.astype(LOW)
-        conv_grad = (
-            driven * m
-            + times_transpose(by_r_low, wr_ref[...])
-            + times_transpose(by_i_low, wi_ref[...])
-        )
-        cg[rows, :] = conv_grad
-        wr_sum[...] += outer_sum(conv_low, by_r_low)
-        wi_sum[...] += outer_sum(conv_low, by_i_low)
-        near = ext[pl.ds(base, CHUNK + 8), :]
-        rows_of = [conv_grad * near[8 - k : 8 - k + CHUNK] for k in range(4)]
-        rows_of += [conv_grad, by_r, by_i, by_log * r]
-        return tuple(
-            total + jnp.sum(member, axis=0, keepdims=True) for total, member in zip(sums, rows_of)
-        )
-
-    zero = jnp.zeros((1, channels), WIDE)
-    totals = lax.fori_loop(0, chunks, grads, (zero,) * 8)
-    @pl.loop(0, chunks)
-    def _(c):
-        base = pl.multiple_of(c * CHUNK, CHUNK)
-        near = cg[pl.ds(base, CHUNK + 8), :]
-        total = jnp.zeros((CHUNK, channels), WIDE)
-        for k in range(4):
-            total = total + par_ref[k : k + 1, :] * near[k : k + CHUNK]
-        both[pl.ds(base, CHUNK), :channels] = total.astype(LOW)
-
+    def fed_beside(n):
+        @pl.when(n == 2)
+        def _():
+            @pl.loop(1, at.line)
+            def _(far):
+                fed.push(at.nearest(at.line - far))
+
+    mixed_z.distances(mixed_back, fed_beside)
+    def mix_back(factors, prod, cg, carries):
+        keep[5].wait()
+
+        @pl.loop(0, chunks)
+        def _(n):
+            here = pl.ds(pl.multiple_of(n * CHUNK, CHUNK), CHUNK)
+            put(factors, here, jnp.exp(r_ref[here, :] * par_ref[7:8, :]))
+
+        def step(j, n, flow, product):
+            here = pl.ds(segment - 1 - j, 8, stride=segment)
+            factor = factors[n, here, :]
+            adjoint = adj[n, here, :] + flow
+            adj[n, here, :] = adjoint
+            prod[n, here, :] = product
+            return factor * adjoint, factor * product
+
+        flow, through = scan_segments(step, segment, lane_tiles(channels))
+        flow, through = flow[:, :channels], through[:, :channels]
+        carry = jnp.zeros((1, channels), WIDE)
+        for k in range(7, -1, -1):
+            carries[k : k + 1, :] = carry
+            carry = flow[k : k + 1] + through[k : k + 1] * carry
+        for n in (6, 7, 8):
+            keep[n].wait()
+        cg[pl.ds(positions, 8), :] = jnp.zeros((8, channels), WIDE)
+        wr_sum[...] = jnp.zeros_like(wr_sum)
+        wi_sum[...] = jnp.zeros_like(wi_sum)
+
+        def grads(c, sums):
+            base = pl.multiple_of(c * CHUNK, CHUNK)
+            rows = pl.ds(base, CHUNK)
+            adjoint = get(adj, rows, channels) + get(prod, rows, channels) * carries[pl.ds(base // segment, 1), :]
+            before = st_ref[pl.ds(base, CHUNK + 8), :][7 : 7 + CHUNK]
+            conv_low = conv_ref[rows, :]
+            conv = conv_low.astype(WIDE)
+            r = r_ref[rows, :]
+            gate = i_ref[rows, :]
+            factor = get(factors, rows, channels)
+            m = jnp.sqrt(one_minus_exp(-2.0 * (r * par_ref[7:8, :])))
+            driven = adjoint * gate
+            by_log = adjoint * before * factor - driven * conv * factor * factor / m
+            by_r = by_log * par_ref[7:8, :] * r * (1.0 - r)
+            by_i = adjoint * m * conv * gate * (1.0 - gate)
+            by_r_low = by_r.astype(LOW)
+            by_i_low = by_i.astype(LOW)
+            conv_grad = (
+                driven * m
+                + times_transpose(by_r_low, wr_ref[...])
+                + times_transpose(by_i_low, wi_ref[...])
+            )
+            cg[rows, :] = conv_grad
+            wr_sum[...] += outer_sum(conv_low, by_r_low)
+            wi_sum[...] += outer_sum(conv_low, by_i_low)
+            near = ext[pl.ds(base, CHUNK + 8), :]
+            rows_of = [conv_grad * near[8 - k : 8 - k + CHUNK] for k in range(4)]
+            rows_of += [conv_grad, by_r, by_i, by_log * r]
+            return tuple(
+                total + jnp.sum(member, axis=0, keepdims=True) for total, member in zip(sums, rows_of)
+            )
+
+        zero = jnp.zeros((1, channels), WIDE)
+        totals = lax.fori_loop(0, chunks, grads, (zero,) * 8)
+        for k in range(8):
+            totals_ref[k : k + 1, :] = totals[k]
+        @pl.loop(0, chunks)
+        def _(c):
+            base = pl.multiple_of(c * CHUNK, CHUNK)
+            near = cg[pl.ds(base, CHUNK + 8), :]
+            total = jnp.zeros((CHUNK, channels), WIDE)
+            for k in range(4):
+                total = total + par_ref[k : k + 1, :] * near[k : k + CHUNK]
+            both[pl.ds(base, CHUNK), :channels] = total.astype(LOW)
+
+    tiles = pltpu.VMEM((lane_tiles(channels), positions, 128), WIDE)
+    pl.run_scoped(
+        mix_back, tiles, tiles, pltpu.VMEM((positions + 8, channels), WIDE), pltpu.VMEM((8, channels), WIDE)
+    )
     fed.join()
     keep[9].wait()
 
@@ -1089,9 +1114,7 @@
         @pl.loop(0, shards)
         def _(j):
             value = times_transpose(rows, in_whole[j].reshape(width // shards, 2 * channels))
-            first = at.c == 0
-            own[chip, :, columns_of(j)] = jnp.where(first, value[:block], value[block:]).astype(LOW)
-            other[chip, :, columns_of(j)] = jnp.where(first, value[block:], value[:block]).astype(LOW)
+            parts[chip, :, :, columns_of(j)] = value.astype(LOW).reshape(2, block, value.shape[1])
 
         sums.across(chip).start()
 
@@ -1113,7 +1136,7 @@
         small[group, :local, :size] = wr_sum[part, :size]
         small[group, :local, size:] = wi_sum[part, :size]
         for k in range(8):
-            small[group, local + k : local + k + 1, :local] = totals[k][:, part]
+            small[group, local + k : local + k + 1, :local] = totals_ref[k : k + 1, part]
     small_xy.start()
     keep[11].wait()
 
@@ -1190,7 +1213,7 @@
     out_xy.start()
     gain_row[...] = jnp.zeros_like(gain_row)
 
-    for n in (13, 14, 15):
+    for n in (12, 13, 14):
         keep[n].wait()
 
     def store_result(here, total):
@@ -1251,7 +1274,7 @@
 
 
 def back(
-    mixed, fed_own, fed_other, middle, middle_grad, tokens, gains, par, wr, wi,
+    mixed, hidden, down_whole, middle, middle_grad, tokens, gains, par, wr, wi,
     out_whole, in_whole, normed, product, ext, pre, conv, r, i, st, glu_grad, down_grad, mlp_sums, size,
 ):
     shards, groups, rows, both = in_whole.shape
@@ -1259,7 +1282,6 @@
     positions, channels = product.shape
     line, pieces, halves = shards // 2, 2, 2
     local = channels // groups
-    low = pltpu.VMEM((line, block, width), LOW)
     short = jax.ShapeDtypeStruct((block, width), LOW)
     glu_shape = glu_grad.shape[1:]
     in_shape = (groups, shards, rows, both)
@@ -1271,7 +1293,7 @@
         jax.ShapeDtypeStruct(glu_grad.shape, LOW), jax.ShapeDtypeStruct(in_shape, LOW),
         jax.ShapeDtypeStruct(down_grad.shape, LOW),
     ]
-    late = [fed_own, middle, middle_grad, tokens]
+    late = [middle, middle_grad, tokens]
     far = [out_whole, in_whole, normed, product, ext, pre, conv, r, i, st]
     near = [in_whole, out_whole, product, ext, pre, conv, r, i, st]
     return pl.pallas_call(
@@ -1287,8 +1309,7 @@
             pltpu.VMEM((2 * block, channels), WIDE),
             pltpu.VMEM((2, groups, rows, both), LOW),
         ]
-        + [pltpu.VMEM((lane_tiles(channels), positions, 128), WIDE)] * 3
-        + [pltpu.VMEM((positions + 8, channels), WIDE), pltpu.VMEM((8, channels), WIDE)]
+        + [pltpu.VMEM((lane_tiles(channels), positions, 128), WIDE), pltpu.VMEM((8, channels), WIDE)]
         + [pltpu.VMEM((channels, channels), WIDE)] * 2
         + [
             pltpu.VMEM((channels, width), WIDE),
@@ -1303,9 +1324,7 @@
             pltpu.VMEM(in_shape, LOW),
             pltpu.VMEM(in_shape[1:], LOW),
         ]
-        + LineScatter.scratch(line, block, width, halves)[1:]
-        + [low]
-        + LineScatter.scratch(line, block, width, halves)[1:]
+        + LineScatter.scratch(line, block, width, halves) * 2
         + [
             dma(22), dma(shards, pieces, 3), dma(shards, pieces), dma(2, groups), dma(2, groups), dma(2),
             dma(2, groups), dma(2, groups), dma(2, groups), dma(2, groups),
@@ -1316,9 +1335,82 @@
         ),
         name="back",
     )(
-        mixed, fed_own, fed_other, middle, middle_grad, tokens, gains, par, wr, wi, *far,
+        mixed, hidden, down_whole, middle, middle_grad, tokens, gains, par, wr, wi, *far,
         glu_grad, down_grad, mlp_sums,
     )
+
+
+def settle_kernel(
+    glu_far, ins_far, outs_far, down_heard, down_grad,
+    gate_far, up_far, lru_far, gelu_far, out_far, down_far,
+    glu, ins, outs, parts, gate_sum, up_sum, lru_sum, gelu_sum, out_sum, down_sum, sems, leave_sems,
+):
+    shards, rows, both = glu.shape
+    groups = outs.shape[0]
+    units, channels = both // 2, ins.shape[2] // 2
+    f = lax.axis_index("fsdp")
+    keep = [(glu_far, glu), (ins_far, ins), (outs_far, outs), (down_grad.at[f], parts.at[f])]
+    for hop in range(1, groups):
+        origin = lax.rem(f + hop, groups)
+        keep.append((down_heard.at[origin], parts.at[origin]))
+    keep = [pltpu.make_async_copy(a, b, sems.at[n]) for n, (a, b) in enumerate(keep)]
+    for copy in keep:
+        copy.start()
+    leaving = [
+        (gate_sum, gate_far), (up_sum, up_far), (lru_sum, lru_far), (gelu_sum, gelu_far),
+        (out_sum, out_far), (down_sum, down_far),
+    ]
+    leaving = [pltpu.make_async_copy(a, b, leave_sems.at[n]) for n, (a, b) in enumerate(leaving)]
+    keep[0].wait()
+    for half, whole in enumerate((gate_sum, up_sum)):
+        for shard in range(shards):
+            part = slice(half * units, (half + 1) * units)
+            whole[:, shard * units : (shard + 1) * units] = glu[shard, :, part].astype(WIDE)
+        leaving[half].start()
+    keep[1].wait()
+    for half, whole in enumerate((lru_sum, gelu_sum)):
+        for shard in range(shards):
+            part = slice(half * channels, (half + 1) * channels)
+            whole[:, shard * channels : (shard + 1) * channels] = ins[shard, :, part].astype(WIDE)
+        leaving[2 + half].start()
+
+    def add(terms, total):
+        @pl.loop(0, total.shape[0] // 16)
+        def _(n):
+            here = pl.ds(pl.multiple_of(n * 16, 16), 16)
+            value = terms[0, here, :].astype(WIDE)
+            for origin in range(1, groups):
+                value = value + terms[origin, here, :].astype(WIDE)
+            total[here, :] = value
+
+    keep[2].wait()
+    add(outs, out_sum)
+    leaving[4].start()
+    for copy in keep[3:]:
+        copy.wait()
+    add(parts, down_sum)
+    leaving[5].start()
+    for copy in leaving:
+        copy.wait()
+
+
+def settle(glu, ins, outs, down_heard, down_grad):
+    shards, rows, both = glu.shape
+    groups, local, width = outs.shape
+    units, channels = both // 2, ins.shape[2] // 2
+    shapes = [(rows, shards * units)] * 2 + [(rows, shards * channels)] * 2
+    shapes += [(local, width), down_grad.shape[1:]]
+    return pl.pallas_call(
+        settle_kernel,
+        out_shape=[jax.ShapeDtypeStruct(shape, WIDE) for shape in shapes],
+        in_specs=[ANY] * 5,
+        out_specs=[ANY] * 6,
+        scratch_shapes=[pltpu.VMEM(member.shape, LOW) for member in (glu, ins, outs, down_grad)]
+        + [pltpu.VMEM(shape, WIDE) for shape in shapes]
+        + [dma(groups + 3), dma(6)],
+        compiler_params=pltpu.CompilerParams(vmem_limit_bytes=VMEM_BYTES),
+        name="settle",
+    )(glu, ins, outs, down_heard, down_grad)
 
 
 def mixer_forward_kernel(
@@ -1697,10 +1789,6 @@
     resid_in = tokens.reshape(positions, width).astype(WIDE)
     grad_low = cotangent.reshape(positions, width)
 
-    def by_column(first, second):
-        parts = [member.reshape(rows, shards, -1) for member in (first, second)]
-        return jnp.concatenate(parts, axis=2).transpose(1, 0, 2)
-
     own_decay = decay_param.astype(WIDE)
     vecs = jnp.concatenate(
         [
@@ -1716,39 +1804,35 @@
         normed, in_whole, ext, branch_pre, conv_low, recur_gate, input_gate, states, product, par, wr, wi,
         gains, glu_mine, out_whole, down_whole,
     ) = mix_in(
-        tokens_low, by_column(lru_in_weight, gelu_in_weight), by_column(gate_weight, up_weight),
-        out_weight, down_weight, jnp.concatenate([recurrence_weight, input_gate_weight], axis=1),
-        vecs, gain_shard, groups,
-    )
-    out_whole = out_whole.reshape(-1, width)
-    middle, middle_grad, mixed_low, mlp_sums, fed_own, fed_other, glu_grad, down_grad = feed(
-        product, out_whole, glu_mine, down_whole.reshape(-1, width), grad_low, tokens_low, gains, groups
+        tokens_low, lru_in_weight, gelu_in_weight, gate_weight, up_weight, out_weight, down_weight,
+        recurrence_weight, input_gate_weight, vecs, gain_shard, shards, groups,
+    )
+    out_whole, down_whole = out_whole.reshape(-1, width), down_whole.reshape(-1, width)
+    middle, middle_grad, mixed_low, mlp_sums, hidden, glu_grad, down_grad = feed(
+        product, out_whole, glu_mine, down_whole, grad_low, tokens_low, gains, groups
     )
     down_grad = down_grad.reshape(groups, -1, width)
     (
         result, tokens_grad, glu_out, in_out, out_heard, small_heard, gain_out, unused, unused, down_heard,
     ) = back(
-        mixed_low, fed_own, fed_other, middle, middle_grad, tokens_low, gains, par, wr, wi,
+        mixed_low, hidden, down_whole, middle, middle_grad, tokens_low, gains, par, wr, wi,
         out_whole, in_whole, normed, product, ext, branch_pre, conv_low, recur_gate, input_gate, states,
         glu_grad, down_grad, mlp_sums, size,
     )
     small_rows = recurrence_weight.shape[0]
-    mine = jnp.arange(groups)[:, None, None] == lax.axis_index("fsdp")
-    down_heard = jnp.where(mine, down_grad, down_heard)
-
-    def rows_of(parts, first, size):
-        return parts[:, :, first : first + size].astype(WIDE).transpose(1, 0, 2).reshape(rows, -1)
-
+    gate_sum, up_sum, lru_sum, gelu_sum, out_sum, down_sum = settle(
+        glu_out, in_out, out_heard, down_heard, down_grad
+    )
     small = jnp.sum(small_heard, axis=0)
+    gain_grads = jnp.sum(gain_out, axis=0)
     vector_sums = small[small_rows:, :small_rows]
-    gain_grads = jnp.sum(gain_out, axis=0)
     return (
         result.reshape(tokens.shape),
         tokens_grad.reshape(tokens.shape),
         gain_grads[0],
-        rows_of(in_out, 0, channels),
-        rows_of(in_out, channels, channels),
-        jnp.sum(out_heard.astype(WIDE), axis=0),
+        lru_sum,
+        gelu_sum,
+        out_sum,
         vector_sums[:4].T,
         vector_sums[4],
         small[:small_rows, :size],
@@ -1757,9 +1841,9 @@
         vector_sums[6],
         vector_sums[7] * RATE_SCALE * jax.nn.sigmoid(-own_decay),
         gain_grads[1],
-        rows_of(glu_out, 0, hidden_width),
-        rows_of(glu_out, hidden_width, hidden_width),
-        jnp.sum(down_heard.astype(WIDE), axis=0),
+        gate_sum,
+        up_sum,
+        down_sum,
     )
 
 

time: 455 us -> 441 us (0.969)
  local copies, waits for them, and re-layouts: 11.8 us -> 3.95 us
  other arithmetic: 12 us -> 6.32 us
    pallas_call x1, Pallas kernels: 152 us -> 143 us  [feed(): pl.pallas_call(feed_kernel, out_shape=outs, in_specs=[ANY] * 5 + [HELD] *...]
    reshape x11 -> x0, local copies, waits for them, and re-layouts: 7.74 us -> none  [the longest x6 5.53 us: rows_of(): parts[:, :, first:first + size].astype(WIDE).transpose(1, 0, 2)]
    reduce_sum x2 -> x0, other arithmetic: 6.64 us -> none  [the longest x1 5.6 us: aligned(): jnp.sum(down_heard.astype(WIDE), axis=0)]
    pallas_call x0 -> x1, Pallas kernels: none -> 5.82 us  [settle(): pl.pallas_call(settle_kernel, out_shape=[jax.ShapeDtypeStruct(shape, WIDE...]
where the time goes in v6:
time: 441 us; the launch traced here: 440 us
  Pallas kernels  429 us (97%)
  other arithmetic  6.32 us (1%)
    pallas_call x1, Pallas kernels, back(): pl.pallas_call(back_kernel, out_shape=outs, in_specs=[ANY] * 6 + [HELD] *...  171 us
    pallas_call x1, Pallas kernels, feed(): pl.pallas_call(feed_kernel, out_shape=outs, in_specs=[ANY] * 5 + [HELD] *...  143 us
    pallas_call x1, Pallas kernels, mix_in(): pl.pallas_call(mix_in_kernel, out_shape=saved + held + far, in_specs=[HEL...  109 us

profile of v6, /device:TPU:0, one launch (start us, length us, event | category | flops | bytes accessed | tf_op | source)
XLA Modules:
  0.0 440.1 jit_solution(2347921555943190301)
XLA Ops:
  0.7 0.7 fusion.6
  1.3 0.7 convert_bitcast_fusion
  2.0 0.7 maximum_convert_fusion
  2.7 0.6 pad_maximum_fusion.vecs
  3.3 1.3 fusion.3.gain_shard
  4.6 109.1 %mix_in.1 = (bf16[8,128,2048]{2,1,0:T(8,128)(2,1)}, bf16[8,4,64,640]{3,2,1,0:T(8,128)(2,1)}, f32[1032,320]{1,0:T(8,128)}, f32[1024,320]{1,0:T(8,128)}, bf16[1024...) custom-call(bf16[128,2048]{1,0:T(8,128)(2,1)} %bitcast.38, ...), custom_call_target="tpu_custom_call" | custom-call | tf_op jit(solution)/shard_map/mix_in/pallas_call | solution.py:627
  113.7 143.0 %feed.1 = (f32[128,2048]{1,0:T(8,128)}, f32[128,2048]{1,0:T(8,128)}, bf16[128,2048]{1,0:T(8,128)(2,1)}, f32[8,2048]{1,0:T(8,128)}, bf16[1024,768]{1,0:T(8,128)(2...) custom-call(bf16[1024,320]{1,0:T(8,128)(2,1)} %get-tuple-element.54.product_far, ...), custom_call_target="tpu_custom_call" | custom-call | tf_op jit(solution)/shard_map/feed/pallas_call | solution.py:875
  256.6 0.0 copy-start.2
  256.7 171.3 %back.1 = (bf16[128,2048]{1,0:T(8,128)(2,1)}, bf16[128,2048]{1,0:T(8,128)(2,1)}, bf16[8,64,1536]{2,1,0:T(8,128)(2,1)}, bf16[8,64,640]{2,1,0:T(8,128)(2,1)}, bf16...) custom-call(bf16[128,2048]{1,0:T(8,128)(2,1)} %get-tuple-element.59., ...), custom_call_target="tpu_custom_call" | custom-call | tf_op jit(solution)/shard_map/back/pallas_call | solution.py:1299
  427.9 0.8 reduce_sum.18
  428.7 1.1 reduce_sum.19
  429.8 0.5 slice_bitcast_fusion.4
  430.3 0.0 copy-done.2
  430.3 0.5 divide_multiply_fusion
  430.9 0.5 slice_bitcast_fusion.1
  431.4 0.6 slice_bitcast_fusion
  432.0 0.7 fusion.7
  432.7 0.0 copy-start.1
  432.7 0.0 copy-start
  432.7 5.8 %settle.1 = (f32[64,6144]{1,0:T(8,128)}, f32[64,6144]{1,0:T(8,128)}, f32[64,2560]{1,0:T(8,128)}, f32[64,2560]{1,0:T(8,128)}, f32[80,2048]{1,0:T(8,128)}, /*index=5*/f32[192,2048]{1,0:T(8,128)}) custom-call(bf16[8,64,1536]{2,1,0:T(8,128)(2,1)} %get-tuple-element.80.glu_far, bf16[8,64,640]{2,1,0:T(8,128)(2,1)} %get-tuple-element.81.ins_far, ...), custom_call_target="tpu_custom_call" | custom-call | tf_op jit(solution)/shard_map/settle/pallas_call | solution.py:1403
  438.5 0.0 copy-done.1
  438.5 0.8 copy.36
  439.3 0.0 copy-done
  439.3 0.8 copy.37
Async XLA Ops:
  256.6 173.7 %copy-start.2 = (bf16[80]{0:T(256)(128)(2,1)S(1)}, bf16[80]{0:T(256)(128)(2,1)}, u32[]{:S(2)}) copy-start(bf16[80]{0:T(256)(128)(2,1)} %param.29) | copy-start | bytes 484
  432.7 5.8 %copy-start.1 = (bf16[128,2048]{1,0:T(8,128)(2,1)S(1)}, bf16[128,2048]{1,0:T(8,128)(2,1)}, u32[]{:S(2)}) copy-start(bf16[128,2048]{1,0:T(8,128)(2,1)} %get-tuple-element.77) | copy-start | bytes 1572868
  432.7 6.6 %copy-start = (bf16[128,2048]{1,0:T(8,128)(2,1)S(1)}, bf16[128,2048]{1,0:T(8,128)(2,1)}, u32[]{:S(2)}) copy-start(bf16[128,2048]{1,0:T(8,128)(2,1)} %get-tuple-element.78) | copy-start | bytes 1572868

commit v7 on v6

--- a/solution.py
+++ b/solution.py
@@ -10,6 +10,7 @@
 EPSILON = 1e-06
 RATE_SCALE = 8.0
 CHUNK = 128
+EARLY = 2
 LOW = jnp.bfloat16
 WIDE = jnp.float32
 
@@ -395,11 +396,11 @@
 
 def mix_in_kernel(
     tokens, lru_rows, gelu_rows, gate_rows, up_rows, out_shard, down_shard, gate_block, input_block,
-    vecs, gain_shard,
+    taps, biases, rates, both_gains,
     normed_far, in_far, ext_far, pre_far, conv_far, r_far, i_far, st_far,
     product_far, par_ref, wr_ref, wi_ref, gains, glu_mine, out_whole, down_whole,
     normed, in_whole, ext, pre_ref, conv_ref, r_ref, i_ref, st_ref, product_ref,
-    in_shard, glu_shard, small, held, small_all, vecs_all, gain_all, factors, drive, prod,
+    in_shard, glu_shard, small, vecs, gain_shard, held, small_all, vecs_all, gain_all, factors, drive, prod,
     local_sems, tok_send, tok_recv, in_sems, in_xy_send, in_xy_recv, glu_sems, xy_sems, gain_sems, leave_sems,
 ):
     groups, shards = in_whole.shape[1], in_whole.shape[0]
@@ -422,6 +423,11 @@
     size = gate_block.shape[1]
     small[:, :size] = gate_block[...]
     small[:, size:] = input_block[...]
+    vecs[0:4, :] = taps[...].astype(WIDE)
+    vecs[4:7, :] = biases[...].astype(WIDE)
+    vecs[7:8, :] = rates[...]
+    gain_shard[...] = jnp.zeros_like(gain_shard)
+    gain_shard[0:2, :] = both_gains[...].astype(WIDE)
     leaving = [
         (normed, normed_far), (in_whole, in_far), (ext, ext_far), (pre_ref, pre_far), (conv_ref, conv_far),
         (r_ref, r_far), (i_ref, i_far), (st_ref, st_far), (product_ref, product_far),
@@ -482,7 +488,9 @@
         in_z.arrive(d)
         in_xy(in_z.source(d)).start()
     out_xy.start()
-    glu_z.start()
+    early = min(3, shards)
+    for d in range(1, early):
+        glu_z.copy(d).start()
     down_xy.start()
     gain_z.finish()
     for origin in range(shards):
@@ -502,7 +510,13 @@
                 lambda here: held[slot, here, :].astype(WIDE), gains[0:1, :], store, tokens.shape[0]
             )
 
-    gather.distances(take)
+    def rest(n):
+        @pl.when(n == at.line - 1)
+        def _():
+            for d in range(early, shards):
+                glu_z.copy(d).start()
+
+    gather.distances(take, rest)
     leaving[0].start()
     keep[6].wait()
     vecs_xy.finish()
@@ -596,7 +610,7 @@
 
 def mix_in(
     tokens, lru_rows, gelu_rows, gate_rows, up_rows, out_shard, down_shard, gate_block, input_block,
-    vecs, gain_shard, shards, groups,
+    taps, biases, rates, both_gains, shards, groups,
 ):
     rows = lru_rows.shape[0]
     block, width = tokens.shape
@@ -604,6 +618,7 @@
     both = 2 * channels
     in_shape = (shards, rows, both)
     glu_shape = (shards, rows, 2 * (gate_rows.shape[1] // shards))
+    local = gate_block.shape[0]
     small_shape = (gate_block.shape[0], 2 * gate_block.shape[1])
     pieces = 2
     wide = jax.ShapeDtypeStruct((positions, channels), WIDE)
@@ -627,15 +642,16 @@
     return pl.pallas_call(
         mix_in_kernel,
         out_shape=saved + held + far,
-        in_specs=[HELD] * 9 + [ANY] * 2,
+        in_specs=[HELD] * 13,
         out_specs=[ANY] * len(saved) + [HELD] * len(held) + [ANY] * len(far),
         scratch_shapes=[pltpu.VMEM(member.shape, member.dtype) for member in saved]
         + [
             pltpu.VMEM(in_shape, LOW), pltpu.VMEM(glu_shape, LOW), pltpu.VMEM(small_shape, LOW),
+            pltpu.VMEM((8, local), WIDE), pltpu.VMEM((8, rows), WIDE),
             pltpu.VMEM((shards, block, width), LOW),
             pltpu.VMEM((groups,) + small_shape, LOW),
-            pltpu.VMEM((groups,) + vecs.shape, WIDE),
-            pltpu.VMEM((shards, groups) + gain_shard.shape, WIDE),
+            pltpu.VMEM((groups, 8, local), WIDE),
+            pltpu.VMEM((shards, groups, 8, rows), WIDE),
         ]
         + [pltpu.VMEM((lane_tiles(channels), positions, 128), WIDE)] * 3
         + [
@@ -648,16 +664,16 @@
         name="mix_in",
     )(
         tokens, lru_rows, gelu_rows, gate_rows, up_rows, out_shard, down_shard, gate_block, input_block,
-        vecs, gain_shard,
+        taps, biases, rates, both_gains,
     )
 
 
 def feed_kernel(
     product_far, out_far, glu_mine, down_in, cotangent, tokens, gains,
-    middle, middle_grad, mixed_low, gain_sums, hidden_far, glu_grad, down_grad,
+    middle, middle_grad, mixed_low, gain_sums, hidden_far, glu_grad, down_grad, glu_first,
     product, out_whole, held, cots, glu, down, both, hidden, wide_pair, hidden_pair, normed2, staged, down_staged,
     parts, heard, into, sib_send, sib_recv, line_send, line_recv,
-    local_sems, glu_send, glu_recv, two_send, two_recv, cot_send, cot_recv, stage_sems,
+    local_sems, glu_send, glu_recv, two_send, two_recv, cot_send, cot_recv, stage_sems, first_sems,
 ):
     shards, groups = glu.shape[0], glu.shape[1]
     at = Place(shards, groups)
@@ -800,8 +816,6 @@
 
     hidden_leave = pltpu.make_async_copy(hidden, hidden_far, local_sems.at[6])
     hidden_leave.start()
-    sums.join()
-
     def glu_out(j):
         return pltpu.make_async_copy(
             staged.at[lax.rem(j, 2)], glu_grad.at[:, j], stage_sems.at[lax.rem(j, 2)]
@@ -810,13 +824,16 @@
     def glu_sums(first, last):
         @pl.loop(first, last)
         def _(j):
-            @pl.when(j >= 2)
+            @pl.when(j >= first + 2)
             def _():
                 glu_out(j - 2).wait()
 
             rows = held[:, :, columns_of(j)].reshape(shards * block, 256)
             staged[lax.rem(j, 2)] = outer_sum(rows, both[...]).astype(LOW).reshape(staged.shape[1:])
             glu_out(j).start()
+
+        for j in range(max(last - 2, first), last):
+            glu_out(j).wait()
 
     def down_out(j):
         return pltpu.make_async_copy(
@@ -834,8 +851,16 @@
             down_staged[lax.rem(j, 2)] = outer_sum(hidden[:, columns_of(j)], grads).astype(LOW)
             down_out(j).start()
 
+    early = glu_first.shape[1]
+    glu_early = Spread(
+        at, lambda peer: glu_grad.at[peer, pl.ds(0, early)], lambda origin: glu_first.at[origin],
+        first_sems.at[0], first_sems.at[1],
+    )
+    glu_sums(0, early)
+    glu_early.start()
+    sums.join()
     down_sums()
-    glu_sums(0, shards)
+    glu_sums(early, shards)
     gain_sums[...] = jnp.zeros_like(gain_sums)
 
     def back(here, grad):
@@ -849,11 +874,10 @@
         gain_sums[0:1, :] += jnp.sum(grad * values * scale, axis=0, keepdims=True)
 
     sums.finish(back)
-    for j in range(shards - 2, shards):
-        glu_out(j).wait()
     for j in range(max(units // 256 - 2, 0), units // 256):
         down_out(j).wait()
     hidden_leave.wait()
+    glu_early.finish()
     sums.sent()
     two_z.sent()
     cot_z.sent()
@@ -870,13 +894,14 @@
         jax.ShapeDtypeStruct((shards * block, units), LOW),
         jax.ShapeDtypeStruct((groups, shards, rows, both), LOW),
         jax.ShapeDtypeStruct((units, width), LOW),
+        jax.ShapeDtypeStruct((groups, EARLY, rows, both), LOW),
     ]
     gathered = pltpu.VMEM((shards, block, width), LOW)
     return pl.pallas_call(
         feed_kernel,
         out_shape=outs,
         in_specs=[ANY] * 5 + [HELD] * 2,
-        out_specs=[HELD] * 4 + [ANY] * 3,
+        out_specs=[HELD] * 4 + [ANY] * 4,
         scratch_shapes=[
             pltpu.VMEM(product.shape, LOW), pltpu.VMEM(out_whole.shape, LOW),
             gathered, gathered,
@@ -893,7 +918,7 @@
         + LineScatter.scratch(line, block, width, thirds)
         + [
             dma(8), dma(shards, groups), dma(shards, groups), dma(shards, pieces, 3), dma(shards, pieces),
-            dma(shards, pieces, 3), dma(shards, pieces), dma(4),
+            dma(shards, pieces, 3), dma(shards, pieces), dma(4), dma(2, groups),
         ],
         compiler_params=pltpu.CompilerParams(
             collective_id=2, has_side_effects=True, vmem_limit_bytes=VMEM_BYTES
@@ -905,7 +930,7 @@
 def back_kernel(
     mixed, hidden_far, down_far, middle_far, middle_grad_far, tokens_far, gains, par_ref, wr_ref, wi_ref,
     out_far, in_far, normed_far, product_far, ext_far, pre_far, conv_far, r_far, i_far, st_far,
-    glu_grad, down_grad, mlp_parts,
+    glu_grad, glu_first, down_grad, mlp_parts,
     result, tokens_grad, glu_out, in_out, out_heard, small_heard, gain_out, glu_heard, in_grad, down_heard,
     middle, middle_grad, tokens, held, in_whole, out_whole, product, ext, pre, conv_ref, r_ref, i_ref, st_ref,
     both, pair_grad, staged, adj, totals_ref, wr_sum, wi_sum,
@@ -946,7 +971,11 @@
             at, lambda peer: src.at[peer], lambda origin: dst.at[origin], sems.at[0], sems.at[1], "seq"
         )
 
-    glu_xy = over_fsdp(glu_grad, glu_heard, glu_xy_sems)
+    early = glu_first.shape[1]
+    glu_xy = Spread(
+        at, lambda peer: glu_grad.at[peer, pl.ds(early, shards - early)], lambda origin: glu_heard.at[origin],
+        glu_xy_sems.at[0], glu_xy_sems.at[1],
+    )
     in_xy = over_fsdp(in_grad, in_heard, in_xy_sems)
     out_xy = over_fsdp(out_grad, out_heard, out_sems)
     down_xy = over_fsdp(down_grad, down_heard, down_sems)
@@ -1163,11 +1192,12 @@
     sums.join()
     glu_xy.finish()
 
-    def glu_load(d, origin):
+    def glu_load(d, origin, first=False):
         peer = lax.rem(s + d, shards)
         half = lax.rem(d, 2)
+        source = glu_first.at[origin, peer] if first else glu_heard.at[origin, peer - early]
         return pltpu.make_async_copy(
-            glu_heard.at[origin, peer], glu_parts.at[half, origin], glu_sems.at[2 + half, origin]
+            source, glu_parts.at[half, origin], glu_sems.at[2 + half, origin]
         )
 
     def glu_load_own(d):
@@ -1179,8 +1209,12 @@
 
     def glu_loads(d):
         glu_load_own(d).start()
-        for hop in range(1, groups):
-            glu_load(d, lax.rem(f + hop, groups)).start()
+        peer = lax.rem(s + d, shards)
+        for first, known in ((True, peer < early), (False, peer >= early)):
+            @pl.when(known)
+            def _():
+                for hop in range(1, groups):
+                    glu_load(d, lax.rem(f + hop, groups), first).start()
 
     def add(parts, total, peer):
         @pl.loop(0, total.shape[1] // 16)
@@ -1200,7 +1234,10 @@
             glu_loads(d + 1)
 
         for origin in range(groups):
-            glu_load(d, origin).wait()
+            pltpu.make_async_copy(
+                glu_first.at[origin, 0], glu_parts.at[lax.rem(d, 2), origin],
+                glu_sems.at[2 + lax.rem(d, 2), origin],
+            ).wait()
         add(glu_parts.at[lax.rem(d, 2)], glu_sum, lax.rem(s + d, shards))
 
         @pl.when(d < shards)
@@ -1275,7 +1312,7 @@
 
 def back(
     mixed, hidden, down_whole, middle, middle_grad, tokens, gains, par, wr, wi,
-    out_whole, in_whole, normed, product, ext, pre, conv, r, i, st, glu_grad, down_grad, mlp_sums, size,
+    out_whole, in_whole, normed, product, ext, pre, conv, r, i, st, glu_grad, glu_first, down_grad, mlp_sums, size,
 ):
     shards, groups, rows, both = in_whole.shape
     block, width = tokens.shape
@@ -1290,7 +1327,8 @@
         jax.ShapeDtypeStruct((groups, local, width), LOW),
         jax.ShapeDtypeStruct((groups, local + 8, 2 * size), WIDE),
         jax.ShapeDtypeStruct((shards, 8, rows), WIDE),
-        jax.ShapeDtypeStruct(glu_grad.shape, LOW), jax.ShapeDtypeStruct(in_shape, LOW),
+        jax.ShapeDtypeStruct((groups, shards - glu_first.shape[1]) + glu_grad.shape[2:], LOW),
+        jax.ShapeDtypeStruct(in_shape, LOW),
         jax.ShapeDtypeStruct(down_grad.shape, LOW),
     ]
     late = [middle, middle_grad, tokens]
@@ -1299,7 +1337,7 @@
     return pl.pallas_call(
         back_kernel,
         out_shape=outs,
-        in_specs=[ANY] * 6 + [HELD] * 4 + [ANY] * (len(far) + 2) + [HELD],
+        in_specs=[ANY] * 6 + [HELD] * 4 + [ANY] * (len(far) + 3) + [HELD],
         out_specs=[HELD] * 2 + [ANY] * 8,
         scratch_shapes=[pltpu.VMEM(member.shape, member.dtype) for member in late]
         + [pltpu.VMEM((shards, block, width), LOW)]
@@ -1336,20 +1374,23 @@
         name="back",
     )(
         mixed, hidden, down_whole, middle, middle_grad, tokens, gains, par, wr, wi, *far,
-        glu_grad, down_grad, mlp_sums,
+        glu_grad, glu_first, down_grad, mlp_sums,
     )
 
 
 def settle_kernel(
-    glu_far, ins_far, outs_far, down_heard, down_grad,
-    gate_far, up_far, lru_far, gelu_far, out_far, down_far,
-    glu, ins, outs, parts, gate_sum, up_sum, lru_sum, gelu_sum, out_sum, down_sum, sems, leave_sems,
+    glu_far, ins_far, outs_far, down_heard, down_grad, result_far, tokens_far,
+    result_out, tokens_out, gate_far, up_far, lru_far, gelu_far, out_far, down_far,
+    result, tokens, glu, ins, outs, parts, gate_sum, up_sum, lru_sum, gelu_sum, out_sum, down_sum, sems, leave_sems,
 ):
     shards, rows, both = glu.shape
     groups = outs.shape[0]
     units, channels = both // 2, ins.shape[2] // 2
     f = lax.axis_index("fsdp")
-    keep = [(glu_far, glu), (ins_far, ins), (outs_far, outs), (down_grad.at[f], parts.at[f])]
+    keep = [
+        (glu_far, glu), (ins_far, ins), (outs_far, outs), (result_far, result), (tokens_far, tokens),
+        (down_grad.at[f], parts.at[f]),
+    ]
     for hop in range(1, groups):
         origin = lax.rem(f + hop, groups)
         keep.append((down_heard.at[origin], parts.at[origin]))
@@ -1358,7 +1399,7 @@
         copy.start()
     leaving = [
         (gate_sum, gate_far), (up_sum, up_far), (lru_sum, lru_far), (gelu_sum, gelu_far),
-        (out_sum, out_far), (down_sum, down_far),
+        (out_sum, out_far), (down_sum, down_far), (result, result_out), (tokens, tokens_out),
     ]
     leaving = [pltpu.make_async_copy(a, b, leave_sems.at[n]) for n, (a, b) in enumerate(leaving)]
     keep[0].wait()
@@ -1383,10 +1424,13 @@
                 value = value + terms[origin, here, :].astype(WIDE)
             total[here, :] = value
 
+    for n in (3, 4):
+        keep[n].wait()
+        leaving[n + 3].start()
     keep[2].wait()
     add(outs, out_sum)
     leaving[4].start()
-    for copy in keep[3:]:
+    for copy in keep[5:]:
         copy.wait()
     add(parts, down_sum)
     leaving[5].start()
@@ -1394,7 +1438,7 @@
         copy.wait()
 
 
-def settle(glu, ins, outs, down_heard, down_grad):
+def settle(glu, ins, outs, down_heard, down_grad, result, tokens):
     shards, rows, both = glu.shape
     groups, local, width = outs.shape
     units, channels = both // 2, ins.shape[2] // 2
@@ -1402,15 +1446,16 @@
     shapes += [(local, width), down_grad.shape[1:]]
     return pl.pallas_call(
         settle_kernel,
-        out_shape=[jax.ShapeDtypeStruct(shape, WIDE) for shape in shapes],
-        in_specs=[ANY] * 5,
-        out_specs=[ANY] * 6,
-        scratch_shapes=[pltpu.VMEM(member.shape, LOW) for member in (glu, ins, outs, down_grad)]
+        out_shape=[jax.ShapeDtypeStruct(result.shape, LOW)] * 2
+        + [jax.ShapeDtypeStruct(shape, WIDE) for shape in shapes],
+        in_specs=[ANY] * 7,
+        out_specs=[ANY] * 8,
+        scratch_shapes=[pltpu.VMEM(member.shape, LOW) for member in (result, tokens, glu, ins, outs, down_grad)]
         + [pltpu.VMEM(shape, WIDE) for shape in shapes]
-        + [dma(groups + 3), dma(6)],
+        + [dma(groups + 5), dma(8)],
         compiler_params=pltpu.CompilerParams(vmem_limit_bytes=VMEM_BYTES),
         name="settle",
-    )(glu, ins, outs, down_heard, down_grad)
+    )(glu, ins, outs, down_heard, down_grad, result, tokens)
 
 
 def mixer_forward_kernel(
@@ -1790,25 +1835,19 @@
     grad_low = cotangent.reshape(positions, width)
 
     own_decay = decay_param.astype(WIDE)
-    vecs = jnp.concatenate(
-        [
-            conv_weight.astype(WIDE).T,
-            jnp.stack([conv_bias, recurrence_bias, input_gate_bias]).astype(WIDE),
-            -RATE_SCALE * jax.nn.softplus(-own_decay)[None],
-        ],
-        axis=0,
-    )
-    gain_shard = jnp.pad(jnp.stack([mix_gain, mlp_gain]).astype(WIDE), ((0, 6), (0, 0)))
+    rates = -RATE_SCALE * jax.nn.softplus(-own_decay)[None]
     tokens_low = tokens.reshape(positions, width)
     (
         normed, in_whole, ext, branch_pre, conv_low, recur_gate, input_gate, states, product, par, wr, wi,
         gains, glu_mine, out_whole, down_whole,
     ) = mix_in(
         tokens_low, lru_in_weight, gelu_in_weight, gate_weight, up_weight, out_weight, down_weight,
-        recurrence_weight, input_gate_weight, vecs, gain_shard, shards, groups,
+        recurrence_weight, input_gate_weight, conv_weight.T,
+        jnp.stack([conv_bias, recurrence_bias, input_gate_bias]), rates, jnp.stack([mix_gain, mlp_gain]),
+        shards, groups,
     )
     out_whole, down_whole = out_whole.reshape(-1, width), down_whole.reshape(-1, width)
-    middle, middle_grad, mixed_low, mlp_sums, hidden, glu_grad, down_grad = feed(
+    middle, middle_grad, mixed_low, mlp_sums, hidden, glu_grad, down_grad, glu_first = feed(
         product, out_whole, glu_mine, down_whole, grad_low, tokens_low, gains, groups
     )
     down_grad = down_grad.reshape(groups, -1, width)
@@ -1817,11 +1856,11 @@
     ) = back(
         mixed_low, hidden, down_whole, middle, middle_grad, tokens_low, gains, par, wr, wi,
         out_whole, in_whole, normed, product, ext, branch_pre, conv_low, recur_gate, input_gate, states,
-        glu_grad, down_grad, mlp_sums, size,
+        glu_grad, glu_first, down_grad, mlp_sums, size,
     )
     small_rows = recurrence_weight.shape[0]
-    gate_sum, up_sum, lru_sum, gelu_sum, out_sum, down_sum = settle(
-        glu_out, in_out, out_heard, down_heard, down_grad
+    result, tokens_grad, gate_sum, up_sum, lru_sum, gelu_sum, out_sum, down_sum = settle(
+        glu_out, in_out, out_heard, down_heard, down_grad, result, tokens_grad
     )
     small = jnp.sum(small_heard, axis=0)
     gain_grads = jnp.sum(gain_out, axis=0)

time: 441 us -> 427 us (0.968)
  Pallas kernels: 429 us -> 419 us
    pallas_call x1, Pallas kernels: 109 us -> 101 us  [mix_in(): pl.pallas_call(mix_in_kernel, out_shape=saved + held + far, in_specs=[HEL...]
where the time goes in v7:
time: 427 us
  Pallas kernels  419 us (98%)
    pallas_call x1, Pallas kernels, back(): pl.pallas_call(back_kernel, out_shape=outs, in_specs=[ANY] * 6 + [HELD] *...  169 us
    pallas_call x1, Pallas kernels, feed(): pl.pallas_call(feed_kernel, out_shape=outs, in_specs=[ANY] * 5 + [HELD] *...  143 us
    pallas_call x1, Pallas kernels, mix_in(): pl.pallas_call(mix_in_kernel, out_shape=saved + held + far, in_specs=[HEL...  101 us

profile of v7, /device:TPU:0, one launch (start us, length us, event | category | flops | bytes accessed | tf_op | source)
XLA Modules:
  0.0 426.8 jit_solution(9847507305645516346)
XLA Ops:
  0.7 1.2 pad_maximum_fusion.1.both_gains
  1.8 1.2 fusion.2.rates
  3.0 1.3 pad_maximum_fusion.biases
  4.3 100.9 %mix_in.1 = (bf16[8,128,2048]{2,1,0:T(8,128)(2,1)}, bf16[8,4,64,640]{3,2,1,0:T(8,128)(2,1)}, f32[1032,320]{1,0:T(8,128)}, f32[1024,320]{1,0:T(8,128)}, bf16[1024...) custom-call(bf16[128,2048]{1,0:T(8,128)(2,1)} %bitcast.37, ...), custom_call_target="tpu_custom_call" | custom-call | tf_op jit(solution)/shard_map/mix_in/pallas_call | solution.py:642
  105.2 142.7 %feed.1 = (f32[128,2048]{1,0:T(8,128)}, f32[128,2048]{1,0:T(8,128)}, bf16[128,2048]{1,0:T(8,128)(2,1)}, f32[8,2048]{1,0:T(8,128)}, bf16[1024,768]{1,0:T(8,128)(2...) custom-call(bf16[1024,320]{1,0:T(8,128)(2,1)} %get-tuple-element.57.product_far, ...), custom_call_target="tpu_custom_call" | custom-call | tf_op jit(solution)/shard_map/feed/pallas_call | solution.py:900
  248.0 169.0 %back.1 = (bf16[128,2048]{1,0:T(8,128)(2,1)}, bf16[128,2048]{1,0:T(8,128)(2,1)}, bf16[8,64,1536]{2,1,0:T(8,128)(2,1)}, bf16[8,64,640]{2,1,0:T(8,128)(2,1)}, bf16...) custom-call(bf16[128,2048]{1,0:T(8,128)(2,1)} %get-tuple-element.62., ...), custom_call_target="tpu_custom_call" | custom-call | tf_op jit(solution)/shard_map/back/pallas_call | solution.py:1337
  417.0 0.0 copy-start.1
  417.0 0.0 copy-start
  417.0 0.0 copy-start.2
  417.0 6.8 %settle.1 = (bf16[128,2048]{1,0:T(8,128)(2,1)}, bf16[128,2048]{1,0:T(8,128)(2,1)}, f32[64,6144]{1,0:T(8,128)}, f32[64,6144]{1,0:T(8,128)}, f32[64,2560]{1,0:T(8,...) custom-call(bf16[8,64,1536]{2,1,0:T(8,128)(2,1)} %get-tuple-element.81.glu_far, ...), custom_call_target="tpu_custom_call" | custom-call | tf_op jit(solution)/shard_map/settle/pallas_call | solution.py:1447
  423.8 0.0 copy-done.1
  423.9 0.0 copy-done
  423.9 0.5 slice_bitcast_fusion.4
  424.4 0.0 copy-done.2
  424.4 0.5 divide_multiply_fusion
  425.0 0.5 slice_bitcast_fusion.1
  425.5 0.6 slice_bitcast_fusion
  426.1 0.7 fusion.3
  (2 shorter events, 0.0 us)
Async XLA Ops:
  417.0 6.9 %copy-start.1 = (f32[8,8,64]{2,1,0:T(8,128)S(1)}, f32[8,8,64]{2,1,0:T(8,128)}, u32[]{:S(2)}) copy-start(f32[8,8,64]{2,1,0:T(8,128)} %get-tuple-element.89) | copy-start | bytes 49156
  417.0 6.9 %copy-start = (f32[4,88,320]{2,1,0:T(8,128)S(1)}, f32[4,88,320]{2,1,0:T(8,128)}, u32[]{:S(2)}) copy-start(f32[4,88,320]{2,1,0:T(8,128)} %get-tuple-element.93) | copy-start | bytes 1351684
  417.0 7.5 %copy-start.2 = (bf16[80]{0:T(256)(128)(2,1)S(1)}, bf16[80]{0:T(256)(128)(2,1)}, u32[]{:S(2)}) copy-start(bf16[80]{0:T(256)(128)(2,1)} %param.29) | copy-start | bytes 484

commit v8 on v7

--- a/solution.py
+++ b/solution.py
@@ -1136,6 +1136,7 @@
     )
     fed.join()
     keep[9].wait()
+    down_xy.start()
 
     def project(chip):
         rows = both[pl.ds(pl.multiple_of(chip * pair, pair), pair), :]
@@ -1276,7 +1277,6 @@
     gain_xy.start()
     in_own.wait()
     in_xy.finish()
-    down_xy.start()
 
     @pl.loop(1, shards + 1)
     def _(d):

time: 427 us -> 416 us (0.974)
  Pallas kernels: 419 us -> 408 us
    pallas_call x1, Pallas kernels: 169 us -> 158 us  [back(): pl.pallas_call(back_kernel, out_shape=outs, in_specs=[ANY] * 6 + [HELD] *...]
where the time goes in v8:
time: 416 us
  Pallas kernels  408 us (98%)
  other arithmetic  4.21 us (1%)
    pallas_call x1, Pallas kernels, back(): pl.pallas_call(back_kernel, out_shape=outs, in_specs=[ANY] * 6 + [HELD] *...  158 us
    pallas_call x1, Pallas kernels, feed(): pl.pallas_call(feed_kernel, out_shape=outs, in_specs=[ANY] * 5 + [HELD] *...  143 us
    pallas_call x1, Pallas kernels, mix_in(): pl.pallas_call(mix_in_kernel, out_shape=saved + held + far, in_specs=[HEL...  101 us

profile of v8, /device:TPU:0, one launch (start us, length us, event | category | flops | bytes accessed | tf_op | source)
XLA Modules:
  0.0 415.7 jit_solution(12352072773841161682)
XLA Ops:
  0.7 1.2 pad_maximum_fusion.1.both_gains
  1.8 1.2 fusion.2.rates
  3.0 1.3 pad_maximum_fusion.biases
  4.3 100.9 %mix_in.1 = (bf16[8,128,2048]{2,1,0:T(8,128)(2,1)}, bf16[8,4,64,640]{3,2,1,0:T(8,128)(2,1)}, f32[1032,320]{1,0:T(8,128)}, f32[1024,320]{1,0:T(8,128)}, bf16[1024...) custom-call(bf16[128,2048]{1,0:T(8,128)(2,1)} %bitcast.37, ...), custom_call_target="tpu_custom_call" | custom-call | tf_op jit(solution)/shard_map/mix_in/pallas_call | solution.py:642
  105.2 142.7 %feed.1 = (f32[128,2048]{1,0:T(8,128)}, f32[128,2048]{1,0:T(8,128)}, bf16[128,2048]{1,0:T(8,128)(2,1)}, f32[8,2048]{1,0:T(8,128)}, bf16[1024,768]{1,0:T(8,128)(2...) custom-call(bf16[1024,320]{1,0:T(8,128)(2,1)} %get-tuple-element.57.product_far, ...), custom_call_target="tpu_custom_call" | custom-call | tf_op jit(solution)/shard_map/feed/pallas_call | solution.py:900
  248.0 157.9 %back.1 = (bf16[128,2048]{1,0:T(8,128)(2,1)}, bf16[128,2048]{1,0:T(8,128)(2,1)}, bf16[8,64,1536]{2,1,0:T(8,128)(2,1)}, bf16[8,64,640]{2,1,0:T(8,128)(2,1)}, bf16...) custom-call(bf16[128,2048]{1,0:T(8,128)(2,1)} %get-tuple-element.62., ...), custom_call_target="tpu_custom_call" | custom-call | tf_op jit(solution)/shard_map/back/pallas_call | solution.py:1337
  405.9 0.0 copy-start.1
  405.9 0.0 copy-start
  405.9 0.0 copy-start.2
  405.9 6.8 %settle.1 = (bf16[128,2048]{1,0:T(8,128)(2,1)}, bf16[128,2048]{1,0:T(8,128)(2,1)}, f32[64,6144]{1,0:T(8,128)}, f32[64,6144]{1,0:T(8,128)}, f32[64,2560]{1,0:T(8,...) custom-call(bf16[8,64,1536]{2,1,0:T(8,128)(2,1)} %get-tuple-element.81.glu_far, ...), custom_call_target="tpu_custom_call" | custom-call | tf_op jit(solution)/shard_map/settle/pallas_call | solution.py:1447
  412.8 0.0 copy-done.1
  412.8 0.0 copy-done
  412.9 0.5 slice_bitcast_fusion.4
  413.4 0.0 copy-done.2
  413.4 0.5 divide_multiply_fusion
  413.9 0.5 slice_bitcast_fusion.1
  414.4 0.6 slice_bitcast_fusion
  415.0 0.7 fusion.3
  (2 shorter events, 0.0 us)
Async XLA Ops:
  405.9 6.9 %copy-start.1 = (f32[8,8,64]{2,1,0:T(8,128)S(1)}, f32[8,8,64]{2,1,0:T(8,128)}, u32[]{:S(2)}) copy-start(f32[8,8,64]{2,1,0:T(8,128)} %get-tuple-element.89) | copy-start | bytes 49156
  405.9 6.9 %copy-start = (f32[4,88,320]{2,1,0:T(8,128)S(1)}, f32[4,88,320]{2,1,0:T(8,128)}, u32[]{:S(2)}) copy-start(f32[4,88,320]{2,1,0:T(8,128)} %get-tuple-element.93) | copy-start | bytes 1351684
  405.9 7.5 %copy-start.2 = (bf16[80]{0:T(256)(128)(2,1)S(1)}, bf16[80]{0:T(256)(128)(2,1)}, u32[]{:S(2)}) copy-start(bf16[80]{0:T(256)(128)(2,1)} %param.29) | copy-start | bytes 484

commit v9 on v8

--- a/solution.py
+++ b/solution.py
@@ -1151,8 +1151,11 @@
     for k in range(at.line // 2):
         project(at.line - 1 - k)
         project(k)
-        sums.push(at.line - 1 - k)
-        sums.push(k)
+        sums.push(at.line - 1 - k, 0, 1)
+        sums.push(k, 0, 1)
+    for k in range(at.line // 2):
+        sums.push(at.line - 1 - k, 1)
+        sums.push(k, 1)
     mixed_z.sent()
     keep[11].start()
     local = small.shape[1] - 8

time: 416 us -> 420 us (level)
  no operation moved by 1% of the time
where the time goes in v9:
time: 420 us
  Pallas kernels  412 us (98%)
  other arithmetic  4.21 us (1%)
    pallas_call x1, Pallas kernels, back(): pl.pallas_call(back_kernel, out_shape=outs, in_specs=[ANY] * 6 + [HELD] *...  162 us
    pallas_call x1, Pallas kernels, feed(): pl.pallas_call(feed_kernel, out_shape=outs, in_specs=[ANY] * 5 + [HELD] *...  143 us
    pallas_call x1, Pallas kernels, mix_in(): pl.pallas_call(mix_in_kernel, out_shape=saved + held + far, in_specs=[HEL...  101 us

profile of v9, /device:TPU:0, one launch (start us, length us, event | category | flops | bytes accessed | tf_op | source)
XLA Modules:
  0.0 419.5 jit_solution(6844969083385592469)
XLA Ops:
  0.7 1.2 pad_maximum_fusion.1.both_gains
  1.8 1.2 fusion.2.rates
  3.0 1.3 pad_maximum_fusion.biases
  4.3 100.9 %mix_in.1 = (bf16[8,128,2048]{2,1,0:T(8,128)(2,1)}, bf16[8,4,64,640]{3,2,1,0:T(8,128)(2,1)}, f32[1032,320]{1,0:T(8,128)}, f32[1024,320]{1,0:T(8,128)}, bf16[1024...) custom-call(bf16[128,2048]{1,0:T(8,128)(2,1)} %bitcast.37, ...), custom_call_target="tpu_custom_call" | custom-call | tf_op jit(solution)/shard_map/mix_in/pallas_call | solution.py:642
  105.2 142.7 %feed.1 = (f32[128,2048]{1,0:T(8,128)}, f32[128,2048]{1,0:T(8,128)}, bf16[128,2048]{1,0:T(8,128)(2,1)}, f32[8,2048]{1,0:T(8,128)}, bf16[1024,768]{1,0:T(8,128)(2...) custom-call(bf16[1024,320]{1,0:T(8,128)(2,1)} %get-tuple-element.57.product_far, ...), custom_call_target="tpu_custom_call" | custom-call | tf_op jit(solution)/shard_map/feed/pallas_call | solution.py:900
  248.0 161.7 %back.1 = (bf16[128,2048]{1,0:T(8,128)(2,1)}, bf16[128,2048]{1,0:T(8,128)(2,1)}, bf16[8,64,1536]{2,1,0:T(8,128)(2,1)}, bf16[8,64,640]{2,1,0:T(8,128)(2,1)}, bf16...) custom-call(bf16[128,2048]{1,0:T(8,128)(2,1)} %get-tuple-element.62., ...), custom_call_target="tpu_custom_call" | custom-call | tf_op jit(solution)/shard_map/back/pallas_call | solution.py:1340
  409.7 0.0 copy-start.1
  409.7 0.0 copy-start
  409.7 0.0 copy-start.2
  409.7 6.8 %settle.1 = (bf16[128,2048]{1,0:T(8,128)(2,1)}, bf16[128,2048]{1,0:T(8,128)(2,1)}, f32[64,6144]{1,0:T(8,128)}, f32[64,6144]{1,0:T(8,128)}, f32[64,2560]{1,0:T(8,...) custom-call(bf16[8,64,1536]{2,1,0:T(8,128)(2,1)} %get-tuple-element.81.glu_far, ...), custom_call_target="tpu_custom_call" | custom-call | tf_op jit(solution)/shard_map/settle/pallas_call | solution.py:1450
  416.6 0.0 copy-done.1
  416.6 0.0 copy-done
  416.6 0.5 slice_bitcast_fusion.4
  417.2 0.0 copy-done.2
  417.2 0.5 divide_multiply_fusion
  417.7 0.5 slice_bitcast_fusion.1
  418.2 0.6 slice_bitcast_fusion
  418.8 0.7 fusion.3
  (2 shorter events, 0.0 us)
Async XLA Ops:
  409.7 6.9 %copy-start.1 = (f32[8,8,64]{2,1,0:T(8,128)S(1)}, f32[8,8,64]{2,1,0:T(8,128)}, u32[]{:S(2)}) copy-start(f32[8,8,64]{2,1,0:T(8,128)} %get-tuple-element.89) | copy-start | bytes 49156
  409.7 6.9 %copy-start = (f32[4,88,320]{2,1,0:T(8,128)S(1)}, f32[4,88,320]{2,1,0:T(8,128)}, u32[]{:S(2)}) copy-start(f32[4,88,320]{2,1,0:T(8,128)} %get-tuple-element.93) | copy-start | bytes 1351684
  409.7 7.5 %copy-start.2 = (bf16[80]{0:T(256)(128)(2,1)S(1)}, bf16[80]{0:T(256)(128)(2,1)}, u32[]{:S(2)}) copy-start(bf16[80]{0:T(256)(128)(2,1)} %param.29) | copy-start | bytes 484
